TPU v7x, 256 devices: a whole 4x4x8 slice. The times are simulated.
256 devices in a mesh: gx: 4 (over x), wa: 64 (over y, z, core).
Axes of the slice: x: 4, y: 4, z: 8, core: 2. Of those that a mesh axis runs over, the one named last changes fastest.
Arguments:
- mixing_ratio: float32 [1536, 48, 1536], P('wa', 'gx'), may hold values from 0 to 1
- thermal_state: float32 [1536, 48, 1536], P('wa', 'gx'), may hold values from 1 to 3
- streamwise_speed: float32 [1536, 1536], P('wa'), may hold values from 0.5 to 2
- implicit_derivative_matrix: bfloat16 [1536, 1536], replicated, may hold values from -0.15625 to 0.15625
- stored_entry_slices: bfloat16 [2, 1536, 8, 1536], P(None, 'wa', 'gx'), may hold values from 0 to 2
- orifice_region_flag: int32 [1536, 1536], P('wa'), may hold values 0 or 1
- arriving_slice_number: int32 [1], replicated, may hold values from 0 to 7
- joint_frequency_class: int32 [1536, 48, 12], P('wa', 'gx'), may hold values from 0 to 4095
Outputs:
- mixture_next: float32 [1536, 48, 1536], P('wa', 'gx')
- temperature_next: float32 [1536, 48, 1536], P('wa', 'gx')
- histogram: float32 [64, 64], replicated
All inputs are finite; a program needn't handle non-finite values. No bound on the sum of `orifice_region_flag` on one device may be relied on, other than what follows from the above.
Results may differ from a plain program's by a relative error of at most 0.00057.
Values may be sent and summed in bfloat16 or wider, within the bound.
No kernel may reach another device: no remote copies, remote signals or barrier semaphores. Data moves between devices by JAX's collectives and lax.ppermute only.
A program may use at most 128 MiB of HBM per device.

v0:
```python
import jax
import jax.numpy as jnp
from jax import lax
from jax.sharding import PartitionSpec as P

HB = 64
ZBLK = 128


mixing_diffusivity = 0.3
heat_diffusivity = 0.4
release_rate = 0.5
phase_step = 0.2


def from_root(block, axis, source):
    block = jnp.where(lax.axis_index(axis) == source, block, jnp.zeros_like(block))
    return lax.psum(block, axis)


def with_halo(block, sides, width):
    for axis, dim in sides:
        count = lax.axis_size(axis)
        forward = [(i, i + 1) for i in range(count - 1)]
        backward = [(target, source) for source, target in forward]
        low = lax.ppermute(
            lax.slice_in_dim(block, block.shape[dim] - width, None, axis=dim), axis, forward
        )
        high = lax.ppermute(lax.slice_in_dim(block, 0, width, axis=dim), axis, backward)
        block = jnp.concatenate([low, block, high], axis=dim)
    return block


def line_terms(pencil, implicit_derivative_matrix):
    radial_slope = jnp.einsum(
        "ij,...jc->...ic", implicit_derivative_matrix, pencil, preferred_element_type=jnp.float32
    ).astype(jnp.bfloat16)
    radial_curve = jnp.einsum(
        "ij,...jc->...ic",
        implicit_derivative_matrix,
        radial_slope,
        preferred_element_type=jnp.float32,
    ).astype(jnp.bfloat16)
    return (radial_slope, radial_curve)


def body(
    mixing_ratio,
    thermal_state,
    streamwise_speed,
    implicit_derivative_matrix,
    stored_entry_slices,
    orifice_region_flag,
    arriving_slice_number,
    joint_frequency_class,
):
    transported_quantities = jnp.stack([mixing_ratio, thermal_state])
    row_count, plane_count, depth_count = mixing_ratio.shape
    column_count = plane_count * depth_count
    rounded = transported_quantities.astype(jnp.bfloat16)
    flattened = rounded.reshape(2, row_count, column_count)
    held_count = stored_entry_slices.shape[2]
    plane_index = arriving_slice_number[0]
    owner = plane_index // held_count
    held_plane = lax.dynamic_index_in_dim(
        stored_entry_slices, plane_index % held_count, 2, keepdims=False
    )
    database_plane = from_root(held_plane, "gx", owner)
    padded = with_halo(transported_quantities.astype(jnp.bfloat16), (("gx", 2),), 1).astype(
        transported_quantities.dtype
    )
    slope, curve = line_terms(
        lax.all_to_all(flattened[0:1], "wa", split_axis=2, concat_axis=1, tiled=True),
        implicit_derivative_matrix,
    )
    mixture_lines = lax.all_to_all(
        jnp.stack([slope, curve], axis=1), "wa", split_axis=2, concat_axis=3, tiled=True
    )
    slope, curve = line_terms(
        lax.all_to_all(flattened[1:2], "wa", split_axis=2, concat_axis=1, tiled=True),
        implicit_derivative_matrix,
    )
    heat_lines = lax.all_to_all(curve[:, None], "wa", split_axis=2, concat_axis=3, tiled=True)
    returned = jnp.concatenate([mixture_lines, heat_lines], axis=1)
    returned = returned.reshape(3, row_count, plane_count, depth_count)
    mixture_radial_slope = returned[0]
    radial_curve = returned[1:3]
    depth_slope = jnp.einsum(
        "fyxj,kj->fyxk", rounded, implicit_derivative_matrix, preferred_element_type=jnp.float32
    ).astype(jnp.bfloat16)
    depth_curve = jnp.einsum(
        "fyxj,kj->fyxk", depth_slope, implicit_derivative_matrix, preferred_element_type=jnp.float32
    )
    coflow = jnp.array([0.0, 1.0], jnp.float32)[:, None, None]
    inflow_cells = jnp.where(
        orifice_region_flag[None] == 1, database_plane.astype(jnp.float32), coflow
    )
    slab_index = lax.axis_index("gx")
    slab_count = lax.axis_size("gx")
    upstream_edge = jnp.where(slab_index == 0, inflow_cells, padded[:, :, 0])
    downstream_edge = jnp.where(
        slab_index == slab_count - 1, transported_quantities[:, :, -1], padded[:, :, -1]
    )
    extended = jnp.concatenate(
        [upstream_edge[:, :, None], transported_quantities, downstream_edge[:, :, None]], axis=2
    )
    upstream = extended[:, :, :-2]
    downstream = extended[:, :, 2:]
    axial_slope = (downstream - upstream) * 0.5
    axial_curve = downstream - 2.0 * transported_quantities + upstream
    radial_float = mixture_radial_slope.astype(jnp.float32)
    depth_float = depth_slope[0].astype(jnp.float32)
    dissipation = (
        2.0 * mixing_diffusivity * (axial_slope[0] ** 2 + radial_float**2 + depth_float**2)
    )
    laplace = axial_curve + radial_curve.astype(jnp.float32) + depth_curve
    diffusivity = jnp.array([mixing_diffusivity, heat_diffusivity], jnp.float32)[
        :, None, None, None
    ]
    release = jnp.stack([jnp.zeros_like(dissipation), release_rate * dissipation])
    plane_numbers = (slab_index * plane_count + jnp.arange(plane_count, dtype=jnp.int32)).astype(
        jnp.float32
    )
    fringe = (1.0 / (1.0 + plane_numbers / plane_count))[None, None, :, None]
    relaxation = fringe * (inflow_cells[:, :, None, :] - transported_quantities)
    rhs = (
        -streamwise_speed[None, :, None, :] * axial_slope
        + diffusivity * laplace
        + release
        + relaxation
    )
    updated = transported_quantities + phase_step * rhs
    block_sums = dissipation.reshape(row_count, plane_count, depth_count // ZBLK, ZBLK).sum(axis=-1)
    local_bins = jax.ops.segment_sum(
        block_sums.reshape(-1), joint_frequency_class.reshape(-1), num_segments=HB * HB
    )
    summed = lax.psum(local_bins, ("gx", "wa"))
    per_bin = row_count * lax.axis_size("wa") * plane_count * slab_count * depth_count // (HB * HB)
    histogram = (summed / per_bin).reshape(HB, HB)
    return (updated[0], updated[1], histogram)


def solution(mesh):
    in_specs = (
        P("wa", "gx", None),
        P("wa", "gx", None),
        P("wa", None),
        P(),
        P(None, "wa", "gx", None),
        P("wa", None),
        P(),
        P("wa", "gx", None),
    )
    out_specs = (P("wa", "gx", None), P("wa", "gx", None), P())
    return jax.shard_map(body, mesh=mesh, in_specs=in_specs, out_specs=out_specs, check_vma=False)
```

profile of v0, /device:TPU:1, one launch (start us, length us, event | category | flops | bytes accessed | tf_op | source)
XLA Modules:
  0.0 657.2 jit_solution(7611706944321994911)
XLA Ops:
  10.6 14.3 %copy.57 = bf16[1,24,18432]{1,0,2:T(2,128)(2,1)} copy(bf16[1,24,18432]{2,1,0:T(8,128)(2,1)S(1)} %bitcast.127) | data formatting | bytes 1769472 | tf_op jit(solution)/shard_map/slice | solution.py:80
  25.5 101.9 %reduce = bf16[18432,24]{1,0:T(8,128)(2,1)} reduce(bf16[18432,1,24]{2,1,0:T(2,128)(2,1)} %bitcast.109, bf16[]{:T(256)} %broadcast.51), dimensions={1}, to_apply=%bitcast.91.reduce_sub_computation | reduce | bytes 1769474
  127.4 8.6 %reshape.108 = bf16[64,2,3456]{2,1,0:T(2,128)(2,1)} reshape(bf16[18432,24]{1,0:T(8,128)(2,1)} %reduce) | data formatting | bytes 1769472
  136.0 13.8 %all-to-all-start.2 = ((bf16[64,2,3456]{2,1,0:T(2,128)(2,1)}), bf16[64,2,3456]{2,1,0:T(2,128)(2,1)S(1)}, u32[]{:S(2)}, u32[]{:S(2)}) async-start(bf16[64,2,3456]{2,1,0:T(2,128)(2,1)} %reshape.108), calls=%async_computation.2 | async-start | bytes 1769472 | tf_op jit(solution)/shard_map/all_to_all | solution.py:80
  152.0 17.5 %copy.50 = bf16[1,24,18432]{1,0,2:T(2,128)(2,1)} copy(bf16[1,24,18432]{2,1,0:T(8,128)(2,1)} %bitcast.128) | data formatting | bytes 1769472 | tf_op jit(solution)/shard_map/slice | solution.py:73
  169.4 101.9 %reduce.2 = bf16[18432,24]{1,0:T(8,128)(2,1)} reduce(bf16[18432,1,24]{2,1,0:T(2,128)(2,1)} %bitcast.110, bf16[]{:T(256)} %broadcast.51), dimensions={1}, to_apply=%bitcast.95.reduce_sub_computation | reduce | bytes 1769474
  271.4 8.6 %reshape.112 = bf16[64,2,3456]{2,1,0:T(2,128)(2,1)} reshape(bf16[18432,24]{1,0:T(8,128)(2,1)} %reduce.2) | data formatting | bytes 1769472
  280.0 10.8 %all-to-all-start = ((bf16[64,2,3456]{2,1,0:T(2,128)(2,1)}), bf16[64,2,3456]{2,1,0:T(2,128)(2,1)}, u32[]{:S(2)}, u32[]{:S(2)}) async-start(bf16[64,2,3456]{2,1,0:T(2,128)(2,1)} %reshape.112), calls=%async_computation | async-start | bytes 1769472 | tf_op jit(solution)/shard_map/all_to_all | solution.py:73
  290.8 18.3 %reshape.109 = bf16[18432,1,24]{2,1,0:T(2,128)(2,1)} reshape(bf16[64,2,3456]{2,1,0:T(2,128)(2,1)S(1)} %all-to-all-done.2) | data formatting | bytes 1769472
  309.1 17.9 %copy.58 = bf16[1,24,18432]{2,1,0:T(8,128)(2,1)} copy(bf16[1,24,18432]{1,0,2:T(2,128)(2,1)} %bitcast.111) | data formatting | bytes 1769472 | tf_op jit(solution)/shard_map/all_to_all | solution.py:80
  331.7 7.9 %fusion.19 = bf16[1,1,1536,288]{2,3,1,0:T(8,128)(2,1)S(1)} fusion(bf16[1536,1536]{1,0:T(8,128)(2,1)} %param.13, bf16[1536,288]{1,0:T(8,128)(2,1)} %bitcast.129), kind=kOutput, calls=%fused_computation.28 | convolution fusion | flops 2718793728 | bytes 6488064 | tf_op jit(solution)/shard_map/ij,...jc->...ic/dot_general | solution.py:38
  344.3 9.4 %reduce.1 = bf16[1536,288]{1,0:T(8,128)(2,1)S(1)} reduce(bf16[1536,1,1,288]{3,2,1,0:T(2,128)(2,1)} %bitcast.121, bf16[]{:T(256)} %broadcast.51), dimensions={1,2}, to_apply=%bitcast.93.reduce_sub_computation | reduce | bytes 1769474
  356.5 10.5 %all-to-all-start.3 = ((bf16[64,2,3456]{2,1,0:T(2,128)(2,1)}), bf16[64,2,3456]{2,1,0:T(2,128)(2,1)}, u32[]{:S(2)}, u32[]{:S(2)}) async-start(bf16[64,2,3456]{2,1,0:T(2,128)(2,1)} %reshape.110), calls=%async_computation.3 | async-start | bytes 1769472 | tf_op jit(solution)/shard_map/all_to_all | solution.py:83
  373.9 21.2 %reshape.113 = bf16[18432,1,24]{2,1,0:T(2,128)(2,1)} reshape(bf16[64,2,3456]{2,1,0:T(2,128)(2,1)} %all-to-all-done) | data formatting | bytes 1769472
  395.1 17.9 %copy.51 = bf16[1,24,18432]{2,1,0:T(8,128)(2,1)} copy(bf16[1,24,18432]{1,0,2:T(2,128)(2,1)} %bitcast.112) | data formatting | bytes 1769472 | tf_op jit(solution)/shard_map/all_to_all | solution.py:73
  424.5 6.6 %copy.53 = bf16[1,2,1536,288]{3,1,0,2:T(2,128)(2,1)} copy(bf16[1,2,1536,288]{2,3,1,0:T(8,128)(2,1)} %pad_maximum_fusion.6) | data formatting | bytes 3538944 | tf_op jit(solution)/shard_map/stack | solution.py:77
  431.1 11.2 %all-to-all-start.1 = ((bf16[1,2,1536,288]{3,1,0,2:T(2,128)(2,1)}), bf16[1,2,1536,288]{3,1,0,2:T(2,128)(2,1)}, u32[]{:S(2)}, u32[]{:S(2)}) async-start(bf16[1,2,1536,288]{3,1,0,2:T(2,128)(2,1)} %copy.53), calls=%async_computation.1 | async-start | bytes 4718592 | tf_op jit(solution)/shard_map/all_to_all | solution.py:76
  444.1 6.7 %fusion.13 = bf16[2,24,12,1536]{3,1,2,0:T(8,128)(2,1)} fusion(bf16[2,24,12,1536]{3,1,2,0:T(8,128)(2,1)S(1)} %fusion.16, bf16[1536,1536]{1,0:T(8,128)(2,1)} %param.13), kind=kOutput, calls=%fused_computation.20 | convolution fusion | flops 2718793728 | bytes 8257536 | tf_op jit(solution)/shard_map/fyxj,kj->fyxk/dot_general | solution.py:88
  452.6 39.1 %all-reduce.3.cloned.1.call-done = bf16[2,24,1536]{2,1,0:T(8,128)(2,1)} async-done(((bf16[2,24,1536]{2,1,0:T(8,128)(2,1)}), bf16[2,24,1536]{2,1,0:T(8,128)(2,1)}) %all-reduce.3.cloned.1.call-update) | async-done | bytes 147472 | tf_op jit(solution)/shard_map/psum | solution.py:18
  498.6 7.3 %reshape.111 = bf16[1536,1,1,288]{3,2,1,0:T(2,128)(2,1)S(1)} reshape(bf16[64,2,3456]{2,1,0:T(2,128)(2,1)} %all-to-all-done.3) | data formatting | bytes 1769472
  522.7 5.4 reshape.95
  534.1 7.6 %fusion.10 = f32[2,24,12,1536]{3,1,2,0:T(8,128)S(1)} fusion(f32[2,24,12,1536]{3,2,1,0:T(8,128)S(1)} %copy-done.8, f32[1,24,12,1536]{3,1,2,0:T(8,128)S(1)} %get-tuple-element.4, bf16[2,24,12,1536]{3,1,2,0:T(8,128)(2,1)S(1)} %copy-done.11, bf16[1536,1536]{1,0:T(8,128)(2,1)} %param.13, f32[1,24,12,1536]{3,1,2,0:T(8,128)S(1)} %bitcast.116, ...), kind=kOutput, calls=%fused_computation.19 | convolution fusion | flops 2735603712 | bytes 19906616 | tf_op jit(solution)/shard_map/fyxj,kj->fyxk/dot_general | solution.py:91
  552.1 19.4 %scatter_custom_fusion = f32[4096]{0:T(1024)S(1)} fusion(s32[3456]{0:T(1024)S(1)} %reshape.98, f32[3456]{0:T(1024)S(1)} %reshape.100, f32[]{:T(128)} %constant.62.clone.1), kind=kCustom, calls=%fused_computation.61 | custom fusion | flops 3456 | bytes 16388 | tf_op jit(solution)/shard_map/scatter-add | solution.py:134
  571.5 77.6 %psum.15 = f32[4096]{0:T(1024)S(1)} all-reduce(f32[4096]{0:T(1024)S(1)} %scatter_custom_fusion), channel_id=1, replica_groups=mesh['gx'=4,'wa'=64] {'gx','wa'}, use_global_device_ids=true, to_apply=%region_3.4 | all-reduce | flops 4096 | bytes 32768 | tf_op jit(solution)/shard_map/psum | solution.py:137
  (97 shorter events, 80.0 us)
Async XLA Ops:
  7.2 435.2 %copy-start = (bf16[2,24,2,1536]{3,2,1,0:T(2,128)(2,1)S(1)}, bf16[2,24,2,1536]{3,2,1,0:T(2,128)(2,1)}, u32[]{:S(2)}) copy-start(bf16[2,24,2,1536]{3,2,1,0:T(2,128)(2,1)} %param.14) | copy-start | bytes 884740
  136.0 144.0 %all-to-all-start.2 = ((bf16[64,2,3456]{2,1,0:T(2,128)(2,1)}), bf16[64,2,3456]{2,1,0:T(2,128)(2,1)S(1)}, u32[]{:S(2)}, u32[]{:S(2)}) async-start(bf16[64,2,3456]{2,1,0:T(2,128)(2,1)} %reshape.108), calls=%async_computation.2 | async-start | bytes 1769472 | tf_op jit(solution)/shard_map/all_to_all | solution.py:80
  280.0 76.5 %all-to-all-start = ((bf16[64,2,3456]{2,1,0:T(2,128)(2,1)}), bf16[64,2,3456]{2,1,0:T(2,128)(2,1)}, u32[]{:S(2)}, u32[]{:S(2)}) async-start(bf16[64,2,3456]{2,1,0:T(2,128)(2,1)} %reshape.112), calls=%async_computation | async-start | bytes 1769472 | tf_op jit(solution)/shard_map/all_to_all | solution.py:73
  356.5 74.6 %all-to-all-start.3 = ((bf16[64,2,3456]{2,1,0:T(2,128)(2,1)}), bf16[64,2,3456]{2,1,0:T(2,128)(2,1)}, u32[]{:S(2)}, u32[]{:S(2)}) async-start(bf16[64,2,3456]{2,1,0:T(2,128)(2,1)} %reshape.110), calls=%async_computation.3 | async-start | bytes 1769472 | tf_op jit(solution)/shard_map/all_to_all | solution.py:83
  367.7 83.9 %collective-permute-start.1 = (bf16[2,24,1,1536]{3,1,2,0:T(8,128)(2,1)}, bf16[2,24,1,1536]{3,1,2,0:T(8,128)(2,1)S(1)}, u32[]{:S(2)}, u32[]{:S(2)}) collective-permute-start(bf16[2,24,1,1536]{3,1,2,0:T(8,128)(2,1)} %get-tuple-element.9), channel_id=1, source_target_pairs={{64,0},{128,64},{192,128},{65,1},{129,65},{193,129},{66,2},{130,66... | collective-permute-start | bytes 442376 | tf_op jit(solution)/shard_map/ppermute | solution.py:29
  369.0 82.6 %collective-permute-start = (bf16[2,24,1,1536]{3,1,2,0:T(8,128)(2,1)}, bf16[2,24,1,1536]{3,1,2,0:T(8,128)(2,1)S(1)}, u32[]{:S(2)}, u32[]{:S(2)}) collective-permute-start(bf16[2,24,1,1536]{3,1,2,0:T(8,128)(2,1)} %get-tuple-element.8), channel_id=1, source_target_pairs={{0,64},{64,128},{128,192},{1,65},{65,129},{129,193},{2,66},{66,130... | collective-permute-start | bytes 442376 | tf_op jit(solution)/shard_map/ppermute | solution.py:26
  416.0 5.5 slice-start
  416.7 4.8 slice-start.1
  431.1 12.3 %copy-start.13 = (f32[24,1536]{1,0:T(8,128)S(1)}, f32[24,1536]{1,0:T(8,128)}, u32[]{:S(2)}) copy-start(f32[24,1536]{1,0:T(8,128)} %param.12) | copy-start | bytes 442372
  431.1 76.7 %all-to-all-start.1 = ((bf16[1,2,1536,288]{3,1,0,2:T(2,128)(2,1)}), bf16[1,2,1536,288]{3,1,0,2:T(2,128)(2,1)}, u32[]{:S(2)}, u32[]{:S(2)}) async-start(bf16[1,2,1536,288]{3,1,0,2:T(2,128)(2,1)} %copy.53), calls=%async_computation.1 | async-start | bytes 4718592 | tf_op jit(solution)/shard_map/all_to_all | solution.py:76
  442.3 49.5 %all-reduce.3.cloned.1.call-start = ((), (), s32[]{:S(2)}) async-start(), calls=%async_computation.4 | async-start | bytes 294912 | tf_op jit(solution)/shard_map/psum | solution.py:18
  444.1 6.7 %copy-start.14 = (s32[24,1536]{1,0:T(8,128)S(1)}, s32[24,1536]{1,0:T(8,128)}, u32[]{:S(2)}) copy-start(s32[24,1536]{1,0:T(8,128)} %param.15) | copy-start | bytes 442372
  444.1 6.7 %copy-start.16 = (s32[24,12,12]{0,2,1:T(8,128)S(1)}, s32[24,12,12]{0,2,1:T(8,128)}, u32[]{:S(2)}) copy-start(s32[24,12,12]{0,2,1:T(8,128)} %param.17) | copy-start | bytes 41476
  522.7 5.4 copy-start.6
  522.7 10.4 %copy-start.12 = (f32[2,24,1536]{2,1,0:T(8,128)S(1)}, f32[2,24,1536]{2,1,0:T(8,128)}, u32[]{:S(2)}) copy-start(f32[2,24,1536]{2,1,0:T(8,128)} %get-tuple-element.12) | copy-start | bytes 884740
  522.7 10.4 %copy-start.15 = (f32[24,1536]{1,0:T(8,128)S(1)}, f32[24,1536]{1,0:T(8,128)}, u32[]{:S(2)}) copy-start(f32[24,1536]{1,0:T(8,128)} %negate_multiply_fusion) | copy-start | bytes 442372
  528.1 5.1 copy-start.3
  528.1 5.1 copy-start.4
  528.1 5.1 copy-start.8
  528.1 5.1 copy-start.10
  528.1 6.0 copy-start.11
  528.1 6.0 copy-start.17
  528.1 6.0 copy-start.18
  545.7 104.1 %copy-start.1 = (bf16[2,24,2,1536]{3,2,1,0:T(2,128)(2,1)S(1)}, bf16[2,24,2,1536]{3,2,1,0:T(2,128)(2,1)}, u32[]{:S(2)}) copy-start(bf16[2,24,2,1536]{3,2,1,0:T(2,128)(2,1)} %param.14) | copy-start | bytes 884740
  (4 other events, 8.6 us)
Sparse Core Ops, SparseCore 0:
  446.0 45.6 all-reduce.2
where the time goes:
time: 670 us; the launch traced here: 657 us
  other arithmetic  258 us (39%)
  local copies, waits for them, and re-layouts  187 us (28%)
  blocking collectives  77.6 us (12%)
  starting transfers between devices  51.8 us (8%)
  waiting for transfers between devices  39.2 us (6%)
  matrix products  28.6 us (4%)
  between operations  15.6 us (2%)
    unnamed x4, other arithmetic  213 us
    psum x1, blocking collectives, body(): summed = lax.psum(local_bins, ('gx', 'wa'))  77.6 us
    unnamed x52, local copies, waits for them, and re-layouts  70.6 us
    psum x1, waiting for transfers between devices, from_root(): return lax.psum(block, axis)  39.1 us
    all_to_all x3, local copies, waits for them, and re-layouts, body(): lax.all_to_all(flattened[1:2], 'wa', split_axis=2, concat_axis=1, tiled=T...  22.6 us
    all_to_all x3, local copies, waits for them, and re-layouts, body(): lax.all_to_all(flattened[0:1], 'wa', split_axis=2, concat_axis=1, tiled=T...  21.6 us
    slice x2, local copies, waits for them, and re-layouts, body(): flattened[0:1]  19.6 us
    scatter-add x1, other arithmetic, body(): jax.ops.segment_sum(block_sums.reshape(-1), joint_frequency_class.reshape...  19.4 us
  transfers between devices with their start and end apart: 7, of which 1 were waited for; matrix products, arithmetic and copies ran while one was open for 41% of the time, Pallas kernels for 0%

commit v1 on v0

v1 whole, which is shorter than its diff:
```python
import functools

import jax
import jax.numpy as jnp
from jax import lax
from jax.experimental import pallas as pl
from jax.experimental.pallas import tpu as pltpu
from jax.sharding import PartitionSpec as P

HB = 64
ZBLK = 128
LANES = 128
ROWS = 8

mixing_diffusivity = 0.3
heat_diffusivity = 0.4
release_rate = 0.5
phase_step = 0.2

VMEM_LIMIT = 56 * 1024 * 1024


def lane_group(shape):
    return lax.broadcasted_iota(jnp.int32, shape, len(shape) - 1) // 32


def blocks(planes, depth):
    per_plane = depth // ZBLK
    for block in range(planes * per_plane):
        yield block, block // per_plane, (block % per_plane) * ZBLK


def pack_kernel(x_ref, spare_ref, out_ref):
    planes, _, depth = x_ref.shape
    whole = 2 * out_ref.shape[0]
    group = lane_group((ROWS, LANES))
    for block, p, k in blocks(planes, depth):
        tiles = [x_ref[p, ROWS * t : ROWS * t + ROWS, k : k + ZBLK] for t in range(3)]
        if block < whole:
            for t in range(3):
                out_ref[block // 2, 3 * (block % 2) + t] = tiles[t].astype(jnp.bfloat16)
            continue
        for q in range(4):
            line = 4 * (block - whole) + q
            packed = spare_ref[line] if spare_ref is not None else jnp.zeros_like(tiles[0])
            for g in range(3):
                shift = (32 * (g - q)) % LANES
                moved = pltpu.roll(tiles[g], shift, 1) if shift else tiles[g]
                packed = jnp.where(group == g, moved, packed)
            out_ref[line, 6] = packed.astype(jnp.bfloat16)


def pack(x, lines, spare=None):
    body = pack_kernel if spare is not None else lambda x_ref, out_ref: pack_kernel(x_ref, None, out_ref)
    operands = (x,) if spare is None else (x, spare)
    return pl.pallas_call(
        body,
        out_shape=jax.ShapeDtypeStruct((lines, 7, ROWS, LANES), jnp.bfloat16),
        compiler_params=pltpu.CompilerParams(vmem_limit_bytes=VMEM_LIMIT),
        cost_estimate=pl.CostEstimate(flops=x.size, bytes_accessed=6 * x.size, transcendentals=0),
        name="pack",
    )(*operands)


def unpack_add_kernel(scale, part_ref, ret_ref, out_ref):
    planes, _, depth = part_ref.shape
    whole = 2 * ret_ref.shape[0]
    group = lane_group((ROWS, LANES))
    for block, p, k in blocks(planes, depth):
        if block < whole:
            tiles = [ret_ref[block // 2, 3 * (block % 2) + t].astype(jnp.float32) for t in range(3)]
        else:
            quarters = [ret_ref[4 * (block - whole) + q, 6].astype(jnp.float32) for q in range(4)]
            tiles = []
            for g in range(3):
                tile = None
                for q in range(4):
                    shift = (32 * (q - g)) % LANES
                    moved = pltpu.roll(quarters[q], shift, 1) if shift else quarters[q]
                    tile = moved if tile is None else jnp.where(group == q, moved, tile)
                tiles.append(tile)
        for t in range(3):
            at = (p, slice(ROWS * t, ROWS * t + ROWS), slice(k, k + ZBLK))
            out_ref[at] = part_ref[at] + scale * tiles[t]


def unpack_add(part, ret, scale):
    return pl.pallas_call(
        functools.partial(unpack_add_kernel, scale),
        out_shape=jax.ShapeDtypeStruct(part.shape, jnp.float32),
        compiler_params=pltpu.CompilerParams(vmem_limit_bytes=VMEM_LIMIT),
        cost_estimate=pl.CostEstimate(flops=2 * part.size, bytes_accessed=10 * part.size, transcendentals=0),
        name="unpack_add",
    )(part, ret)


SOURCES = 16


def unpack_lines(r_ref, x_ref):
    def step(i, carry):
        src = pl.ds(i * SOURCES, SOURCES)
        rows = pl.ds(pl.multiple_of(i * (24 * SOURCES), 24 * SOURCES), 24 * SOURCES)
        for b in range(2):
            tiles = r_ref[src, 3 * b : 3 * b + 3].astype(jnp.float32)
            x_ref[rows, b * LANES : (b + 1) * LANES] = tiles.reshape(24 * SOURCES, LANES).astype(jnp.bfloat16)
        last = r_ref[src, 6].astype(jnp.float32).reshape(ROWS * SOURCES, LANES)
        parts = [last] + [pltpu.roll(last, LANES - 32 * g, 1) for g in (1, 2)]
        tiles = jnp.stack([part.reshape(SOURCES, ROWS, LANES) for part in parts], axis=1)
        x_ref[rows, 2 * LANES : 3 * LANES] = tiles.reshape(24 * SOURCES, LANES).astype(jnp.bfloat16)
        return carry

    lax.fori_loop(0, r_ref.shape[0] // SOURCES, step, 0)


def pack_lines(values, out_ref, i):
    src = pl.ds(i * SOURCES, SOURCES)
    for b in range(2):
        tiles = values[:, b * LANES : (b + 1) * LANES].reshape(SOURCES, 3, ROWS, LANES)
        out_ref[src, 3 * b : 3 * b + 3] = tiles.astype(jnp.bfloat16)
    tiles = values[:, 2 * LANES :].reshape(SOURCES, 3, ROWS, LANES)
    group = lane_group((ROWS * SOURCES, LANES))
    packed = jnp.zeros((ROWS * SOURCES, LANES), jnp.float32)
    for g in range(3):
        tile = tiles[:, g].reshape(ROWS * SOURCES, LANES)
        packed = jnp.where(group == g, pltpu.roll(tile, 32 * g, 1) if g else tile, packed)
    out_ref[src, 6] = packed.reshape(SOURCES, ROWS, LANES).astype(jnp.bfloat16)


def line_kernel(heat, *refs):
    if heat:
        r_ref, d_ref, mixture_slope_ref, out_ref, x_ref, slope_ref = refs
    else:
        r_ref, d_ref, out_ref, slope_ref, sums_ref, x_ref = refs
    unpack_lines(r_ref, x_ref)
    tile = 24 * SOURCES
    count = r_ref.shape[0] // SOURCES

    def slope_step(i, carry):
        rows = pl.ds(pl.multiple_of(i * tile, tile), tile)
        slope = jnp.dot(d_ref[rows, :], x_ref[...], preferred_element_type=jnp.float32).astype(jnp.bfloat16)
        slope_ref[rows, :] = slope
        if not heat:
            squared = slope.astype(jnp.float32) ** 2
            lane = lax.broadcasted_iota(jnp.int32, (tile, LANES), 1)
            sums = jnp.zeros((tile, LANES), jnp.float32)
            for b in range(3):
                part = squared[:, b * LANES : (b + 1) * LANES]
                if b == 2:
                    part = jnp.where(lane < 32, part, 0.0)
                sums = jnp.where(lane == b, jnp.sum(part, axis=1, keepdims=True), sums)
            sums_ref[rows, :] = sums
        return carry

    lax.fori_loop(0, count, slope_step, 0)

    def curve_step(i, carry):
        rows = pl.ds(pl.multiple_of(i * tile, tile), tile)
        curve = jnp.dot(d_ref[rows, :], slope_ref[...], preferred_element_type=jnp.float32)
        if heat:
            slope = mixture_slope_ref[rows, :].astype(jnp.float32)
            curve = heat_diffusivity * curve + (release_rate * 2.0 * mixing_diffusivity) * slope**2
        pack_lines(curve, out_ref, i)
        return carry

    lax.fori_loop(0, count, curve_step, 0)


def line_call(received, matrix, mixture_slope=None):
    heat = mixture_slope is not None
    rows = matrix.shape[0]
    packet = jax.ShapeDtypeStruct(received.shape, jnp.bfloat16)
    wide = (rows, 3 * LANES)
    if heat:
        out_shape = packet
        scratch = [pltpu.VMEM(wide, jnp.bfloat16), pltpu.VMEM(wide, jnp.bfloat16)]
        operands = (received, matrix, mixture_slope)
    else:
        out_shape = (
            packet,
            jax.ShapeDtypeStruct(wide, jnp.bfloat16),
            jax.ShapeDtypeStruct((rows, LANES), jnp.float32),
        )
        scratch = [pltpu.VMEM(wide, jnp.bfloat16)]
        operands = (received, matrix)
    return pl.pallas_call(
        functools.partial(line_kernel, heat),
        out_shape=out_shape,
        scratch_shapes=scratch,
        compiler_params=pltpu.CompilerParams(vmem_limit_bytes=VMEM_LIMIT),
        cost_estimate=pl.CostEstimate(
            flops=4 * rows * rows * 3 * LANES, bytes_accessed=2 * rows * rows + 8 * rows * LANES, transcendentals=0
        ),
        name="heat_lines" if heat else "mixture_lines",
    )(*operands)


def local_kernel(
    fringe_ref, lo_ref, hi_ref, *refs
):
    fields = (refs[0:3], refs[3:6])
    slope_ref, curve_ref, speed_ref, inflow_ref, mix_ref, heat_ref, sums_ref = refs[6:]
    p = pl.program_id(0)
    last = pl.num_programs(0) - 1
    fringe = fringe_ref[p]
    speed = speed_ref[...]
    dissipation = None
    for f, (before, here, after) in enumerate(fields):
        x = here[0]
        upstream = jnp.where(p == 0, lo_ref[f], before[0])
        downstream = jnp.where(p == last, hi_ref[f], after[0])
        axial_slope = (downstream - upstream) * 0.5
        axial_curve = downstream - 2.0 * x + upstream
        diffusivity = (mixing_diffusivity, heat_diffusivity)[f]
        rhs = -speed * axial_slope + diffusivity * (axial_curve + curve_ref[f, 0]) + fringe * (inflow_ref[f] - x)
        if f == 0:
            depth = slope_ref[0, 0].astype(jnp.float32)
            dissipation = (2.0 * mixing_diffusivity) * (axial_slope**2 + depth**2)
            mix_ref[0] = x + phase_step * rhs
        else:
            heat_ref[0] = x + phase_step * (rhs + release_rate * dissipation)
    lane = lax.broadcasted_iota(jnp.int32, sums_ref.shape[1:], 1)
    sums = jnp.zeros(sums_ref.shape[1:], jnp.float32)
    for k in range(dissipation.shape[1] // ZBLK):
        part = jnp.sum(dissipation[:, k * ZBLK : (k + 1) * ZBLK], axis=1, keepdims=True)
        sums = jnp.where(lane == k, part, sums)
    sums_ref[0] = sums


def local_terms(x0, x1, lo, hi, slope, curve, speed, inflow, fringe):
    planes, rows, depth = x0.shape
    plane = lambda move: pl.BlockSpec((1, rows, depth), lambda p: (jnp.clip(p + move, 0, planes - 1), 0, 0))
    fixed = lambda shape: pl.BlockSpec(shape, lambda p: (0,) * len(shape))
    return pl.pallas_call(
        local_kernel,
        grid=(planes,),
        in_specs=[
            pl.BlockSpec(memory_space=pltpu.SMEM),
            fixed((2, rows, depth)),
            fixed((2, rows, depth)),
            plane(-1),
            plane(0),
            plane(1),
            plane(-1),
            plane(0),
            plane(1),
            pl.BlockSpec((1, 1, rows, depth), lambda p: (0, p, 0, 0)),
            pl.BlockSpec((2, 1, rows, depth), lambda p: (0, p, 0, 0)),
            fixed((rows, depth)),
            fixed((2, rows, depth)),
        ],
        out_specs=[
            pl.BlockSpec((1, rows, depth), lambda p: (p, 0, 0)),
            pl.BlockSpec((1, rows, depth), lambda p: (p, 0, 0)),
            pl.BlockSpec((1, rows, LANES), lambda p: (p, 0, 0)),
        ],
        out_shape=[
            jax.ShapeDtypeStruct((planes, rows, depth), jnp.float32),
            jax.ShapeDtypeStruct((planes, rows, depth), jnp.float32),
            jax.ShapeDtypeStruct((planes, rows, LANES), jnp.float32),
        ],
        compiler_params=pltpu.CompilerParams(vmem_limit_bytes=VMEM_LIMIT),
        cost_estimate=pl.CostEstimate(flops=60 * x0.size, bytes_accessed=34 * x0.size, transcendentals=0),
        name="local_terms",
    )(fringe, lo, hi, x0, x0, x0, x1, x1, x1, slope, curve, speed, inflow)


def bin_sums(values, classes):
    row = classes // HB
    column = classes % HB
    bins = jnp.arange(HB, dtype=jnp.int32)[:, None]
    columns = (bins == column[None]).astype(jnp.bfloat16)
    total = 0.0
    for _ in range(3):
        term = values.astype(jnp.bfloat16)
        values = values - term.astype(jnp.float32)
        rows = jnp.where(bins == row[None], term[None], jnp.zeros((), jnp.bfloat16))
        total = total + jnp.einsum("rn,cn->rc", rows, columns, preferred_element_type=jnp.float32)
    return total


def all_sum(block):
    for axis in ("wa", "gx"):
        count = lax.axis_size(axis)
        step = 1
        while step < count:
            block = block + lax.ppermute(block, axis, [(i, i ^ step) for i in range(count)])
            step *= 2
    return block


def body(
    mixing_ratio,
    thermal_state,
    streamwise_speed,
    implicit_derivative_matrix,
    stored_entry_slices,
    orifice_region_flag,
    arriving_slice_number,
    joint_frequency_class,
):
    matrix = implicit_derivative_matrix
    row_count, plane_count, depth_count = mixing_ratio.shape
    lines = lax.axis_size("wa")
    slab_index = lax.axis_index("gx")
    slab_count = lax.axis_size("gx")
    x0 = jnp.transpose(mixing_ratio, (1, 0, 2))
    x1 = jnp.transpose(thermal_state, (1, 0, 2))

    def exchange(packets):
        return lax.all_to_all(packets, "wa", split_axis=0, concat_axis=0, tiled=True)

    classes = joint_frequency_class.reshape(3, ROWS, plane_count * depth_count // ZBLK)
    whole = classes[:, :, : 2 * lines].reshape(3, ROWS, lines, 2)
    quarter = jnp.repeat(classes[:, :, 2 * lines :], 4, axis=2)[..., None]
    sent_classes = jnp.concatenate([whole, quarter], axis=3).transpose(2, 1, 0, 3).reshape(lines, ROWS, 9)
    spare = jnp.concatenate([sent_classes // HB, sent_classes % HB], axis=2).astype(jnp.float32)
    spare = jnp.pad(spare, ((0, 0), (0, 0), (96, LANES - 96 - 18)))

    lines0 = exchange(pack(x0, lines))
    lines1 = exchange(pack(x1, lines, spare))

    held_count = stored_entry_slices.shape[2]
    plane_index = arriving_slice_number[0]
    owner = plane_index // held_count
    held_plane = lax.dynamic_index_in_dim(stored_entry_slices, plane_index % held_count, 2, keepdims=False)
    database_plane = held_plane
    for move in range(1, slab_count):
        table = [(i, (i + move) % slab_count) for i in range(slab_count)]
        arrived = lax.ppermute(held_plane, "gx", table)
        database_plane = jnp.where((slab_index - move) % slab_count == owner, arrived, database_plane)
    forward = [(i, i + 1) for i in range(slab_count - 1)]
    backward = [(target, source) for source, target in forward]
    first = jnp.stack([x0[0], x1[0]])
    final = jnp.stack([x0[-1], x1[-1]])
    before = lax.ppermute(final.astype(jnp.bfloat16), "gx", forward).astype(jnp.float32)
    after = lax.ppermute(first.astype(jnp.bfloat16), "gx", backward).astype(jnp.float32)
    coflow = jnp.array([0.0, 1.0], jnp.float32)[:, None, None]
    inflow_cells = jnp.where(orifice_region_flag[None] == 1, database_plane.astype(jnp.float32), coflow)
    lo = jnp.where(slab_index == 0, inflow_cells, before)
    hi = jnp.where(slab_index == slab_count - 1, final, after)

    rounded = jnp.stack([x0, x1]).astype(jnp.bfloat16)
    depth_slope = jnp.einsum(
        "fxyj,kj->fxyk", rounded, matrix, preferred_element_type=jnp.float32
    ).astype(jnp.bfloat16)
    depth_curve = jnp.einsum("fxyj,kj->fxyk", depth_slope, matrix, preferred_element_type=jnp.float32)
    plane_numbers = (slab_index * plane_count + jnp.arange(plane_count, dtype=jnp.int32)).astype(jnp.float32)
    fringe = 1.0 / (1.0 + plane_numbers / plane_count)
    part0, part1, local_sums = local_terms(
        x0, x1, lo, hi, depth_slope, depth_curve, streamwise_speed, inflow_cells, fringe
    )

    returned0, mixture_slope, line_sums = line_call(lines0, matrix)
    back0 = exchange(returned0)
    returned1 = line_call(lines1, matrix, mixture_slope)
    back1 = exchange(returned1)

    per_plane = depth_count // ZBLK
    own_values = local_sums[:, :, :per_plane].reshape(-1)
    own_classes = joint_frequency_class.transpose(1, 0, 2).reshape(-1)
    line_values = (2.0 * mixing_diffusivity) * line_sums.reshape(lines, 3, ROWS, LANES)[..., :3].reshape(-1)
    codes = lines1[:, 6, :, 96:114].astype(jnp.int32).reshape(lines, ROWS, 2, 3, 3)
    line_classes = (codes[:, :, 0] * HB + codes[:, :, 1]).transpose(0, 2, 1, 3).reshape(-1)
    bins = bin_sums(
        jnp.concatenate([own_values, line_values]), jnp.concatenate([own_classes, line_classes])
    )
    summed = all_sum(bins)
    per_bin = row_count * lines * plane_count * slab_count * depth_count // (HB * HB)
    histogram = summed / per_bin

    mixture_next = unpack_add(part0, back0, phase_step * mixing_diffusivity)
    temperature_next = unpack_add(part1, back1, phase_step)
    return (jnp.transpose(mixture_next, (1, 0, 2)), jnp.transpose(temperature_next, (1, 0, 2)), histogram)


def solution(mesh):
    in_specs = (
        P("wa", "gx", None),
        P("wa", "gx", None),
        P("wa", None),
        P(),
        P(None, "wa", "gx", None),
        P("wa", None),
        P(),
        P("wa", "gx", None),
    )
    out_specs = (P("wa", "gx", None), P("wa", "gx", None), P())
    return jax.shard_map(body, mesh=mesh, in_specs=in_specs, out_specs=out_specs, check_vma=False)
```

time: 670 us -> 204 us (0.30)
  the two profiles are of different devices: /device:TPU:1 before, /device:TPU:10 now
where the time goes in v1:
time: 204 us; the launch traced here: 201 us
  starting transfers between devices  62.8 us (31%)
  waiting for transfers between devices  53 us (26%)
  Pallas kernels  45.3 us (22%)
  matrix products  14.4 us (7%)
  local copies, waits for them, and re-layouts  12.6 us (6%)
  other arithmetic  11 us (5%)
    ppermute x8, waiting for transfers between devices, all_sum(): lax.ppermute(block, axis, [(i, i ^ step) for i in range(count)])  38.2 us
    all_to_all x4, starting transfers between devices, exchange(): lax.all_to_all(packets, 'wa', split_axis=0, concat_axis=0, tiled=True)  38 us
    pallas_call x2, Pallas kernels, line_call(): pl.pallas_call(functools.partial(line_kernel, heat), out_shape=out_shape,...  22 us
    all_to_all x4, waiting for transfers between devices, exchange(): lax.all_to_all(packets, 'wa', split_axis=0, concat_axis=0, tiled=True)  14.8 us
    ppermute x8, starting transfers between devices, all_sum(): lax.ppermute(block, axis, [(i, i ^ step) for i in range(count)])  13.4 us
    pallas_call x1, Pallas kernels, local_terms(): pl.pallas_call(local_kernel, grid=(planes,), in_specs=[pl.BlockSpec(memor...  11.7 us
    dot_general x1, matrix products, body(): jnp.einsum('fxyj,kj->fxyk', depth_slope, matrix, preferred_element_type=j...  7.02 us
    pallas_call x2, Pallas kernels, unpack_add(): pl.pallas_call(functools.partial(unpack_add_kernel, scale), out_shape=jax...  6.4 us
  transfers between devices with their start and end apart: 17, of which 10 were waited for; matrix products, arithmetic and copies ran while one was open for 17% of the time, Pallas kernels for 21%

profile of v1, /device:TPU:10, one launch (start us, length us, event | category | flops | bytes accessed | tf_op | source)
XLA Modules:
  0.0 200.8 jit_solution(12386780463204205402)
XLA Ops:
  11.8 2.6 %pack.2 = bf16[64,7,8,128]{3,2,1,0:T(8,128)(2,1)} custom-call(f32[12,24,1536]{2,1,0:T(8,128)} %bitcast.82), custom_call_target="tpu_custom_call" | custom-call | flops 442368 | bytes 2654208 | tf_op jit(solution)/shard_map/pack/pallas_call | solution.py:56
  14.4 12.4 %all-to-all-start = ((bf16[64,7,8,128]{3,2,1,0:T(8,128)(2,1)}), bf16[64,7,8,128]{3,2,1,0:T(8,128)(2,1)}, u32[]{:S(2)}, u32[]{:S(2)}) async-start(bf16[64,7,8,128]{3,2,1,0:T(8,128)(2,1)} %pack.2), calls=%async_computation | async-start | bytes 1835008 | tf_op jit(solution)/shard_map/all_to_all | solution.py:311
  33.7 4.7 %collective-permute-start.4 = (bf16[2,24,1536]{2,1,0:T(8,128)(2,1)}, bf16[2,24,1536]{2,1,0:T(8,128)(2,1)}, u32[]{:S(2)}, u32[]{:S(2)}) collective-permute-start(bf16[2,24,1536]{2,1,0:T(8,128)(2,1)} %pad_maximum_fusion.1), channel_id=1, source_target_pairs={{64,0},{128,64},{192,128},{65,1},{129,65},{193,129},{66,2},{130,66... | collective-permute-start | bytes 442376 | tf_op jit(solution)/shard_map/ppermute | solution.py:337
  38.4 2.6 %pack.3 = bf16[64,7,8,128]{3,2,1,0:T(8,128)(2,1)} custom-call(f32[12,24,1536]{2,1,0:T(8,128)} %bitcast.77, f32[64,8,128]{2,1,0:T(8,128)} %pad.4.spare_ref), custom_call_target="tpu_custom_call" | custom-call | flops 442368 | bytes 2654208 | tf_op jit(solution)/shard_map/pack/pallas_call | solution.py:56
  42.1 9.0 %all-to-all-done.refs_0_ = bf16[64,7,8,128]{3,2,1,0:T(8,128)(2,1)} async-done(((bf16[64,7,8,128]{3,2,1,0:T(8,128)(2,1)}), bf16[64,7,8,128]{3,2,1,0:T(8,128)(2,1)}, u32[]{:S(2)}, u32[]{:S(2)}) %all-to-all-start) | async-done | bytes 917536 | tf_op jit(solution)/shard_map/all_to_all | solution.py:311
  51.1 7.6 %all-to-all-start.2 = ((bf16[64,7,8,128]{3,2,1,0:T(8,128)(2,1)}), bf16[64,7,8,128]{3,2,1,0:T(8,128)(2,1)S(1)}, u32[]{:S(2)}, u32[]{:S(2)}) async-start(bf16[64,7,8,128]{3,2,1,0:T(8,128)(2,1)} %pack.3), calls=%async_computation.2 | async-start | bytes 1835008 | tf_op jit(solution)/shard_map/all_to_all | solution.py:311
  58.7 5.6 %fusion.4.refs_6_ = bf16[2,12,24,1536]{3,2,1,0:T(8,128)(2,1)S(1)} fusion(bf16[1536,1536]{1,0:T(8,128)(2,1)} %refs_1_.3, bf16[1,12,24,1536]{3,2,1,0:T(8,128)(2,1)} %fusion.47, bf16[1,12,24,1536]{3,2,1,0:T(8,128)(2,1)S(1)} %fusion.46), kind=kOutput, calls=%fused_computation.4 | convolution fusion | flops 2719678464 | bytes 8257536 | tf_op jit(solution)/shard_map/fxyj,kj->fxyk/dot_general | solution.py:344
  65.5 7.0 %fusion.refs_7_ = f32[2,12,24,1536]{3,2,1,0:T(8,128)} fusion(bf16[2,12,24,1536]{3,2,1,0:T(8,128)(2,1)S(1)} %fusion.4.refs_6_, bf16[1536,1536]{1,0:T(8,128)(2,1)} %refs_1_.3), kind=kOutput, calls=%fused_computation | convolution fusion | flops 2717908992 | bytes 10027008 | tf_op jit(solution)/shard_map/fxyj,kj->fxyk/dot_general | solution.py:347
  72.6 11.1 %mixture_lines.1 = (bf16[64,7,8,128]{3,2,1,0:T(8,128)(2,1)}, bf16[1536,384]{1,0:T(8,128)(2,1)}, f32[1536,128]{1,0:T(8,128)}) custom-call(bf16[64,7,8,128]{3,2,1,0:T(8,128)(2,1)} %all-to-all-done.refs_0_, bf16[1536,1536]{1,0:T(8,128)(2,1)} %refs_1_.3), custom_call_target="tpu_custom_call" | custom-call | flops 3623878656 | bytes 6291456 | tf_op jit(solution)/shard_map/mixture_lines/pallas_call | solution.py:186
  84.6 10.9 %heat_lines.1 = bf16[64,7,8,128]{3,2,1,0:T(8,128)(2,1)} custom-call(bf16[64,7,8,128]{3,2,1,0:T(8,128)(2,1)} %copy-done.7, bf16[1536,1536]{1,0:T(8,128)(2,1)} %refs_1_.3, bf16[1536,384]{1,0:T(8,128)(2,1)} %get-tuple-element.12.refs_2_), custom_call_target="tpu_custom_call" | custom-call | flops 3623878656 | bytes 6291456 | tf_op jit(solution)/shard_map/heat_lines/pallas_call | solution.py:186
  95.5 10.4 %all-to-all-start.3 = ((bf16[64,7,8,128]{3,2,1,0:T(8,128)(2,1)}), bf16[64,7,8,128]{3,2,1,0:T(8,128)(2,1)S(1)}, u32[]{:S(2)}, u32[]{:S(2)}) async-start(bf16[64,7,8,128]{3,2,1,0:T(8,128)(2,1)} %heat_lines.1), calls=%async_computation.3 | async-start | bytes 1835008 | tf_op jit(solution)/shard_map/all_to_all | solution.py:311
  110.5 11.7 %local_terms.1 = (f32[12,24,1536]{2,1,0:T(8,128)}, f32[12,24,1536]{2,1,0:T(8,128)}, f32[12,24,128]{2,1,0:T(8,128)}) custom-call(f32[12]{0:T(128)} %add_divide_fusion.fringe_ref, f32[2,24,1536]{2,1,0:T(8,128)} %get-tuple-element.15.lo_ref, f32[2,24,1536]{2,1,0:T(8,128)} %convert_select_fusion.hi_ref, f32[12,24,1536]{2,1,0:T(8,128)} %bitcast.83, ...), custom_call_target="tpu_custom_call" | custom-call | flops 26542080 | bytes 15040512 | tf_op jit(solution)/shard_map/local_terms/pallas_call | solution.py:234
  124.6 5.8 %all-to-all-done.3.ret_ref = bf16[64,7,8,128]{3,2,1,0:T(8,128)(2,1)S(1)} async-done(((bf16[64,7,8,128]{3,2,1,0:T(8,128)(2,1)}), bf16[64,7,8,128]{3,2,1,0:T(8,128)(2,1)S(1)}, u32[]{:S(2)}, u32[]{:S(2)}) %all-to-all-start.3) | async-done | bytes 917536 | tf_op jit(solution)/shard_map/all_to_all | solution.py:311
  130.4 7.6 %all-to-all-start.1 = ((bf16[64,7,8,128]{3,2,1,0:T(8,128)(2,1)}), bf16[64,7,8,128]{3,2,1,0:T(8,128)(2,1)S(1)}, u32[]{:S(2)}, u32[]{:S(2)}) async-start(bf16[64,7,8,128]{3,2,1,0:T(8,128)(2,1)} %get-tuple-element.10), calls=%async_computation.1 | async-start | bytes 1835008 | tf_op jit(solution)/shard_map/all_to_all | solution.py:311
  143.9 16.7 %collective-permute-done.6 = f32[64,64]{1,0:T(8,128)S(1)} collective-permute-done((f32[64,64]{1,0:T(8,128)S(1)}, f32[64,64]{1,0:T(8,128)S(1)}, u32[]{:S(2)}, u32[]{:S(2)}) %collective-permute-start.6) | collective-permute-done | bytes 16416 | tf_op jit(solution)/shard_map/ppermute | solution.py:287
  161.5 3.9 %collective-permute-done.7 = f32[64,64]{1,0:T(8,128)S(1)} collective-permute-done((f32[64,64]{1,0:T(8,128)S(1)}, f32[64,64]{1,0:T(8,128)S(1)}, u32[]{:S(2)}, u32[]{:S(2)}) %collective-permute-start.7) | collective-permute-done | bytes 16416 | tf_op jit(solution)/shard_map/ppermute | solution.py:287
  165.4 4.7 %collective-permute-start.8 = (f32[64,64]{1,0:T(8,128)S(1)}, f32[64,64]{1,0:T(8,128)S(1)}, u32[]{:S(2)}, u32[]{:S(2)}) collective-permute-start(f32[64,64]{1,0:T(8,128)S(1)} %add.106), channel_id=1, source_target_pairs={{0,8},{1,9},{2,10},{3,11},{4,12},{5,13},{6,14},{7,15},{8,0},{9,1},... | collective-permute-start | bytes 49160 | tf_op jit(solution)/shard_map/ppermute | solution.py:287
  170.1 3.4 %collective-permute-done.8 = f32[64,64]{1,0:T(8,128)S(1)} collective-permute-done((f32[64,64]{1,0:T(8,128)S(1)}, f32[64,64]{1,0:T(8,128)S(1)}, u32[]{:S(2)}, u32[]{:S(2)}) %collective-permute-start.8) | collective-permute-done | bytes 16416 | tf_op jit(solution)/shard_map/ppermute | solution.py:287
  174.0 3.4 %collective-permute-done.9 = f32[64,64]{1,0:T(8,128)S(1)} collective-permute-done((f32[64,64]{1,0:T(8,128)S(1)}, f32[64,64]{1,0:T(8,128)S(1)}, u32[]{:S(2)}, u32[]{:S(2)}) %collective-permute-start.9) | collective-permute-done | bytes 16416 | tf_op jit(solution)/shard_map/ppermute | solution.py:287
  179.8 3.1 %collective-permute-done.10 = f32[64,64]{1,0:T(8,128)S(1)} collective-permute-done((f32[64,64]{1,0:T(8,128)S(1)}, f32[64,64]{1,0:T(8,128)S(1)}, u32[]{:S(2)}, u32[]{:S(2)}) %collective-permute-start.10) | collective-permute-done | bytes 16416 | tf_op jit(solution)/shard_map/ppermute | solution.py:287
  182.9 2.7 %collective-permute-start.11 = (f32[64,64]{1,0:T(8,128)S(1)}, f32[64,64]{1,0:T(8,128)S(1)}, u32[]{:S(2)}, u32[]{:S(2)}) collective-permute-start(f32[64,64]{1,0:T(8,128)S(1)} %add.109), channel_id=1, source_target_pairs={{0,64},{64,0},{128,192},{192,128},{1,65},{65,1},{129,193},{193,129... | collective-permute-start | bytes 49160 | tf_op jit(solution)/shard_map/ppermute | solution.py:287
  188.2 4.6 %collective-permute-done.12 = f32[64,64]{1,0:T(8,128)S(1)} collective-permute-done((f32[64,64]{1,0:T(8,128)S(1)}, f32[64,64]{1,0:T(8,128)S(1)}, u32[]{:S(2)}, u32[]{:S(2)}) %collective-permute-start.12) | collective-permute-done | bytes 16416 | tf_op jit(solution)/shard_map/ppermute | solution.py:287
  193.5 3.2 %unpack_add.3 = f32[12,24,1536]{2,1,0:T(8,128)} custom-call(f32[12,24,1536]{2,1,0:T(8,128)} %get-tuple-element.11.part_ref, bf16[64,7,8,128]{3,2,1,0:T(8,128)(2,1)} %copy-done.4), custom_call_target="tpu_custom_call" | custom-call | flops 884736 | bytes 4423680 | tf_op jit(solution)/shard_map/unpack_add/pallas_call | solution.py:88
  197.6 3.2 %unpack_add.2 = f32[12,24,1536]{2,1,0:T(8,128)} custom-call(f32[12,24,1536]{2,1,0:T(8,128)} %get-tuple-element.9.part_ref, bf16[64,7,8,128]{3,2,1,0:T(8,128)(2,1)} %copy-done.5), custom_call_target="tpu_custom_call" | custom-call | flops 884736 | bytes 4423680 | tf_op jit(solution)/shard_map/unpack_add/pallas_call | solution.py:88
  (104 shorter events, 41.2 us)
Async XLA Ops:
  2.6 105.9 %collective-permute-start = (bf16[2,24,1536]{2,1,0:T(8,128)(2,1)}, bf16[2,24,1536]{2,1,0:T(8,128)(2,1)}, u32[]{:S(2)}, u32[]{:S(2)}) collective-permute-start(bf16[2,24,1536]{2,1,0:T(8,128)(2,1)} %bitcast.70), channel_id=1, source_target_pairs={{0,192},{64,0},{128,64},{192,128},{1,193},{65,1},{129,65},{193,129... | collective-permute-start | bytes 442376 | tf_op jit(solution)/shard_map/ppermute | solution.py:330
  3.1 105.4 %collective-permute-start.1 = (bf16[2,24,1536]{2,1,0:T(8,128)(2,1)}, bf16[2,24,1536]{2,1,0:T(8,128)(2,1)}, u32[]{:S(2)}, u32[]{:S(2)}) collective-permute-start(bf16[2,24,1536]{2,1,0:T(8,128)(2,1)} %bitcast.70), channel_id=1, source_target_pairs={{0,128},{64,192},{128,0},{192,64},{1,129},{65,193},{129,1},{193,65... | collective-permute-start | bytes 442376 | tf_op jit(solution)/shard_map/ppermute | solution.py:330
  5.6 103.0 %collective-permute-start.2 = (bf16[2,24,1536]{2,1,0:T(8,128)(2,1)}, bf16[2,24,1536]{2,1,0:T(8,128)(2,1)}, u32[]{:S(2)}, u32[]{:S(2)}) collective-permute-start(bf16[2,24,1536]{2,1,0:T(8,128)(2,1)} %bitcast.70), channel_id=1, source_target_pairs={{0,64},{64,128},{128,192},{192,0},{1,65},{65,129},{129,193},{193,1... | collective-permute-start | bytes 442376 | tf_op jit(solution)/shard_map/ppermute | solution.py:330
  9.9 98.6 %collective-permute-start.3 = (bf16[2,24,1536]{2,1,0:T(8,128)(2,1)}, bf16[2,24,1536]{2,1,0:T(8,128)(2,1)}, u32[]{:S(2)}, u32[]{:S(2)}) collective-permute-start(bf16[2,24,1536]{2,1,0:T(8,128)(2,1)} %fusion.33), channel_id=1, source_target_pairs={{0,64},{64,128},{128,192},{1,65},{65,129},{129,193},{2,66},{66,130... | collective-permute-start | bytes 442376 | tf_op jit(solution)/shard_map/ppermute | solution.py:336
  14.4 14.9 %copy-start.1 = (f32[24,12,1536]{2,0,1:T(8,128)S(1)}, f32[24,12,1536]{2,0,1:T(8,128)}, u32[]{:S(2)}) copy-start(f32[24,12,1536]{2,0,1:T(8,128)} %param.10) | copy-start | bytes 5308420
  14.4 36.7 %all-to-all-start = ((bf16[64,7,8,128]{3,2,1,0:T(8,128)(2,1)}), bf16[64,7,8,128]{3,2,1,0:T(8,128)(2,1)}, u32[]{:S(2)}, u32[]{:S(2)}) async-start(bf16[64,7,8,128]{3,2,1,0:T(8,128)(2,1)} %pack.2), calls=%async_computation | async-start | bytes 1835008 | tf_op jit(solution)/shard_map/all_to_all | solution.py:311
  32.0 9.0 %copy-start.3 = (f32[24,12,1536]{2,0,1:T(8,128)S(1)}, f32[24,12,1536]{2,0,1:T(8,128)}, u32[]{:S(2)}) copy-start(f32[24,12,1536]{2,0,1:T(8,128)} %param.9) | copy-start | bytes 5308420
  33.7 7.4 %copy-start.2 = (f32[24,12,1536]{2,0,1:T(8,128)S(1)}, f32[24,12,1536]{2,0,1:T(8,128)}, u32[]{:S(2)}) copy-start(f32[24,12,1536]{2,0,1:T(8,128)} %param.10) | copy-start | bytes 5308420
  33.7 73.1 %collective-permute-start.4 = (bf16[2,24,1536]{2,1,0:T(8,128)(2,1)}, bf16[2,24,1536]{2,1,0:T(8,128)(2,1)}, u32[]{:S(2)}, u32[]{:S(2)}) collective-permute-start(bf16[2,24,1536]{2,1,0:T(8,128)(2,1)} %pad_maximum_fusion.1), channel_id=1, source_target_pairs={{64,0},{128,64},{192,128},{65,1},{129,65},{193,129},{66,2},{130,66... | collective-permute-start | bytes 442376 | tf_op jit(solution)/shard_map/ppermute | solution.py:337
  51.1 32.5 %all-to-all-start.2 = ((bf16[64,7,8,128]{3,2,1,0:T(8,128)(2,1)}), bf16[64,7,8,128]{3,2,1,0:T(8,128)(2,1)S(1)}, u32[]{:S(2)}, u32[]{:S(2)}) async-start(bf16[64,7,8,128]{3,2,1,0:T(8,128)(2,1)} %pack.3), calls=%async_computation.2 | async-start | bytes 1835008 | tf_op jit(solution)/shard_map/all_to_all | solution.py:311
  84.6 21.4 %copy-start.10 = (s32[24,1536]{1,0:T(8,128)S(1)}, s32[24,1536]{1,0:T(8,128)}, u32[]{:S(2)}) copy-start(s32[24,1536]{1,0:T(8,128)} %param.14) | copy-start | bytes 442372
  95.5 11.0 %copy-start.9 = (s32[24,12,12]{0,2,1:T(8,128)S(1)}, s32[24,12,12]{0,2,1:T(8,128)}, u32[]{:S(2)}) copy-start(s32[24,12,12]{0,2,1:T(8,128)} %param.16) | copy-start | bytes 41476
  95.5 34.8 %all-to-all-start.3 = ((bf16[64,7,8,128]{3,2,1,0:T(8,128)(2,1)}), bf16[64,7,8,128]{3,2,1,0:T(8,128)(2,1)S(1)}, u32[]{:S(2)}, u32[]{:S(2)}) async-start(bf16[64,7,8,128]{3,2,1,0:T(8,128)(2,1)} %heat_lines.1), calls=%async_computation.3 | async-start | bytes 1835008 | tf_op jit(solution)/shard_map/all_to_all | solution.py:311
  110.5 14.0 %copy-start.8 = (f32[1536,128]{1,0:T(8,128)S(1)}, f32[1536,128]{1,0:T(8,128)}, u32[]{:S(2)}) copy-start(f32[1536,128]{1,0:T(8,128)} %get-tuple-element.14) | copy-start | bytes 2359300
  130.4 8.9 %copy-start.4 = (bf16[64,7,8,128]{3,2,1,0:T(8,128)(2,1)}, bf16[64,7,8,128]{3,2,1,0:T(8,128)(2,1)S(1)}, u32[]{:S(2)}) copy-start(bf16[64,7,8,128]{3,2,1,0:T(8,128)(2,1)S(1)} %all-to-all-done.3.ret_ref) | copy-start | bytes 2752516
  130.4 66.3 %all-to-all-start.1 = ((bf16[64,7,8,128]{3,2,1,0:T(8,128)(2,1)}), bf16[64,7,8,128]{3,2,1,0:T(8,128)(2,1)S(1)}, u32[]{:S(2)}, u32[]{:S(2)}) async-start(bf16[64,7,8,128]{3,2,1,0:T(8,128)(2,1)} %get-tuple-element.10), calls=%async_computation.1 | async-start | bytes 1835008 | tf_op jit(solution)/shard_map/all_to_all | solution.py:311
  141.2 1.3 collective-permute-start.5
  142.5 18.1 %collective-permute-start.6 = (f32[64,64]{1,0:T(8,128)S(1)}, f32[64,64]{1,0:T(8,128)S(1)}, u32[]{:S(2)}, u32[]{:S(2)}) collective-permute-start(f32[64,64]{1,0:T(8,128)S(1)} %add.104), channel_id=1, source_target_pairs={{0,2},{1,3},{2,0},{3,1},{4,6},{5,7},{6,4},{7,5},{8,10},{9,11},{10,... | collective-permute-start | bytes 49160 | tf_op jit(solution)/shard_map/ppermute | solution.py:287
  160.6 4.8 %collective-permute-start.7 = (f32[64,64]{1,0:T(8,128)S(1)}, f32[64,64]{1,0:T(8,128)S(1)}, u32[]{:S(2)}, u32[]{:S(2)}) collective-permute-start(f32[64,64]{1,0:T(8,128)S(1)} %add.105), channel_id=1, source_target_pairs={{0,4},{1,5},{2,6},{3,7},{4,0},{5,1},{6,2},{7,3},{8,12},{9,13},{10,... | collective-permute-start | bytes 49160 | tf_op jit(solution)/shard_map/ppermute | solution.py:287
  165.4 8.1 %collective-permute-start.8 = (f32[64,64]{1,0:T(8,128)S(1)}, f32[64,64]{1,0:T(8,128)S(1)}, u32[]{:S(2)}, u32[]{:S(2)}) collective-permute-start(f32[64,64]{1,0:T(8,128)S(1)} %add.106), channel_id=1, source_target_pairs={{0,8},{1,9},{2,10},{3,11},{4,12},{5,13},{6,14},{7,15},{8,0},{9,1},... | collective-permute-start | bytes 49160 | tf_op jit(solution)/shard_map/ppermute | solution.py:287
  173.5 3.9 %collective-permute-start.9 = (f32[64,64]{1,0:T(8,128)S(1)}, f32[64,64]{1,0:T(8,128)S(1)}, u32[]{:S(2)}, u32[]{:S(2)}) collective-permute-start(f32[64,64]{1,0:T(8,128)S(1)} %add.107), channel_id=1, source_target_pairs={{0,16},{1,17},{2,18},{3,19},{4,20},{5,21},{6,22},{7,23},{8,24},{9,... | collective-permute-start | bytes 49160 | tf_op jit(solution)/shard_map/ppermute | solution.py:287
  177.4 5.4 %collective-permute-start.10 = (f32[64,64]{1,0:T(8,128)S(1)}, f32[64,64]{1,0:T(8,128)S(1)}, u32[]{:S(2)}, u32[]{:S(2)}) collective-permute-start(f32[64,64]{1,0:T(8,128)S(1)} %add.108), channel_id=1, source_target_pairs={{0,32},{1,33},{2,34},{3,35},{4,36},{5,37},{6,38},{7,39},{8,40},{9,... | collective-permute-start | bytes 49160 | tf_op jit(solution)/shard_map/ppermute | solution.py:287
  182.9 4.6 %collective-permute-start.11 = (f32[64,64]{1,0:T(8,128)S(1)}, f32[64,64]{1,0:T(8,128)S(1)}, u32[]{:S(2)}, u32[]{:S(2)}) collective-permute-start(f32[64,64]{1,0:T(8,128)S(1)} %add.109), channel_id=1, source_target_pairs={{0,64},{64,0},{128,192},{192,128},{1,65},{65,1},{129,193},{193,129... | collective-permute-start | bytes 49160 | tf_op jit(solution)/shard_map/ppermute | solution.py:287
  187.4 5.4 %collective-permute-start.12 = (f32[64,64]{1,0:T(8,128)S(1)}, f32[64,64]{1,0:T(8,128)S(1)}, u32[]{:S(2)}, u32[]{:S(2)}) collective-permute-start(f32[64,64]{1,0:T(8,128)S(1)} %add.110), channel_id=1, source_target_pairs={{0,128},{64,192},{128,0},{192,64},{1,129},{65,193},{129,1},{193,65... | collective-permute-start | bytes 49160 | tf_op jit(solution)/shard_map/ppermute | solution.py:287
  (6 other events, 12.5 us)

commit v2 on v1

v2 whole, which is shorter than its diff:
```python
import functools

import jax
import jax.numpy as jnp
from jax import lax
from jax.experimental import pallas as pl
from jax.experimental.pallas import tpu as pltpu
from jax.sharding import PartitionSpec as P

HB = 64
ZBLK = 128
LANES = 128
ROWS = 8

mixing_diffusivity = 0.3
heat_diffusivity = 0.4
release_rate = 0.5
phase_step = 0.2

VMEM_LIMIT = 56 * 1024 * 1024
LOCAL_VMEM_LIMIT = 16 * 1024 * 1024
LINE_VMEM_LIMIT = 40 * 1024 * 1024


PACK_PLANES = 2


def lane_group(shape):
    return lax.broadcasted_iota(jnp.int32, shape, len(shape) - 1) // 32


def rolled(tile, shift):
    shift = shift % LANES
    return pltpu.roll(tile, shift, 1) if shift else tile


def pack_kernel(x0_ref, x1_ref, class_ref, out_ref, wide_ref, high_ref, low_ref):
    step = pl.program_id(0)
    steps = pl.num_programs(0)
    lines = out_ref.shape[0]
    per_plane = x0_ref.shape[2] // ZBLK
    pairs = per_plane // 2
    left = per_plane * PACK_PLANES - (2 * lines - per_plane * PACK_PLANES * (steps - 1))
    first_left = per_plane * PACK_PLANES - left
    group = lane_group((ROWS, LANES))
    sublane = lax.broadcasted_iota(jnp.int32, (ROWS, LANES), 0)
    spare = (lax.broadcasted_iota(jnp.int32, (ROWS, LANES), 1) < 120) & (group == 3)

    def copy_pairs(count):
        for pair in range(count):
            p, k = pair // pairs, (pair % pairs) * 2 * ZBLK
            line = step * (PACK_PLANES * pairs) + pair
            for f, x_ref in enumerate((x0_ref, x1_ref)):
                for b in range(2):
                    for t in range(3):
                        tile = x_ref[p, ROWS * t : ROWS * t + ROWS, k + b * ZBLK : k + (b + 1) * ZBLK]
                        out_ref[line, 7 * f + 3 * b + t] = tile.astype(jnp.bfloat16)

    @pl.when(step == 0)
    def _():
        wide_ref[...] = jnp.zeros_like(wide_ref)
        for p in range(class_ref.shape[0]):
            wide_ref[p, :per_plane, : class_ref.shape[2]] = class_ref[p]
        for p in range(class_ref.shape[0]):
            codes = pltpu.roll(wide_ref[p], 96, 1)
            high = codes // HB
            high_ref[p] = high.astype(jnp.float32)
            low_ref[p] = (codes - HB * high).astype(jnp.float32)

    @pl.when(step < steps - 1)
    def _():
        copy_pairs(PACK_PLANES * pairs)

    @pl.when(step == steps - 1)
    def _():
        copy_pairs(first_left // 2)
        for m in range(left):
            block = first_left + m
            p, k = block // per_plane, (block % per_plane) * ZBLK
            plane, row = class_ref.shape[0] - PACK_PLANES + p, block % per_plane
            for q in range(4):
                line = 4 * m + q
                places = [(2 * line // per_plane, 2 * line % per_plane), (2 * line // per_plane, 2 * line % per_plane + 1)]
                places.append((plane, row))
                classes = jnp.zeros((ROWS, LANES), jnp.float32)
                for at, ref in ((0, high_ref), (3, low_ref)):
                    for b, (cp, cr) in enumerate(places):
                        classes = jnp.where(sublane == at + b, ref[cp, cr : cr + 1, :], classes)
                classes = jnp.where(spare, classes, 0.0)
                for f, x_ref in enumerate((x0_ref, x1_ref)):
                    packed = classes if f == 0 else jnp.zeros_like(classes)
                    for g in range(3):
                        tile = x_ref[p, ROWS * g : ROWS * g + ROWS, k : k + ZBLK]
                        packed = jnp.where(group == g, rolled(tile, 32 * (g - q)), packed)
                    out_ref[line, 7 * f + 6] = packed.astype(jnp.bfloat16)


def pack(x0, x1, classes, lines):
    planes, rows, depth = x0.shape
    part = pl.BlockSpec((PACK_PLANES, rows, depth), lambda i: (i, 0, 0))
    packets = (lines, 14, ROWS, LANES)
    wide = (planes, 2 * ROWS, LANES)
    return pl.pallas_call(
        pack_kernel,
        grid=(planes // PACK_PLANES,),
        in_specs=[part, part, pl.BlockSpec(classes.shape, lambda i: (0, 0, 0))],
        out_specs=pl.BlockSpec(packets, lambda i: (0, 0, 0, 0)),
        out_shape=jax.ShapeDtypeStruct(packets, jnp.bfloat16),
        scratch_shapes=[
            pltpu.VMEM(wide, jnp.int32),
            pltpu.VMEM(wide, jnp.float32),
            pltpu.VMEM(wide, jnp.float32),
        ],
        compiler_params=pltpu.CompilerParams(vmem_limit_bytes=VMEM_LIMIT),
        cost_estimate=pl.CostEstimate(flops=2 * x0.size, bytes_accessed=12 * x0.size, transcendentals=0),
        name="pack",
    )(x0, x1, classes)


def unpack_add_kernel(part0_ref, part1_ref, ret_ref, out0_ref, out1_ref):
    step = pl.program_id(0)
    steps = pl.num_programs(0)
    lines = ret_ref.shape[0]
    per_plane = part0_ref.shape[2] // ZBLK
    pairs = per_plane // 2
    left = per_plane * PACK_PLANES - (2 * lines - per_plane * PACK_PLANES * (steps - 1))
    first_left = per_plane * PACK_PLANES - left
    group = lane_group((ROWS, LANES))
    fields = (
        (part0_ref, out0_ref, phase_step * mixing_diffusivity),
        (part1_ref, out1_ref, phase_step),
    )

    def add_pairs(count):
        for pair in range(count):
            p, k = pair // pairs, (pair % pairs) * 2 * ZBLK
            line = step * (PACK_PLANES * pairs) + pair
            for f, (part_ref, out_ref, scale) in enumerate(fields):
                for b in range(2):
                    for t in range(3):
                        at = (p, slice(ROWS * t, ROWS * t + ROWS), slice(k + b * ZBLK, k + (b + 1) * ZBLK))
                        tile = ret_ref[line, 7 * f + 3 * b + t].astype(jnp.float32)
                        out_ref[at] = part_ref[at] + scale * tile

    @pl.when(step < steps - 1)
    def _():
        add_pairs(PACK_PLANES * pairs)

    @pl.when(step == steps - 1)
    def _():
        add_pairs(first_left // 2)
        for m in range(left):
            block = first_left + m
            p, k = block // per_plane, (block % per_plane) * ZBLK
            for f, (part_ref, out_ref, scale) in enumerate(fields):
                quarters = [ret_ref[4 * m + q, 7 * f + 6].astype(jnp.float32) for q in range(4)]
                for g in range(3):
                    tile = rolled(quarters[0], -32 * g)
                    for q in range(1, 4):
                        tile = jnp.where(group == q, rolled(quarters[q], 32 * (q - g)), tile)
                    at = (p, slice(ROWS * g, ROWS * g + ROWS), slice(k, k + ZBLK))
                    out_ref[at] = part_ref[at] + scale * tile


def unpack_add(part0, part1, returned):
    planes, rows, depth = part0.shape
    part = pl.BlockSpec((PACK_PLANES, rows, depth), lambda i: (i, 0, 0))
    return pl.pallas_call(
        unpack_add_kernel,
        grid=(planes // PACK_PLANES,),
        in_specs=[part, part, pl.BlockSpec(returned.shape, lambda i: (0, 0, 0, 0))],
        out_specs=[part, part],
        out_shape=[jax.ShapeDtypeStruct(part0.shape, jnp.float32)] * 2,
        compiler_params=pltpu.CompilerParams(vmem_limit_bytes=VMEM_LIMIT),
        cost_estimate=pl.CostEstimate(flops=4 * part0.size, bytes_accessed=20 * part0.size, transcendentals=0),
        name="unpack_add",
    )(part0, part1, returned)


SOURCES = 16
WIDE = 2 * LANES
MATMUL_ROWS = 768


def unpack_lines(r_ref, x_ref):
    def step(i, carry):
        src = pl.ds(i * SOURCES, SOURCES)
        rows = pl.ds(pl.multiple_of(i * (24 * SOURCES), 24 * SOURCES), 24 * SOURCES)
        for f in range(2):
            for b in range(2):
                tiles = r_ref[src, 7 * f + 3 * b : 7 * f + 3 * b + 3].astype(jnp.float32)
                x_ref[f, rows, b * LANES : (b + 1) * LANES] = tiles.reshape(24 * SOURCES, LANES).astype(jnp.bfloat16)
            last = r_ref[src, 7 * f + 6].astype(jnp.float32).reshape(ROWS * SOURCES, LANES)
            parts = [rolled(last, -32 * g).reshape(SOURCES, ROWS, LANES) for g in range(3)]
            tiles = jnp.stack(parts, axis=1)
            x_ref[2, rows, f * LANES : (f + 1) * LANES] = tiles.reshape(24 * SOURCES, LANES).astype(jnp.bfloat16)
        return carry

    lax.fori_loop(0, r_ref.shape[0] // SOURCES, step, 0)


def pack_whole(values, out_ref, src, f):
    for b in range(2):
        tiles = values[:, b * LANES : (b + 1) * LANES].reshape(-1, 3, ROWS, LANES)
        out_ref[src, 7 * f + 3 * b : 7 * f + 3 * b + 3] = tiles.astype(jnp.bfloat16)


def pack_quarter(values, out_ref, src, f):
    tiles = values.reshape(-1, 3, ROWS, LANES)
    group = lane_group((tiles.shape[0] * ROWS, LANES))
    packed = jnp.zeros(group.shape, jnp.float32)
    for g in range(3):
        packed = jnp.where(group == g, rolled(tiles[:, g].reshape(group.shape), 32 * g), packed)
    out_ref[src, 7 * f + 6] = packed.reshape(-1, ROWS, LANES).astype(jnp.bfloat16)


def line_kernel(r_ref, d_ref, out_ref, sums_ref, x_ref, slope_ref):
    unpack_lines(r_ref, x_ref)
    tile = MATMUL_ROWS
    count = d_ref.shape[0] // tile

    def slope_step(i, carry):
        rows = pl.ds(pl.multiple_of(i * tile, tile), tile)
        lane = lax.broadcasted_iota(jnp.int32, (tile, LANES), 1)
        sums = jnp.zeros((tile, LANES), jnp.float32)
        for n in range(3):
            slope = jnp.dot(d_ref[rows, :], x_ref[n], preferred_element_type=jnp.float32).astype(jnp.bfloat16)
            slope_ref[n, rows, :] = slope
            if n == 1:
                continue
            for b in range(2) if n == 0 else range(1):
                part = slope[:, b * LANES : (b + 1) * LANES].astype(jnp.float32) ** 2
                if n == 2:
                    part = jnp.where(lane < 32, part, 0.0)
                sums = jnp.where(lane == n + b, jnp.sum(part, axis=1, keepdims=True), sums)
        sums_ref[rows, :] = sums
        return carry

    lax.fori_loop(0, count, slope_step, 0)

    def curve_step(i, carry):
        rows = pl.ds(pl.multiple_of(i * tile, tile), tile)
        src = pl.ds(i * (tile // 24), tile // 24)
        matrix = d_ref[rows, :]

        def heat(curve, slope):
            slope = slope.astype(jnp.float32)
            return heat_diffusivity * curve + (release_rate * 2.0 * mixing_diffusivity) * slope**2

        pack_whole(jnp.dot(matrix, slope_ref[0], preferred_element_type=jnp.float32), out_ref, src, 0)
        curve = jnp.dot(matrix, slope_ref[1], preferred_element_type=jnp.float32)
        pack_whole(heat(curve, slope_ref[0, rows, :]), out_ref, src, 1)
        curve = jnp.dot(matrix, slope_ref[2], preferred_element_type=jnp.float32)
        pack_quarter(curve[:, :LANES], out_ref, src, 0)
        pack_quarter(heat(curve[:, LANES:], slope_ref[2, rows, :LANES]), out_ref, src, 1)
        return carry

    lax.fori_loop(0, count, curve_step, 0)


def line_terms(received, matrix):
    rows = matrix.shape[0]
    wide = (3, rows, WIDE)
    return pl.pallas_call(
        line_kernel,
        out_shape=(
            jax.ShapeDtypeStruct(received.shape, jnp.bfloat16),
            jax.ShapeDtypeStruct((rows, LANES), jnp.float32),
        ),
        scratch_shapes=[pltpu.VMEM(wide, jnp.bfloat16), pltpu.VMEM(wide, jnp.bfloat16)],
        compiler_params=pltpu.CompilerParams(vmem_limit_bytes=LINE_VMEM_LIMIT),
        cost_estimate=pl.CostEstimate(
            flops=12 * rows * rows * WIDE, bytes_accessed=2 * rows * rows + 4 * received.size, transcendentals=0
        ),
        name="line_terms",
    )(received, matrix)


def local_kernel(
    fringe_ref, lo_ref, hi_ref, *refs
):
    fields = (refs[0:3], refs[3:6])
    slope_ref, curve_ref, speed_ref, inflow_ref, mix_ref, heat_ref, sums_ref = refs[6:]
    p = pl.program_id(0)
    last = pl.num_programs(0) - 1
    fringe = fringe_ref[p]
    speed = speed_ref[...]
    dissipation = None
    for f, (before, here, after) in enumerate(fields):
        x = here[0]
        upstream = jnp.where(p == 0, lo_ref[f], before[0])
        downstream = jnp.where(p == last, hi_ref[f], after[0])
        axial_slope = (downstream - upstream) * 0.5
        axial_curve = downstream - 2.0 * x + upstream
        diffusivity = (mixing_diffusivity, heat_diffusivity)[f]
        rhs = -speed * axial_slope + diffusivity * (axial_curve + curve_ref[f, 0]) + fringe * (inflow_ref[f] - x)
        if f == 0:
            depth = slope_ref[0, 0].astype(jnp.float32)
            dissipation = (2.0 * mixing_diffusivity) * (axial_slope**2 + depth**2)
            mix_ref[0] = x + phase_step * rhs
        else:
            heat_ref[0] = x + phase_step * (rhs + release_rate * dissipation)
    lane = lax.broadcasted_iota(jnp.int32, sums_ref.shape[1:], 1)
    sums = jnp.zeros(sums_ref.shape[1:], jnp.float32)
    for k in range(dissipation.shape[1] // ZBLK):
        part = jnp.sum(dissipation[:, k * ZBLK : (k + 1) * ZBLK], axis=1, keepdims=True)
        sums = jnp.where(lane == k, part, sums)
    sums_ref[0] = sums


def local_terms(x0, x1, lo, hi, slope, curve, speed, inflow, fringe):
    planes, rows, depth = x0.shape
    plane = lambda move: pl.BlockSpec((1, rows, depth), lambda p: (jnp.clip(p + move, 0, planes - 1), 0, 0))
    fixed = lambda shape: pl.BlockSpec(shape, lambda p: (0,) * len(shape))
    return pl.pallas_call(
        local_kernel,
        grid=(planes,),
        in_specs=[
            pl.BlockSpec(memory_space=pltpu.SMEM),
            fixed((2, rows, depth)),
            fixed((2, rows, depth)),
            plane(-1),
            plane(0),
            plane(1),
            plane(-1),
            plane(0),
            plane(1),
            pl.BlockSpec((1, 1, rows, depth), lambda p: (0, p, 0, 0)),
            pl.BlockSpec((2, 1, rows, depth), lambda p: (0, p, 0, 0)),
            fixed((rows, depth)),
            fixed((2, rows, depth)),
        ],
        out_specs=[
            pl.BlockSpec((1, rows, depth), lambda p: (p, 0, 0)),
            pl.BlockSpec((1, rows, depth), lambda p: (p, 0, 0)),
            pl.BlockSpec((1, rows, LANES), lambda p: (p, 0, 0)),
        ],
        out_shape=[
            jax.ShapeDtypeStruct((planes, rows, depth), jnp.float32),
            jax.ShapeDtypeStruct((planes, rows, depth), jnp.float32),
            jax.ShapeDtypeStruct((planes, rows, LANES), jnp.float32),
        ],
        compiler_params=pltpu.CompilerParams(vmem_limit_bytes=LOCAL_VMEM_LIMIT),
        cost_estimate=pl.CostEstimate(flops=60 * x0.size, bytes_accessed=34 * x0.size, transcendentals=0),
        name="local_terms",
    )(fringe, lo, hi, x0, x0, x0, x1, x1, x1, slope, curve, speed, inflow)


def bin_sums(values, classes):
    row = classes // HB
    column = classes % HB
    bins = jnp.arange(HB, dtype=jnp.int32)[:, None]
    columns = (bins == column[None]).astype(jnp.bfloat16)
    total = 0.0
    for _ in range(3):
        term = values.astype(jnp.bfloat16)
        values = values - term.astype(jnp.float32)
        rows = jnp.where(bins == row[None], term[None], jnp.zeros((), jnp.bfloat16))
        total = total + jnp.einsum("rn,cn->rc", rows, columns, preferred_element_type=jnp.float32)
    return total


def all_sum(block):
    for axis, bits in (("gx", (1, 2)), ("wa", (1,)), ("wa", (16, 32)), ("wa", (2, 4)), ("wa", (8,))):
        count = lax.axis_size(axis)
        moves = bits if len(bits) == 1 else (bits[0], bits[1], bits[0] + bits[1])
        arrived = [lax.ppermute(block, axis, [(i, i ^ move) for i in range(count)]) for move in moves]
        block = block + arrived[0]
        if len(arrived) == 3:
            block = block + (arrived[1] + arrived[2])
    return block


def body(
    mixing_ratio,
    thermal_state,
    streamwise_speed,
    implicit_derivative_matrix,
    stored_entry_slices,
    orifice_region_flag,
    arriving_slice_number,
    joint_frequency_class,
):
    matrix = implicit_derivative_matrix
    row_count, plane_count, depth_count = mixing_ratio.shape
    lines = lax.axis_size("wa")
    slab_index = lax.axis_index("gx")
    slab_count = lax.axis_size("gx")
    x0 = jnp.transpose(mixing_ratio, (1, 0, 2))
    x1 = jnp.transpose(thermal_state, (1, 0, 2))

    def exchange(packets):
        return lax.all_to_all(packets, "wa", split_axis=0, concat_axis=0, tiled=True)

    classes = jnp.transpose(joint_frequency_class, (1, 2, 0))
    packets = pack(x0, x1, classes, lines)
    packets, x0, x1 = lax.optimization_barrier((packets, x0, x1))
    received = exchange(packets)

    rounded = jnp.stack([x0, x1]).astype(jnp.bfloat16)
    depth_slope = jnp.einsum(
        "fxyj,kj->fxyk", rounded, matrix, preferred_element_type=jnp.float32
    ).astype(jnp.bfloat16)
    depth_slope, stored_entry_slices, x0, x1 = lax.optimization_barrier((depth_slope, stored_entry_slices, x0, x1))

    held_count = stored_entry_slices.shape[2]
    plane_index = arriving_slice_number[0]
    owner = plane_index // held_count
    held_plane = lax.dynamic_index_in_dim(stored_entry_slices, plane_index % held_count, 2, keepdims=False)
    database_plane = held_plane
    for move in range(1, slab_count):
        table = [(i, (i + move) % slab_count) for i in range(slab_count)]
        arrived = lax.ppermute(held_plane, "gx", table)
        database_plane = jnp.where((slab_index - move) % slab_count == owner, arrived, database_plane)
    forward = [(i, i + 1) for i in range(slab_count - 1)]
    backward = [(target, source) for source, target in forward]
    first = jnp.stack([x0[0], x1[0]])
    final = jnp.stack([x0[-1], x1[-1]])
    before = lax.ppermute(final.astype(jnp.bfloat16), "gx", forward).astype(jnp.float32)
    after = lax.ppermute(first.astype(jnp.bfloat16), "gx", backward).astype(jnp.float32)
    coflow = jnp.array([0.0, 1.0], jnp.float32)[:, None, None]
    inflow_cells = jnp.where(orifice_region_flag[None] == 1, database_plane.astype(jnp.float32), coflow)
    lo = jnp.where(slab_index == 0, inflow_cells, before)
    hi = jnp.where(slab_index == slab_count - 1, final, after)

    depth_curve = jnp.einsum("fxyj,kj->fxyk", depth_slope, matrix, preferred_element_type=jnp.float32)
    plane_numbers = (slab_index * plane_count + jnp.arange(plane_count, dtype=jnp.int32)).astype(jnp.float32)
    fringe = 1.0 / (1.0 + plane_numbers / plane_count)
    part0, part1, local_sums = local_terms(
        x0, x1, lo, hi, depth_slope, depth_curve, streamwise_speed, inflow_cells, fringe
    )

    received, part0, part1, local_sums = lax.optimization_barrier((received, part0, part1, local_sums))
    returned, line_sums = line_terms(received, matrix)
    back = exchange(returned)

    per_plane = depth_count // ZBLK
    own_values = local_sums[:, :, :per_plane].transpose(0, 2, 1).reshape(-1)
    own_classes = classes.reshape(-1)
    line_values = (2.0 * mixing_diffusivity) * line_sums.reshape(lines, row_count, LANES)[..., :3]
    line_values = line_values.transpose(0, 2, 1).reshape(-1)
    codes = received[:, 6, :6, 96:120].astype(jnp.int32).reshape(lines, 2, 3, row_count)
    line_classes = (codes[:, 0] * HB + codes[:, 1]).reshape(-1)
    bins = bin_sums(
        jnp.concatenate([own_values, line_values]), jnp.concatenate([own_classes, line_classes])
    )
    summed = all_sum(bins)
    per_bin = row_count * lines * plane_count * slab_count * depth_count // (HB * HB)
    histogram = summed / per_bin

    mixture_next, temperature_next = unpack_add(part0, part1, back)
    return (jnp.transpose(mixture_next, (1, 0, 2)), jnp.transpose(temperature_next, (1, 0, 2)), histogram)


def solution(mesh):
    in_specs = (
        P("wa", "gx", None),
        P("wa", "gx", None),
        P("wa", None),
        P(),
        P(None, "wa", "gx", None),
        P("wa", None),
        P(),
        P("wa", "gx", None),
    )
    out_specs = (P("wa", "gx", None), P("wa", "gx", None), P())
    return jax.shard_map(body, mesh=mesh, in_specs=in_specs, out_specs=out_specs, check_vma=False)
```

time: 204 us -> 148 us (0.73)
  waiting for transfers between devices: 53 us -> 24.6 us
  Pallas kernels: 45.3 us -> 27.4 us
  starting transfers between devices: 62.8 us -> 50.5 us
  local copies, waits for them, and re-layouts: 12.6 us -> 21.1 us
  other arithmetic: 11 us -> 8.04 us
    all_to_all x4 -> x2, starting transfers between devices: 38 us -> 22.3 us  [exchange(): lax.all_to_all(packets, 'wa', split_axis=0, concat_axis=0, tiled=True)]
    ppermute x8 -> x11, waiting for transfers between devices: 38.2 us -> 23.9 us  [all_sum(): lax.ppermute(block, axis, [(i, i ^ move) for i in range(count)])]
    all_to_all x4 -> x2, waiting for transfers between devices: 14.8 us -> 0.72 us  [exchange(): lax.all_to_all(packets, 'wa', split_axis=0, concat_axis=0, tiled=True)]
    pallas_call x6 -> x3, Pallas kernels: 33.5 us -> 22.9 us  [the longest x1 11.5 us: line_terms(): pl.pallas_call(line_kernel, out_shape=(jax.ShapeDtypeStruct(received.shap...]
    unnamed x30 -> x37, local copies, waits for them, and re-layouts: 5.2 us -> 14.6 us
    pallas_call x1, Pallas kernels: 11.7 us -> 4.45 us  [local_terms(): pl.pallas_call(local_kernel, grid=(planes,), in_specs=[pl.BlockSpec(memor...]
    ppermute x8 -> x11, starting transfers between devices: 13.4 us -> 16.8 us  [all_sum(): lax.ppermute(block, axis, [(i, i ^ move) for i in range(count)])]
    another operation x2 -> x0, other arithmetic: 2.57 us -> none
  transfers between devices with their start and end apart: 17 -> 18, of which waited for: 10 -> 10; matrix products, arithmetic and copies ran while one was open for 17% -> 21% of each run, Pallas kernels for 21% -> 3%
where the time goes in v2:
time: 148 us; the launch traced here: 147 us
  starting transfers between devices  50.5 us (34%)
  Pallas kernels  27.4 us (19%)
  waiting for transfers between devices  24.6 us (17%)
  local copies, waits for them, and re-layouts  21.1 us (14%)
  matrix products  13.5 us (9%)
  other arithmetic  8.04 us (5%)
  between operations  1.63 us (1%)
    ppermute x11, waiting for transfers between devices, all_sum(): lax.ppermute(block, axis, [(i, i ^ move) for i in range(count)])  23.9 us
    all_to_all x2, starting transfers between devices, exchange(): lax.all_to_all(packets, 'wa', split_axis=0, concat_axis=0, tiled=True)  22.3 us
    ppermute x11, starting transfers between devices, all_sum(): lax.ppermute(block, axis, [(i, i ^ move) for i in range(count)])  16.8 us
    unnamed x37, local copies, waits for them, and re-layouts  14.6 us
    pallas_call x1, Pallas kernels, line_terms(): pl.pallas_call(line_kernel, out_shape=(jax.ShapeDtypeStruct(received.shap...  11.5 us
    dot_general x1, matrix products, body(): jnp.einsum('fxyj,kj->fxyk', depth_slope, matrix, preferred_element_type=j...  7.62 us
    pallas_call x1, Pallas kernels, unpack_add(): pl.pallas_call(unpack_add_kernel, grid=(planes // PACK_PLANES,), in_specs...  6.27 us
    pallas_call x1, Pallas kernels, pack(): pl.pallas_call(pack_kernel, grid=(planes // PACK_PLANES,), in_specs=[part...  5.17 us
  transfers between devices with their start and end apart: 18, of which 10 were waited for; matrix products, arithmetic and copies ran while one was open for 21% of the time, Pallas kernels for 3%

profile of v2, /device:TPU:10, one launch (start us, length us, event | category | flops | bytes accessed | tf_op | source)
XLA Modules:
  0.0 146.8 jit_solution(10279034976010669783)
XLA Ops:
  0.6 5.2 %pack.1 = bf16[64,14,8,128]{3,2,1,0:T(8,128)(2,1)} custom-call(f32[12,24,1536]{2,1,0:T(8,128)} %bitcast.42, f32[12,24,1536]{2,1,0:T(8,128)} %bitcast.35, s32[12,12,24]{2,1,0:T(8,128)} %bitcast.51), custom_call_target="tpu_custom_call" | custom-call | flops 884736 | bytes 5308416 | tf_op jit(solution)/shard_map/pack/pallas_call | solution.py:103
  5.8 12.5 %all-to-all-start = ((bf16[64,14,8,128]{3,2,1,0:T(8,128)(2,1)}), bf16[64,14,8,128]{3,2,1,0:T(8,128)(2,1)}, u32[]{:S(2)}, u32[]{:S(2)}) async-start(bf16[64,14,8,128]{3,2,1,0:T(8,128)(2,1)} %pack.1), calls=%async_computation | async-start | bytes 3670016 | tf_op jit(solution)/shard_map/all_to_all | solution.py:393
  19.3 2.1 %copy-done.9 = bf16[1536,1536]{1,0:T(8,128)(2,1)S(1)} copy-done((bf16[1536,1536]{1,0:T(8,128)(2,1)S(1)}, bf16[1536,1536]{1,0:T(8,128)(2,1)}, u32[]{:S(2)}) %copy-start.9) | copy-done | bytes 4718616
  21.4 4.1 %fusion.4.refs_6_ = bf16[2,12,24,1536]{3,2,1,0:T(8,128)(2,1)} fusion(bf16[1536,1536]{1,0:T(8,128)(2,1)S(1)} %copy-done.9, bf16[1,12,24,1536]{3,2,1,0:T(8,128)(2,1)S(1)} %get-tuple-element.46, bf16[1,12,24,1536]{3,2,1,0:T(8,128)(2,1)S(1)} %get-tuple-element.47), kind=kOutput, calls=%fused_computation.4 | convolution fusion | flops 2719678464 | bytes 8257536 | tf_op jit(solution)/shard_map/fxyj,kj->fxyk/dot_general | solution.py:401
  26.3 1.6 %dynamic-slice_bitcast_fusion = bf16[2,24,1536]{2,1,0:T(8,128)(2,1)} fusion(bf16[2,24,2,1536]{3,1,0,2:T(8,128)(2,1)} %copy.17, s32[]{:T(128)S(6)} %select_n.99), kind=kLoop, calls=%fused_computation.42 | loop fusion | bytes 294916 | tf_op jit(solution)/shard_map/jit(dynamic_index_in_dim)/squeeze | solution.py:409
  28.4 2.4 %collective-permute-start.1 = (bf16[2,24,1536]{2,1,0:T(8,128)(2,1)}, bf16[2,24,1536]{2,1,0:T(8,128)(2,1)}, u32[]{:S(2)}, u32[]{:S(2)}) collective-permute-start(bf16[2,24,1536]{2,1,0:T(8,128)(2,1)} %dynamic-slice_bitcast_fusion), channel_id=1, source_target_pairs={{0,128},{64,192},{128,0},{192,64},{1,129},{65,193},{129,1},{193,65... | collective-permute-start | bytes 442376 | tf_op jit(solution)/shard_map/ppermute | solution.py:413
  30.8 1.8 %collective-permute-start.2 = (bf16[2,24,1536]{2,1,0:T(8,128)(2,1)}, bf16[2,24,1536]{2,1,0:T(8,128)(2,1)}, u32[]{:S(2)}, u32[]{:S(2)}) collective-permute-start(bf16[2,24,1536]{2,1,0:T(8,128)(2,1)} %dynamic-slice_bitcast_fusion), channel_id=1, source_target_pairs={{0,64},{64,128},{128,192},{192,0},{1,65},{65,129},{129,193},{193,1... | collective-permute-start | bytes 442376 | tf_op jit(solution)/shard_map/ppermute | solution.py:413
  34.0 1.9 %collective-permute-start.3 = (bf16[2,24,1536]{2,1,0:T(8,128)(2,1)}, bf16[2,24,1536]{2,1,0:T(8,128)(2,1)}, u32[]{:S(2)}, u32[]{:S(2)}) collective-permute-start(bf16[2,24,1536]{2,1,0:T(8,128)(2,1)} %fusion.33), channel_id=1, source_target_pairs={{0,64},{64,128},{128,192},{1,65},{65,129},{129,193},{2,66},{66,130... | collective-permute-start | bytes 442376 | tf_op jit(solution)/shard_map/ppermute | solution.py:419
  36.6 4.7 %collective-permute-start.4 = (bf16[2,24,1536]{2,1,0:T(8,128)(2,1)}, bf16[2,24,1536]{2,1,0:T(8,128)(2,1)}, u32[]{:S(2)}, u32[]{:S(2)}) collective-permute-start(bf16[2,24,1536]{2,1,0:T(8,128)(2,1)} %pad_maximum_fusion.1), channel_id=1, source_target_pairs={{64,0},{128,64},{192,128},{65,1},{129,65},{193,129},{66,2},{130,66... | collective-permute-start | bytes 442376 | tf_op jit(solution)/shard_map/ppermute | solution.py:420
  41.3 7.6 %fusion.refs_7_ = f32[2,12,24,1536]{3,2,1,0:T(8,128)} fusion(bf16[2,12,24,1536]{3,2,1,0:T(8,128)(2,1)} %fusion.4.refs_6_, bf16[1536,1536]{1,0:T(8,128)(2,1)} %d_ref.1), kind=kOutput, calls=%fused_computation | convolution fusion | flops 2717908992 | bytes 10027008 | tf_op jit(solution)/shard_map/fxyj,kj->fxyk/dot_general | solution.py:426
  52.1 2.0 %copy-done.2 = f32[2,12,24,1536]{3,2,1,0:T(8,128)S(1)} copy-done((f32[2,12,24,1536]{3,2,1,0:T(8,128)S(1)}, f32[2,12,24,1536]{3,2,1,0:T(8,128)}, u32[]{:S(2)}) %copy-start.2) | copy-done | bytes 3538968
  54.1 4.5 %local_terms.1 = (f32[12,24,1536]{2,1,0:T(8,128)S(1)}, f32[12,24,1536]{2,1,0:T(8,128)S(1)}, f32[12,24,128]{2,1,0:T(8,128)S(1)}) custom-call(f32[12]{0:T(128)S(1)} %add_divide_fusion.fringe_ref, f32[2,24,1536]{2,1,0:T(8,128)S(1)} %get-tuple-element.39.lo_ref, f32[2,24,1536]{2,1,0:T(8,128)S(1)} %convert_select_fusion.hi_ref, f32[12,24,1536]{2,1,0:T(8,128)S(1)} %bitcast.46, ...), custom_call_target="tpu_custom_call" | custom-call | flops 26542080 | bytes 15040512 | tf_op jit(solution)/shard_map/local_terms/pallas_call | solution.py:315
  62.4 2.3 %copy-done.10 = bf16[1536,1536]{1,0:T(8,128)(2,1)S(1)} copy-done((bf16[1536,1536]{1,0:T(8,128)(2,1)S(1)}, bf16[1536,1536]{1,0:T(8,128)(2,1)}, u32[]{:S(2)}) %copy-start.10) | copy-done | bytes 4718616
  64.7 11.5 %line_terms.1 = (bf16[64,14,8,128]{3,2,1,0:T(8,128)(2,1)}, f32[1536,128]{1,0:T(8,128)S(1)}) custom-call(bf16[64,14,8,128]{3,2,1,0:T(8,128)(2,1)} %all-to-all-done.r_ref, bf16[1536,1536]{1,0:T(8,128)(2,1)S(1)} %copy-done.10), custom_call_target="tpu_custom_call" | custom-call | flops 7247757312 | bytes 8388608 | tf_op jit(solution)/shard_map/line_terms/pallas_call | solution.py:264
  76.2 9.7 %all-to-all-start.1 = ((bf16[64,14,8,128]{3,2,1,0:T(8,128)(2,1)}), bf16[64,14,8,128]{3,2,1,0:T(8,128)(2,1)S(1)}, u32[]{:S(2)}, u32[]{:S(2)}) async-start(bf16[64,14,8,128]{3,2,1,0:T(8,128)(2,1)} %get-tuple-element.34), calls=%async_computation.1 | async-start | bytes 3670016 | tf_op jit(solution)/shard_map/all_to_all | solution.py:393
  97.8 1.6 %collective-permute-start.6 = (f32[64,64]{1,0:T(8,128)S(1)}, f32[64,64]{1,0:T(8,128)S(1)}, u32[]{:S(2)}, u32[]{:S(2)}) collective-permute-start(f32[64,64]{1,0:T(8,128)S(1)} %fusion.17), channel_id=1, source_target_pairs={{0,128},{64,192},{128,0},{192,64},{1,129},{65,193},{129,1},{193,65... | collective-permute-start | bytes 49160 | tf_op jit(solution)/shard_map/ppermute | solution.py:367
  99.4 3.2 %collective-permute-start.5 = (f32[64,64]{1,0:T(8,128)S(1)}, f32[64,64]{1,0:T(8,128)S(1)}, u32[]{:S(2)}, u32[]{:S(2)}) collective-permute-start(f32[64,64]{1,0:T(8,128)S(1)} %fusion.17), channel_id=1, source_target_pairs={{0,64},{64,0},{128,192},{192,128},{1,65},{65,1},{129,193},{193,129... | collective-permute-start | bytes 49160 | tf_op jit(solution)/shard_map/ppermute | solution.py:367
  105.8 2.3 %collective-permute-start.10 = (f32[64,64]{1,0:T(8,128)S(1)}, f32[64,64]{1,0:T(8,128)S(1)}, u32[]{:S(2)}, u32[]{:S(2)}) collective-permute-start(f32[64,64]{1,0:T(8,128)S(1)} %add.115), channel_id=1, source_target_pairs={{0,32},{1,33},{2,34},{3,35},{4,36},{5,37},{6,38},{7,39},{8,40},{9,... | collective-permute-start | bytes 49160 | tf_op jit(solution)/shard_map/ppermute | solution.py:367
  108.1 2.4 %collective-permute-start.9 = (f32[64,64]{1,0:T(8,128)S(1)}, f32[64,64]{1,0:T(8,128)S(1)}, u32[]{:S(2)}, u32[]{:S(2)}) collective-permute-start(f32[64,64]{1,0:T(8,128)S(1)} %add.115), channel_id=1, source_target_pairs={{0,16},{1,17},{2,18},{3,19},{4,20},{5,21},{6,22},{7,23},{8,24},{9,... | collective-permute-start | bytes 49160 | tf_op jit(solution)/shard_map/ppermute | solution.py:367
  115.2 1.6 %collective-permute-start.14 = (f32[64,64]{1,0:T(8,128)S(1)}, f32[64,64]{1,0:T(8,128)S(1)}, u32[]{:S(2)}, u32[]{:S(2)}) collective-permute-start(f32[64,64]{1,0:T(8,128)S(1)} %add_add_fusion.1), channel_id=1, source_target_pairs={{0,6},{1,7},{2,4},{3,5},{4,2},{5,3},{6,0},{7,1},{8,14},{9,15},{10,... | collective-permute-start | bytes 49160 | tf_op jit(solution)/shard_map/ppermute | solution.py:367
  117.6 13.0 %collective-permute-done.13 = f32[64,64]{1,0:T(8,128)S(1)} collective-permute-done((f32[64,64]{1,0:T(8,128)S(1)}, f32[64,64]{1,0:T(8,128)S(1)}, u32[]{:S(2)}, u32[]{:S(2)}) %collective-permute-start.13) | collective-permute-done | bytes 16416 | tf_op jit(solution)/shard_map/ppermute | solution.py:367
  130.7 3.7 %collective-permute-start.15 = (f32[64,64]{1,0:T(8,128)S(1)}, f32[64,64]{1,0:T(8,128)S(1)}, u32[]{:S(2)}, u32[]{:S(2)}) collective-permute-start(f32[64,64]{1,0:T(8,128)S(1)} %add_add_fusion), channel_id=1, source_target_pairs={{0,8},{1,9},{2,10},{3,11},{4,12},{5,13},{6,14},{7,15},{8,0},{9,1},... | collective-permute-start | bytes 49160 | tf_op jit(solution)/shard_map/ppermute | solution.py:367
  134.4 4.2 %collective-permute-done.15 = f32[64,64]{1,0:T(8,128)S(1)} collective-permute-done((f32[64,64]{1,0:T(8,128)S(1)}, f32[64,64]{1,0:T(8,128)S(1)}, u32[]{:S(2)}, u32[]{:S(2)}) %collective-permute-start.15) | collective-permute-done | bytes 16416 | tf_op jit(solution)/shard_map/ppermute | solution.py:367
  140.5 6.3 %unpack_add.1 = (f32[12,24,1536]{2,1,0:T(8,128)}, f32[12,24,1536]{2,1,0:T(8,128)}) custom-call(f32[12,24,1536]{2,1,0:T(8,128)} %copy-done.4, f32[12,24,1536]{2,1,0:T(8,128)} %copy-done.5, bf16[64,14,8,128]{3,2,1,0:T(8,128)(2,1)} %copy-done.11), custom_call_target="tpu_custom_call" | custom-call | flops 1769472 | bytes 8847360 | tf_op jit(solution)/shard_map/unpack_add/pallas_call | solution.py:168
  (93 shorter events, 32.9 us)
Async XLA Ops:
  5.8 13.2 %copy-start = (f32[24,12,1536]{2,0,1:T(8,128)S(1)}, f32[24,12,1536]{2,0,1:T(8,128)}, u32[]{:S(2)}) copy-start(f32[24,12,1536]{2,0,1:T(8,128)} %param.10) | copy-start | bytes 5308420
  5.8 13.2 %copy-start.1 = (f32[24,12,1536]{2,0,1:T(8,128)S(1)}, f32[24,12,1536]{2,0,1:T(8,128)}, u32[]{:S(2)}) copy-start(f32[24,12,1536]{2,0,1:T(8,128)} %param.9) | copy-start | bytes 5308420
  5.8 56.6 %all-to-all-start = ((bf16[64,14,8,128]{3,2,1,0:T(8,128)(2,1)}), bf16[64,14,8,128]{3,2,1,0:T(8,128)(2,1)}, u32[]{:S(2)}, u32[]{:S(2)}) async-start(bf16[64,14,8,128]{3,2,1,0:T(8,128)(2,1)} %pack.1), calls=%async_computation | async-start | bytes 3670016 | tf_op jit(solution)/shard_map/all_to_all | solution.py:393
  21.4 4.1 %copy-start.15 = (bf16[2,24,2,1536]{3,2,1,0:T(2,128)(2,1)S(1)}, bf16[2,24,2,1536]{3,2,1,0:T(2,128)(2,1)}, u32[]{:S(2)}) copy-start(bf16[2,24,2,1536]{3,2,1,0:T(2,128)(2,1)} %param.13) | copy-start | bytes 884740
  27.8 23.0 %collective-permute-start = (bf16[2,24,1536]{2,1,0:T(8,128)(2,1)}, bf16[2,24,1536]{2,1,0:T(8,128)(2,1)}, u32[]{:S(2)}, u32[]{:S(2)}) collective-permute-start(bf16[2,24,1536]{2,1,0:T(8,128)(2,1)} %dynamic-slice_bitcast_fusion), channel_id=1, source_target_pairs={{0,192},{64,0},{128,64},{192,128},{1,193},{65,1},{129,65},{193,129... | collective-permute-start | bytes 442376 | tf_op jit(solution)/shard_map/ppermute | solution.py:413
  28.4 22.5 %collective-permute-start.1 = (bf16[2,24,1536]{2,1,0:T(8,128)(2,1)}, bf16[2,24,1536]{2,1,0:T(8,128)(2,1)}, u32[]{:S(2)}, u32[]{:S(2)}) collective-permute-start(bf16[2,24,1536]{2,1,0:T(8,128)(2,1)} %dynamic-slice_bitcast_fusion), channel_id=1, source_target_pairs={{0,128},{64,192},{128,0},{192,64},{1,129},{65,193},{129,1},{193,65... | collective-permute-start | bytes 442376 | tf_op jit(solution)/shard_map/ppermute | solution.py:413
  30.8 20.1 %collective-permute-start.2 = (bf16[2,24,1536]{2,1,0:T(8,128)(2,1)}, bf16[2,24,1536]{2,1,0:T(8,128)(2,1)}, u32[]{:S(2)}, u32[]{:S(2)}) collective-permute-start(bf16[2,24,1536]{2,1,0:T(8,128)(2,1)} %dynamic-slice_bitcast_fusion), channel_id=1, source_target_pairs={{0,64},{64,128},{128,192},{192,0},{1,65},{65,129},{129,193},{193,1... | collective-permute-start | bytes 442376 | tf_op jit(solution)/shard_map/ppermute | solution.py:413
  34.0 16.8 %collective-permute-start.3 = (bf16[2,24,1536]{2,1,0:T(8,128)(2,1)}, bf16[2,24,1536]{2,1,0:T(8,128)(2,1)}, u32[]{:S(2)}, u32[]{:S(2)}) collective-permute-start(bf16[2,24,1536]{2,1,0:T(8,128)(2,1)} %fusion.33), channel_id=1, source_target_pairs={{0,64},{64,128},{128,192},{1,65},{65,129},{129,193},{2,66},{66,130... | collective-permute-start | bytes 442376 | tf_op jit(solution)/shard_map/ppermute | solution.py:419
  36.6 12.3 %copy-start.16 = (s32[24,1536]{1,0:T(8,128)S(1)}, s32[24,1536]{1,0:T(8,128)}, u32[]{:S(2)}) copy-start(s32[24,1536]{1,0:T(8,128)} %param.14) | copy-start | bytes 442372
  36.6 13.0 %collective-permute-start.4 = (bf16[2,24,1536]{2,1,0:T(8,128)(2,1)}, bf16[2,24,1536]{2,1,0:T(8,128)(2,1)}, u32[]{:S(2)}, u32[]{:S(2)}) collective-permute-start(bf16[2,24,1536]{2,1,0:T(8,128)(2,1)} %pad_maximum_fusion.1), channel_id=1, source_target_pairs={{64,0},{128,64},{192,128},{65,1},{129,65},{193,129},{66,2},{130,66... | collective-permute-start | bytes 442376 | tf_op jit(solution)/shard_map/ppermute | solution.py:420
  76.2 9.8 %copy-start.14 = (s32[24,12,12]{0,2,1:T(8,128)S(1)}, s32[24,12,12]{0,2,1:T(8,128)}, u32[]{:S(2)}) copy-start(s32[24,12,12]{0,2,1:T(8,128)} %param.16) | copy-start | bytes 41476
  76.2 13.2 %copy-start.7 = (f32[12,24,128]{2,1,0:T(8,128)S(1)}, f32[12,24,128]{2,1,0:T(8,128)}, u32[]{:S(2)}) copy-start(f32[12,24,128]{2,1,0:T(8,128)} %copy-done.6) | copy-start | bytes 442372
  76.2 63.1 %all-to-all-start.1 = ((bf16[64,14,8,128]{3,2,1,0:T(8,128)(2,1)}), bf16[64,14,8,128]{3,2,1,0:T(8,128)(2,1)S(1)}, u32[]{:S(2)}, u32[]{:S(2)}) async-start(bf16[64,14,8,128]{3,2,1,0:T(8,128)(2,1)} %get-tuple-element.34), calls=%async_computation.1 | async-start | bytes 3670016 | tf_op jit(solution)/shard_map/all_to_all | solution.py:393
  97.8 5.9 %collective-permute-start.6 = (f32[64,64]{1,0:T(8,128)S(1)}, f32[64,64]{1,0:T(8,128)S(1)}, u32[]{:S(2)}, u32[]{:S(2)}) collective-permute-start(f32[64,64]{1,0:T(8,128)S(1)} %fusion.17), channel_id=1, source_target_pairs={{0,128},{64,192},{128,0},{192,64},{1,129},{65,193},{129,1},{193,65... | collective-permute-start | bytes 49160 | tf_op jit(solution)/shard_map/ppermute | solution.py:367
  99.4 4.3 %collective-permute-start.7 = (f32[64,64]{1,0:T(8,128)S(1)}, f32[64,64]{1,0:T(8,128)S(1)}, u32[]{:S(2)}, u32[]{:S(2)}) collective-permute-start(f32[64,64]{1,0:T(8,128)S(1)} %fusion.17), channel_id=1, source_target_pairs={{0,192},{64,128},{128,64},{192,0},{1,193},{65,129},{129,65},{193,1... | collective-permute-start | bytes 49160 | tf_op jit(solution)/shard_map/ppermute | solution.py:367
  99.4 5.1 %collective-permute-start.5 = (f32[64,64]{1,0:T(8,128)S(1)}, f32[64,64]{1,0:T(8,128)S(1)}, u32[]{:S(2)}, u32[]{:S(2)}) collective-permute-start(f32[64,64]{1,0:T(8,128)S(1)} %fusion.17), channel_id=1, source_target_pairs={{0,64},{64,0},{128,192},{192,128},{1,65},{65,1},{129,193},{193,129... | collective-permute-start | bytes 49160 | tf_op jit(solution)/shard_map/ppermute | solution.py:367
  104.5 1.3 collective-permute-start.8
  105.8 5.6 %collective-permute-start.10 = (f32[64,64]{1,0:T(8,128)S(1)}, f32[64,64]{1,0:T(8,128)S(1)}, u32[]{:S(2)}, u32[]{:S(2)}) collective-permute-start(f32[64,64]{1,0:T(8,128)S(1)} %add.115), channel_id=1, source_target_pairs={{0,32},{1,33},{2,34},{3,35},{4,36},{5,37},{6,38},{7,39},{8,40},{9,... | collective-permute-start | bytes 49160 | tf_op jit(solution)/shard_map/ppermute | solution.py:367
  108.1 4.3 %collective-permute-start.11 = (f32[64,64]{1,0:T(8,128)S(1)}, f32[64,64]{1,0:T(8,128)S(1)}, u32[]{:S(2)}, u32[]{:S(2)}) collective-permute-start(f32[64,64]{1,0:T(8,128)S(1)} %add.115), channel_id=1, source_target_pairs={{0,48},{1,49},{2,50},{3,51},{4,52},{5,53},{6,54},{7,55},{8,56},{9,... | collective-permute-start | bytes 49160 | tf_op jit(solution)/shard_map/ppermute | solution.py:367
  108.1 5.9 %collective-permute-start.9 = (f32[64,64]{1,0:T(8,128)S(1)}, f32[64,64]{1,0:T(8,128)S(1)}, u32[]{:S(2)}, u32[]{:S(2)}) collective-permute-start(f32[64,64]{1,0:T(8,128)S(1)} %add.115), channel_id=1, source_target_pairs={{0,16},{1,17},{2,18},{3,19},{4,20},{5,21},{6,22},{7,23},{8,24},{9,... | collective-permute-start | bytes 49160 | tf_op jit(solution)/shard_map/ppermute | solution.py:367
  114.0 16.6 %collective-permute-start.13 = (f32[64,64]{1,0:T(8,128)S(1)}, f32[64,64]{1,0:T(8,128)S(1)}, u32[]{:S(2)}, u32[]{:S(2)}) collective-permute-start(f32[64,64]{1,0:T(8,128)S(1)} %add_add_fusion.1), channel_id=1, source_target_pairs={{0,4},{1,5},{2,6},{3,7},{4,0},{5,1},{6,2},{7,3},{8,12},{9,13},{10,... | collective-permute-start | bytes 49160 | tf_op jit(solution)/shard_map/ppermute | solution.py:367
  115.2 15.5 %collective-permute-start.14 = (f32[64,64]{1,0:T(8,128)S(1)}, f32[64,64]{1,0:T(8,128)S(1)}, u32[]{:S(2)}, u32[]{:S(2)}) collective-permute-start(f32[64,64]{1,0:T(8,128)S(1)} %add_add_fusion.1), channel_id=1, source_target_pairs={{0,6},{1,7},{2,4},{3,5},{4,2},{5,3},{6,0},{7,1},{8,14},{9,15},{10,... | collective-permute-start | bytes 49160 | tf_op jit(solution)/shard_map/ppermute | solution.py:367
  116.8 13.9 %collective-permute-start.12 = (f32[64,64]{1,0:T(8,128)S(1)}, f32[64,64]{1,0:T(8,128)S(1)}, u32[]{:S(2)}, u32[]{:S(2)}) collective-permute-start(f32[64,64]{1,0:T(8,128)S(1)} %add_add_fusion.1), channel_id=1, source_target_pairs={{0,2},{1,3},{2,0},{3,1},{4,6},{5,7},{6,4},{7,5},{8,10},{9,11},{10,... | collective-permute-start | bytes 49160 | tf_op jit(solution)/shard_map/ppermute | solution.py:367
  130.7 7.9 %collective-permute-start.15 = (f32[64,64]{1,0:T(8,128)S(1)}, f32[64,64]{1,0:T(8,128)S(1)}, u32[]{:S(2)}, u32[]{:S(2)}) collective-permute-start(f32[64,64]{1,0:T(8,128)S(1)} %add_add_fusion), channel_id=1, source_target_pairs={{0,8},{1,9},{2,10},{3,11},{4,12},{5,13},{6,14},{7,15},{8,0},{9,1},... | collective-permute-start | bytes 49160 | tf_op jit(solution)/shard_map/ppermute | solution.py:367
  (11 other events, 17.4 us)

commit v3 on v2

--- a/solution.py
+++ b/solution.py
@@ -19,10 +19,11 @@
 
 VMEM_LIMIT = 56 * 1024 * 1024
 LOCAL_VMEM_LIMIT = 16 * 1024 * 1024
-LINE_VMEM_LIMIT = 40 * 1024 * 1024
-
-
-PACK_PLANES = 2
+LINE_VMEM_LIMIT = 56 * 1024 * 1024
+UNPACK_VMEM_LIMIT = 50 * 1024 * 1024
+
+
+PACK_PLANES = 6
 
 
 def lane_group(shape):
@@ -117,30 +118,30 @@
     )(x0, x1, classes)
 
 
-def unpack_add_kernel(part0_ref, part1_ref, ret_ref, out0_ref, out1_ref):
+def unpack_add_kernel(parts_ref, ret_ref, out0_ref, out1_ref):
     step = pl.program_id(0)
     steps = pl.num_programs(0)
     lines = ret_ref.shape[0]
-    per_plane = part0_ref.shape[2] // ZBLK
+    per_plane = parts_ref.shape[3] // ZBLK
     pairs = per_plane // 2
     left = per_plane * PACK_PLANES - (2 * lines - per_plane * PACK_PLANES * (steps - 1))
     first_left = per_plane * PACK_PLANES - left
     group = lane_group((ROWS, LANES))
     fields = (
-        (part0_ref, out0_ref, phase_step * mixing_diffusivity),
-        (part1_ref, out1_ref, phase_step),
+        (out0_ref, phase_step * mixing_diffusivity),
+        (out1_ref, phase_step),
     )
 
     def add_pairs(count):
         for pair in range(count):
             p, k = pair // pairs, (pair % pairs) * 2 * ZBLK
             line = step * (PACK_PLANES * pairs) + pair
-            for f, (part_ref, out_ref, scale) in enumerate(fields):
+            for f, (out_ref, scale) in enumerate(fields):
                 for b in range(2):
                     for t in range(3):
                         at = (p, slice(ROWS * t, ROWS * t + ROWS), slice(k + b * ZBLK, k + (b + 1) * ZBLK))
                         tile = ret_ref[line, 7 * f + 3 * b + t].astype(jnp.float32)
-                        out_ref[at] = part_ref[at] + scale * tile
+                        out_ref[at] = parts_ref[(f, *at)] + scale * tile
 
     @pl.when(step < steps - 1)
     def _():
@@ -152,34 +153,37 @@
         for m in range(left):
             block = first_left + m
             p, k = block // per_plane, (block % per_plane) * ZBLK
-            for f, (part_ref, out_ref, scale) in enumerate(fields):
+            for f, (out_ref, scale) in enumerate(fields):
                 quarters = [ret_ref[4 * m + q, 7 * f + 6].astype(jnp.float32) for q in range(4)]
                 for g in range(3):
                     tile = rolled(quarters[0], -32 * g)
                     for q in range(1, 4):
                         tile = jnp.where(group == q, rolled(quarters[q], 32 * (q - g)), tile)
                     at = (p, slice(ROWS * g, ROWS * g + ROWS), slice(k, k + ZBLK))
-                    out_ref[at] = part_ref[at] + scale * tile
-
-
-def unpack_add(part0, part1, returned):
-    planes, rows, depth = part0.shape
+                    out_ref[at] = parts_ref[(f, *at)] + scale * tile
+
+
+def unpack_add(parts, returned):
+    _, planes, rows, depth = parts.shape
     part = pl.BlockSpec((PACK_PLANES, rows, depth), lambda i: (i, 0, 0))
     return pl.pallas_call(
         unpack_add_kernel,
         grid=(planes // PACK_PLANES,),
-        in_specs=[part, part, pl.BlockSpec(returned.shape, lambda i: (0, 0, 0, 0))],
+        in_specs=[
+            pl.BlockSpec((2, PACK_PLANES, rows, depth), lambda i: (0, i, 0, 0)),
+            pl.BlockSpec(returned.shape, lambda i: (0, 0, 0, 0)),
+        ],
         out_specs=[part, part],
-        out_shape=[jax.ShapeDtypeStruct(part0.shape, jnp.float32)] * 2,
-        compiler_params=pltpu.CompilerParams(vmem_limit_bytes=VMEM_LIMIT),
-        cost_estimate=pl.CostEstimate(flops=4 * part0.size, bytes_accessed=20 * part0.size, transcendentals=0),
+        out_shape=[jax.ShapeDtypeStruct(parts.shape[1:], jnp.float32)] * 2,
+        compiler_params=pltpu.CompilerParams(vmem_limit_bytes=UNPACK_VMEM_LIMIT),
+        cost_estimate=pl.CostEstimate(flops=2 * parts.size, bytes_accessed=10 * parts.size, transcendentals=0),
         name="unpack_add",
-    )(part0, part1, returned)
+    )(parts, returned)
 
 
 SOURCES = 16
 WIDE = 2 * LANES
-MATMUL_ROWS = 768
+MATMUL_ROWS = 1536
 
 
 def unpack_lines(r_ref, x_ref):
@@ -214,8 +218,11 @@
     out_ref[src, 7 * f + 6] = packed.reshape(-1, ROWS, LANES).astype(jnp.bfloat16)
 
 
-def line_kernel(r_ref, d_ref, out_ref, sums_ref, x_ref, slope_ref):
+def line_kernel(r_ref, matrix_ref, out_ref, sums_ref, x_ref, slope_ref, d_ref, arrived):
+    copy = pltpu.make_async_copy(matrix_ref, d_ref, arrived)
+    copy.start()
     unpack_lines(r_ref, x_ref)
+    copy.wait()
     tile = MATMUL_ROWS
     count = d_ref.shape[0] // tile
 
@@ -267,7 +274,13 @@
             jax.ShapeDtypeStruct(received.shape, jnp.bfloat16),
             jax.ShapeDtypeStruct((rows, LANES), jnp.float32),
         ),
-        scratch_shapes=[pltpu.VMEM(wide, jnp.bfloat16), pltpu.VMEM(wide, jnp.bfloat16)],
+        in_specs=[pl.BlockSpec(memory_space=pltpu.VMEM), pl.BlockSpec(memory_space=pl.ANY)],
+        scratch_shapes=[
+            pltpu.VMEM(wide, jnp.bfloat16),
+            pltpu.VMEM(wide, jnp.bfloat16),
+            pltpu.VMEM(matrix.shape, matrix.dtype),
+            pltpu.SemaphoreType.DMA,
+        ],
         compiler_params=pltpu.CompilerParams(vmem_limit_bytes=LINE_VMEM_LIMIT),
         cost_estimate=pl.CostEstimate(
             flops=12 * rows * rows * WIDE, bytes_accessed=2 * rows * rows + 4 * received.size, transcendentals=0
@@ -280,7 +293,7 @@
     fringe_ref, lo_ref, hi_ref, *refs
 ):
     fields = (refs[0:3], refs[3:6])
-    slope_ref, curve_ref, speed_ref, inflow_ref, mix_ref, heat_ref, sums_ref = refs[6:]
+    slope_ref, curve_ref, speed_ref, inflow_ref, parts_ref, sums_ref = refs[6:]
     p = pl.program_id(0)
     last = pl.num_programs(0) - 1
     fringe = fringe_ref[p]
@@ -297,9 +310,9 @@
         if f == 0:
             depth = slope_ref[0, 0].astype(jnp.float32)
             dissipation = (2.0 * mixing_diffusivity) * (axial_slope**2 + depth**2)
-            mix_ref[0] = x + phase_step * rhs
+            parts_ref[0, 0] = x + phase_step * rhs
         else:
-            heat_ref[0] = x + phase_step * (rhs + release_rate * dissipation)
+            parts_ref[1, 0] = x + phase_step * (rhs + release_rate * dissipation)
     lane = lax.broadcasted_iota(jnp.int32, sums_ref.shape[1:], 1)
     sums = jnp.zeros(sums_ref.shape[1:], jnp.float32)
     for k in range(dissipation.shape[1] // ZBLK):
@@ -331,13 +344,11 @@
             fixed((2, rows, depth)),
         ],
         out_specs=[
-            pl.BlockSpec((1, rows, depth), lambda p: (p, 0, 0)),
-            pl.BlockSpec((1, rows, depth), lambda p: (p, 0, 0)),
+            pl.BlockSpec((2, 1, rows, depth), lambda p: (0, p, 0, 0)),
             pl.BlockSpec((1, rows, LANES), lambda p: (p, 0, 0)),
         ],
         out_shape=[
-            jax.ShapeDtypeStruct((planes, rows, depth), jnp.float32),
-            jax.ShapeDtypeStruct((planes, rows, depth), jnp.float32),
+            jax.ShapeDtypeStruct((2, planes, rows, depth), jnp.float32),
             jax.ShapeDtypeStruct((planes, rows, LANES), jnp.float32),
         ],
         compiler_params=pltpu.CompilerParams(vmem_limit_bytes=LOCAL_VMEM_LIMIT),
@@ -360,15 +371,17 @@
     return total
 
 
-def all_sum(block):
+def all_sum(block, last_after):
     for axis, bits in (("gx", (1, 2)), ("wa", (1,)), ("wa", (16, 32)), ("wa", (2, 4)), ("wa", (8,))):
+        if bits == (8,):
+            block, last_after = lax.optimization_barrier((block, last_after))
         count = lax.axis_size(axis)
         moves = bits if len(bits) == 1 else (bits[0], bits[1], bits[0] + bits[1])
         arrived = [lax.ppermute(block, axis, [(i, i ^ move) for i in range(count)]) for move in moves]
         block = block + arrived[0]
         if len(arrived) == 3:
             block = block + (arrived[1] + arrived[2])
-    return block
+    return block, last_after
 
 
 def body(
@@ -426,11 +439,11 @@
     depth_curve = jnp.einsum("fxyj,kj->fxyk", depth_slope, matrix, preferred_element_type=jnp.float32)
     plane_numbers = (slab_index * plane_count + jnp.arange(plane_count, dtype=jnp.int32)).astype(jnp.float32)
     fringe = 1.0 / (1.0 + plane_numbers / plane_count)
-    part0, part1, local_sums = local_terms(
+    parts, local_sums = local_terms(
         x0, x1, lo, hi, depth_slope, depth_curve, streamwise_speed, inflow_cells, fringe
     )
 
-    received, part0, part1, local_sums = lax.optimization_barrier((received, part0, part1, local_sums))
+    received, parts, local_sums = lax.optimization_barrier((received, parts, local_sums))
     returned, line_sums = line_terms(received, matrix)
     back = exchange(returned)
 
@@ -444,11 +457,11 @@
     bins = bin_sums(
         jnp.concatenate([own_values, line_values]), jnp.concatenate([own_classes, line_classes])
     )
-    summed = all_sum(bins)
+    summed, back = all_sum(bins, back)
     per_bin = row_count * lines * plane_count * slab_count * depth_count // (HB * HB)
     histogram = summed / per_bin
 
-    mixture_next, temperature_next = unpack_add(part0, part1, back)
+    mixture_next, temperature_next = unpack_add(parts, back)
     return (jnp.transpose(mixture_next, (1, 0, 2)), jnp.transpose(temperature_next, (1, 0, 2)), histogram)
 
 

time: 148 us -> 138 us (0.932)
  local copies, waits for them, and re-layouts: 21.1 us -> 10.9 us
  waiting for transfers between devices: 24.6 us -> 28.6 us
  Pallas kernels: 27.4 us -> 24.4 us
  other arithmetic: 8.04 us -> 6.47 us
    unnamed x37 -> x33, local copies, waits for them, and re-layouts: 14.6 us -> 7.64 us
    ppermute x11, waiting for transfers between devices: 23.9 us -> 27.3 us  [all_sum(): lax.ppermute(block, axis, [(i, i ^ move) for i in range(count)])]
    pallas_call x1, Pallas kernels: 6.27 us -> 3.55 us  [unpack_add(): pl.pallas_call(unpack_add_kernel, grid=(planes // PACK_PLANES,), in_specs...]
    pallas_call x1, Pallas kernels: 5.17 us -> 3.54 us  [pack(): pl.pallas_call(pack_kernel, grid=(planes // PACK_PLANES,), in_specs=[part...]
  transfers between devices with their start and end apart: 18 -> 18, of which waited for: 10 -> 10; matrix products, arithmetic and copies ran while one was open for 21% -> 17% of each run, Pallas kernels for 3% -> 6%
where the time goes in v3:
time: 138 us; the launch traced here: 136 us
  starting transfers between devices  50.8 us (37%)
  waiting for transfers between devices  28.6 us (21%)
  Pallas kernels  24.4 us (18%)
  matrix products  13.5 us (10%)
  local copies, waits for them, and re-layouts  10.9 us (8%)
  other arithmetic  6.47 us (5%)
  between operations  1.74 us (1%)
    ppermute x11, waiting for transfers between devices, all_sum(): lax.ppermute(block, axis, [(i, i ^ move) for i in range(count)])  27.3 us
    all_to_all x2, starting transfers between devices, exchange(): lax.all_to_all(packets, 'wa', split_axis=0, concat_axis=0, tiled=True)  21.7 us
    ppermute x11, starting transfers between devices, all_sum(): lax.ppermute(block, axis, [(i, i ^ move) for i in range(count)])  17.5 us
    pallas_call x1, Pallas kernels, line_terms(): pl.pallas_call(line_kernel, out_shape=(jax.ShapeDtypeStruct(received.shap...  12.8 us
    unnamed x33, local copies, waits for them, and re-layouts  7.64 us
    dot_general x1, matrix products, body(): jnp.einsum('fxyj,kj->fxyk', depth_slope, matrix, preferred_element_type=j...  7.57 us
    ppermute x1, starting transfers between devices, body(): lax.ppermute(first.astype(jnp.bfloat16), 'gx', backward).astype(jnp.float32)  4.86 us
    ppermute x3, starting transfers between devices, body(): arrived = lax.ppermute(held_plane, 'gx', table)  4.75 us
  transfers between devices with their start and end apart: 18, of which 10 were waited for; matrix products, arithmetic and copies ran while one was open for 17% of the time, Pallas kernels for 6%

profile of v3, /device:TPU:10, one launch (start us, length us, event | category | flops | bytes accessed | tf_op | source)
XLA Modules:
  0.0 136.3 jit_solution(5636518814467907798)
XLA Ops:
  0.6 3.5 %pack.1 = bf16[64,14,8,128]{3,2,1,0:T(8,128)(2,1)} custom-call(f32[12,24,1536]{2,1,0:T(8,128)} %bitcast.42, f32[12,24,1536]{2,1,0:T(8,128)} %bitcast.35, s32[12,12,24]{2,1,0:T(8,128)} %bitcast.51), custom_call_target="tpu_custom_call" | custom-call | flops 884736 | bytes 5308416 | tf_op jit(solution)/shard_map/pack/pallas_call | solution.py:104
  4.2 12.5 %all-to-all-start = ((bf16[64,14,8,128]{3,2,1,0:T(8,128)(2,1)}), bf16[64,14,8,128]{3,2,1,0:T(8,128)(2,1)}, u32[]{:S(2)}, u32[]{:S(2)}) async-start(bf16[64,14,8,128]{3,2,1,0:T(8,128)(2,1)} %pack.1), calls=%async_computation | async-start | bytes 3670016 | tf_op jit(solution)/shard_map/all_to_all | solution.py:406
  17.6 2.1 %copy-done.14 = bf16[1536,1536]{1,0:T(8,128)(2,1)S(1)} copy-done((bf16[1536,1536]{1,0:T(8,128)(2,1)S(1)}, bf16[1536,1536]{1,0:T(8,128)(2,1)}, u32[]{:S(2)}) %copy-start.14) | copy-done | bytes 4718616
  19.8 4.1 %fusion.4.refs_6_ = bf16[2,12,24,1536]{3,2,1,0:T(8,128)(2,1)} fusion(bf16[1536,1536]{1,0:T(8,128)(2,1)S(1)} %copy-done.14, bf16[1,12,24,1536]{3,2,1,0:T(8,128)(2,1)S(1)} %get-tuple-element.46, bf16[1,12,24,1536]{3,2,1,0:T(8,128)(2,1)S(1)} %get-tuple-element.47), kind=kOutput, calls=%fused_computation.4 | convolution fusion | flops 2719678464 | bytes 8257536 | tf_op jit(solution)/shard_map/fxyj,kj->fxyk/dot_general | solution.py:414
  24.6 1.6 %dynamic-slice_bitcast_fusion = bf16[2,24,1536]{2,1,0:T(8,128)(2,1)} fusion(bf16[2,24,2,1536]{3,1,0,2:T(8,128)(2,1)} %copy.17, s32[]{:T(128)S(6)} %select_n.99), kind=kLoop, calls=%fused_computation.42 | loop fusion | bytes 294916 | tf_op jit(solution)/shard_map/jit(dynamic_index_in_dim)/squeeze | solution.py:422
  26.7 2.4 %collective-permute-start.1 = (bf16[2,24,1536]{2,1,0:T(8,128)(2,1)}, bf16[2,24,1536]{2,1,0:T(8,128)(2,1)}, u32[]{:S(2)}, u32[]{:S(2)}) collective-permute-start(bf16[2,24,1536]{2,1,0:T(8,128)(2,1)} %dynamic-slice_bitcast_fusion), channel_id=1, source_target_pairs={{0,128},{64,192},{128,0},{192,64},{1,129},{65,193},{129,1},{193,65... | collective-permute-start | bytes 442376 | tf_op jit(solution)/shard_map/ppermute | solution.py:426
  29.2 1.8 %collective-permute-start.2 = (bf16[2,24,1536]{2,1,0:T(8,128)(2,1)}, bf16[2,24,1536]{2,1,0:T(8,128)(2,1)}, u32[]{:S(2)}, u32[]{:S(2)}) collective-permute-start(bf16[2,24,1536]{2,1,0:T(8,128)(2,1)} %dynamic-slice_bitcast_fusion), channel_id=1, source_target_pairs={{0,64},{64,128},{128,192},{192,0},{1,65},{65,129},{129,193},{193,1... | collective-permute-start | bytes 442376 | tf_op jit(solution)/shard_map/ppermute | solution.py:426
  32.4 1.9 %collective-permute-start.3 = (bf16[2,24,1536]{2,1,0:T(8,128)(2,1)}, bf16[2,24,1536]{2,1,0:T(8,128)(2,1)}, u32[]{:S(2)}, u32[]{:S(2)}) collective-permute-start(bf16[2,24,1536]{2,1,0:T(8,128)(2,1)} %fusion.33), channel_id=1, source_target_pairs={{0,64},{64,128},{128,192},{1,65},{65,129},{129,193},{2,66},{66,130... | collective-permute-start | bytes 442376 | tf_op jit(solution)/shard_map/ppermute | solution.py:432
  35.0 4.9 %collective-permute-start.4 = (bf16[2,24,1536]{2,1,0:T(8,128)(2,1)}, bf16[2,24,1536]{2,1,0:T(8,128)(2,1)}, u32[]{:S(2)}, u32[]{:S(2)}) collective-permute-start(bf16[2,24,1536]{2,1,0:T(8,128)(2,1)} %pad_maximum_fusion.1), channel_id=1, source_target_pairs={{64,0},{128,64},{192,128},{65,1},{129,65},{193,129},{66,2},{130,66... | collective-permute-start | bytes 442376 | tf_op jit(solution)/shard_map/ppermute | solution.py:433
  39.9 7.6 %fusion.refs_7_ = f32[2,12,24,1536]{3,2,1,0:T(8,128)} fusion(bf16[2,12,24,1536]{3,2,1,0:T(8,128)(2,1)} %fusion.4.refs_6_, bf16[1536,1536]{1,0:T(8,128)(2,1)} %matrix_ref.1), kind=kOutput, calls=%fused_computation | convolution fusion | flops 2717908992 | bytes 10027008 | tf_op jit(solution)/shard_map/fxyj,kj->fxyk/dot_general | solution.py:439
  50.6 2.0 %copy-done.2 = f32[2,12,24,1536]{3,2,1,0:T(8,128)S(1)} copy-done((f32[2,12,24,1536]{3,2,1,0:T(8,128)S(1)}, f32[2,12,24,1536]{3,2,1,0:T(8,128)}, u32[]{:S(2)}) %copy-start.2) | copy-done | bytes 3538968
  52.6 4.4 %local_terms.1 = (f32[2,12,24,1536]{3,2,1,0:T(8,128)S(1)}, f32[12,24,128]{2,1,0:T(8,128)S(1)}) custom-call(f32[12]{0:T(128)S(1)} %add_divide_fusion.fringe_ref, f32[2,24,1536]{2,1,0:T(8,128)S(1)} %get-tuple-element.39.lo_ref, f32[2,24,1536]{2,1,0:T(8,128)S(1)} %convert_select_fusion.hi_ref, f32[12,24,1536]{2,1,0:T(8,128)S(1)} %bitcast.46, ...), custom_call_target="tpu_custom_call" | custom-call | flops 26542080 | bytes 15040512 | tf_op jit(solution)/shard_map/local_terms/pallas_call | solution.py:328
  57.0 1.7 %copy-done.3 = f32[2,12,24,1536]{3,2,1,0:T(8,128)} copy-done((f32[2,12,24,1536]{3,2,1,0:T(8,128)}, f32[2,12,24,1536]{3,2,1,0:T(8,128)S(1)}, u32[]{:S(2)}) %copy-start.3) | copy-done | bytes 3538968
  60.7 12.8 %line_terms.1 = (bf16[64,14,8,128]{3,2,1,0:T(8,128)(2,1)}, f32[1536,128]{1,0:T(8,128)}) custom-call(bf16[64,14,8,128]{3,2,1,0:T(8,128)(2,1)} %all-to-all-done.r_ref, bf16[1536,1536]{1,0:T(8,128)(2,1)} %matrix_ref.1), custom_call_target="tpu_custom_call" | custom-call | flops 7247757312 | bytes 8388608 | tf_op jit(solution)/shard_map/line_terms/pallas_call | solution.py:271
  73.6 9.2 %all-to-all-start.1 = ((bf16[64,14,8,128]{3,2,1,0:T(8,128)(2,1)}), bf16[64,14,8,128]{3,2,1,0:T(8,128)(2,1)S(1)}, u32[]{:S(2)}, u32[]{:S(2)}) async-start(bf16[64,14,8,128]{3,2,1,0:T(8,128)(2,1)} %get-tuple-element.34), calls=%async_computation.1 | async-start | bytes 3670016 | tf_op jit(solution)/shard_map/all_to_all | solution.py:406
  88.6 3.4 %collective-permute-start.5 = (f32[64,64]{1,0:T(8,128)S(1)}, f32[64,64]{1,0:T(8,128)S(1)}, u32[]{:S(2)}, u32[]{:S(2)}) collective-permute-start(f32[64,64]{1,0:T(8,128)S(1)} %fusion.17), channel_id=1, source_target_pairs={{0,64},{64,0},{128,192},{192,128},{1,65},{65,1},{129,193},{193,129... | collective-permute-start | bytes 49160 | tf_op jit(solution)/shard_map/ppermute | solution.py:380
  95.2 2.3 %collective-permute-start.10 = (f32[64,64]{1,0:T(8,128)S(1)}, f32[64,64]{1,0:T(8,128)S(1)}, u32[]{:S(2)}, u32[]{:S(2)}) collective-permute-start(f32[64,64]{1,0:T(8,128)S(1)} %add.115), channel_id=1, source_target_pairs={{0,32},{1,33},{2,34},{3,35},{4,36},{5,37},{6,38},{7,39},{8,40},{9,... | collective-permute-start | bytes 49160 | tf_op jit(solution)/shard_map/ppermute | solution.py:380
  97.5 2.4 %collective-permute-start.9 = (f32[64,64]{1,0:T(8,128)S(1)}, f32[64,64]{1,0:T(8,128)S(1)}, u32[]{:S(2)}, u32[]{:S(2)}) collective-permute-start(f32[64,64]{1,0:T(8,128)S(1)} %add.115), channel_id=1, source_target_pairs={{0,16},{1,17},{2,18},{3,19},{4,20},{5,21},{6,22},{7,23},{8,24},{9,... | collective-permute-start | bytes 49160 | tf_op jit(solution)/shard_map/ppermute | solution.py:380
  99.9 1.9 %collective-permute-done.10 = f32[64,64]{1,0:T(8,128)S(1)} collective-permute-done((f32[64,64]{1,0:T(8,128)S(1)}, f32[64,64]{1,0:T(8,128)S(1)}, u32[]{:S(2)}, u32[]{:S(2)}) %collective-permute-start.10) | collective-permute-done | bytes 16416 | tf_op jit(solution)/shard_map/ppermute | solution.py:380
  102.4 2.4 %collective-permute-start.13 = (f32[64,64]{1,0:T(8,128)S(1)}, f32[64,64]{1,0:T(8,128)S(1)}, u32[]{:S(2)}, u32[]{:S(2)}) collective-permute-start(f32[64,64]{1,0:T(8,128)S(1)} %add_add_fusion.1), channel_id=1, source_target_pairs={{0,4},{1,5},{2,6},{3,7},{4,0},{5,1},{6,2},{7,3},{8,12},{9,13},{10,... | collective-permute-start | bytes 49160 | tf_op jit(solution)/shard_map/ppermute | solution.py:380
  104.8 1.8 %collective-permute-start.14 = (f32[64,64]{1,0:T(8,128)S(1)}, f32[64,64]{1,0:T(8,128)S(1)}, u32[]{:S(2)}, u32[]{:S(2)}) collective-permute-start(f32[64,64]{1,0:T(8,128)S(1)} %add_add_fusion.1), channel_id=1, source_target_pairs={{0,6},{1,7},{2,4},{3,5},{4,2},{5,3},{6,0},{7,1},{8,14},{9,15},{10,... | collective-permute-start | bytes 49160 | tf_op jit(solution)/shard_map/ppermute | solution.py:380
  106.7 20.8 %collective-permute-done.13 = f32[64,64]{1,0:T(8,128)S(1)} collective-permute-done((f32[64,64]{1,0:T(8,128)S(1)}, f32[64,64]{1,0:T(8,128)S(1)}, u32[]{:S(2)}, u32[]{:S(2)}) %collective-permute-start.13) | collective-permute-done | bytes 16416 | tf_op jit(solution)/shard_map/ppermute | solution.py:380
  127.6 3.7 %collective-permute-start.15 = (f32[64,64]{1,0:T(8,128)S(1)}, f32[64,64]{1,0:T(8,128)S(1)}, u32[]{:S(2)}, u32[]{:S(2)}) collective-permute-start(f32[64,64]{1,0:T(8,128)S(1)} %add_add_fusion), channel_id=1, source_target_pairs={{0,8},{1,9},{2,10},{3,11},{4,12},{5,13},{6,14},{7,15},{8,0},{9,1},... | collective-permute-start | bytes 49160 | tf_op jit(solution)/shard_map/ppermute | solution.py:380
  131.3 3.6 %unpack_add.1 = (f32[12,24,1536]{2,1,0:T(8,128)}, f32[12,24,1536]{2,1,0:T(8,128)}) custom-call(f32[2,12,24,1536]{3,2,1,0:T(8,128)} %copy-done.3, bf16[64,14,8,128]{3,2,1,0:T(8,128)(2,1)S(1)} %all-to-all-done.1.ret_ref), custom_call_target="tpu_custom_call" | custom-call | flops 1769472 | bytes 8847360 | tf_op jit(solution)/shard_map/unpack_add/pallas_call | solution.py:169
  (89 shorter events, 19.7 us)
Async XLA Ops:
  4.2 13.2 %copy-start = (f32[24,12,1536]{2,0,1:T(8,128)S(1)}, f32[24,12,1536]{2,0,1:T(8,128)}, u32[]{:S(2)}) copy-start(f32[24,12,1536]{2,0,1:T(8,128)} %param.10) | copy-start | bytes 5308420
  4.2 13.2 %copy-start.1 = (f32[24,12,1536]{2,0,1:T(8,128)S(1)}, f32[24,12,1536]{2,0,1:T(8,128)}, u32[]{:S(2)}) copy-start(f32[24,12,1536]{2,0,1:T(8,128)} %param.9) | copy-start | bytes 5308420
  4.2 56.6 %all-to-all-start = ((bf16[64,14,8,128]{3,2,1,0:T(8,128)(2,1)}), bf16[64,14,8,128]{3,2,1,0:T(8,128)(2,1)}, u32[]{:S(2)}, u32[]{:S(2)}) async-start(bf16[64,14,8,128]{3,2,1,0:T(8,128)(2,1)} %pack.1), calls=%async_computation | async-start | bytes 3670016 | tf_op jit(solution)/shard_map/all_to_all | solution.py:406
  26.2 23.1 %collective-permute-start = (bf16[2,24,1536]{2,1,0:T(8,128)(2,1)}, bf16[2,24,1536]{2,1,0:T(8,128)(2,1)}, u32[]{:S(2)}, u32[]{:S(2)}) collective-permute-start(bf16[2,24,1536]{2,1,0:T(8,128)(2,1)} %dynamic-slice_bitcast_fusion), channel_id=1, source_target_pairs={{0,192},{64,0},{128,64},{192,128},{1,193},{65,1},{129,65},{193,129... | collective-permute-start | bytes 442376 | tf_op jit(solution)/shard_map/ppermute | solution.py:426
  26.7 22.6 %collective-permute-start.1 = (bf16[2,24,1536]{2,1,0:T(8,128)(2,1)}, bf16[2,24,1536]{2,1,0:T(8,128)(2,1)}, u32[]{:S(2)}, u32[]{:S(2)}) collective-permute-start(bf16[2,24,1536]{2,1,0:T(8,128)(2,1)} %dynamic-slice_bitcast_fusion), channel_id=1, source_target_pairs={{0,128},{64,192},{128,0},{192,64},{1,129},{65,193},{129,1},{193,65... | collective-permute-start | bytes 442376 | tf_op jit(solution)/shard_map/ppermute | solution.py:426
  29.2 20.2 %collective-permute-start.2 = (bf16[2,24,1536]{2,1,0:T(8,128)(2,1)}, bf16[2,24,1536]{2,1,0:T(8,128)(2,1)}, u32[]{:S(2)}, u32[]{:S(2)}) collective-permute-start(bf16[2,24,1536]{2,1,0:T(8,128)(2,1)} %dynamic-slice_bitcast_fusion), channel_id=1, source_target_pairs={{0,64},{64,128},{128,192},{192,0},{1,65},{65,129},{129,193},{193,1... | collective-permute-start | bytes 442376 | tf_op jit(solution)/shard_map/ppermute | solution.py:426
  32.4 16.9 %collective-permute-start.3 = (bf16[2,24,1536]{2,1,0:T(8,128)(2,1)}, bf16[2,24,1536]{2,1,0:T(8,128)(2,1)}, u32[]{:S(2)}, u32[]{:S(2)}) collective-permute-start(bf16[2,24,1536]{2,1,0:T(8,128)(2,1)} %fusion.33), channel_id=1, source_target_pairs={{0,64},{64,128},{128,192},{1,65},{65,129},{129,193},{2,66},{66,130... | collective-permute-start | bytes 442376 | tf_op jit(solution)/shard_map/ppermute | solution.py:432
  35.0 12.4 %copy-start.13 = (s32[24,1536]{1,0:T(8,128)S(1)}, s32[24,1536]{1,0:T(8,128)}, u32[]{:S(2)}) copy-start(s32[24,1536]{1,0:T(8,128)} %param.14) | copy-start | bytes 442372
  35.0 13.1 %collective-permute-start.4 = (bf16[2,24,1536]{2,1,0:T(8,128)(2,1)}, bf16[2,24,1536]{2,1,0:T(8,128)(2,1)}, u32[]{:S(2)}, u32[]{:S(2)}) collective-permute-start(bf16[2,24,1536]{2,1,0:T(8,128)(2,1)} %pad_maximum_fusion.1), channel_id=1, source_target_pairs={{64,0},{128,64},{192,128},{65,1},{129,65},{193,129},{66,2},{130,66... | collective-permute-start | bytes 442376 | tf_op jit(solution)/shard_map/ppermute | solution.py:433
  73.6 9.2 %copy-start.11 = (s32[24,12,12]{0,2,1:T(8,128)S(1)}, s32[24,12,12]{0,2,1:T(8,128)}, u32[]{:S(2)}) copy-start(s32[24,12,12]{0,2,1:T(8,128)} %param.16) | copy-start | bytes 41476
  73.6 10.8 %copy-start.6 = (f32[12,24,128]{2,1,0:T(8,128)S(1)}, f32[12,24,128]{2,1,0:T(8,128)}, u32[]{:S(2)}) copy-start(f32[12,24,128]{2,1,0:T(8,128)} %copy-done.5) | copy-start | bytes 442372
  73.6 11.0 %copy-start.10 = (f32[1536,128]{1,0:T(8,128)S(1)}, f32[1536,128]{1,0:T(8,128)}, u32[]{:S(2)}) copy-start(f32[1536,128]{1,0:T(8,128)} %get-tuple-element.33) | copy-start | bytes 2359300
  73.6 54.0 %all-to-all-start.1 = ((bf16[64,14,8,128]{3,2,1,0:T(8,128)(2,1)}), bf16[64,14,8,128]{3,2,1,0:T(8,128)(2,1)S(1)}, u32[]{:S(2)}, u32[]{:S(2)}) async-start(bf16[64,14,8,128]{3,2,1,0:T(8,128)(2,1)} %get-tuple-element.34), calls=%async_computation.1 | async-start | bytes 3670016 | tf_op jit(solution)/shard_map/all_to_all | solution.py:406
  87.2 5.8 %collective-permute-start.6 = (f32[64,64]{1,0:T(8,128)S(1)}, f32[64,64]{1,0:T(8,128)S(1)}, u32[]{:S(2)}, u32[]{:S(2)}) collective-permute-start(f32[64,64]{1,0:T(8,128)S(1)} %fusion.17), channel_id=1, source_target_pairs={{0,128},{64,192},{128,0},{192,64},{1,129},{65,193},{129,1},{193,65... | collective-permute-start | bytes 49160 | tf_op jit(solution)/shard_map/ppermute | solution.py:380
  88.6 4.4 %collective-permute-start.7 = (f32[64,64]{1,0:T(8,128)S(1)}, f32[64,64]{1,0:T(8,128)S(1)}, u32[]{:S(2)}, u32[]{:S(2)}) collective-permute-start(f32[64,64]{1,0:T(8,128)S(1)} %fusion.17), channel_id=1, source_target_pairs={{0,192},{64,128},{128,64},{192,0},{1,193},{65,129},{129,65},{193,1... | collective-permute-start | bytes 49160 | tf_op jit(solution)/shard_map/ppermute | solution.py:380
  88.6 5.3 %collective-permute-start.5 = (f32[64,64]{1,0:T(8,128)S(1)}, f32[64,64]{1,0:T(8,128)S(1)}, u32[]{:S(2)}, u32[]{:S(2)}) collective-permute-start(f32[64,64]{1,0:T(8,128)S(1)} %fusion.17), channel_id=1, source_target_pairs={{0,64},{64,0},{128,192},{192,128},{1,65},{65,1},{129,193},{193,129... | collective-permute-start | bytes 49160 | tf_op jit(solution)/shard_map/ppermute | solution.py:380
  93.9 1.3 collective-permute-start.8
  95.2 6.6 %collective-permute-start.10 = (f32[64,64]{1,0:T(8,128)S(1)}, f32[64,64]{1,0:T(8,128)S(1)}, u32[]{:S(2)}, u32[]{:S(2)}) collective-permute-start(f32[64,64]{1,0:T(8,128)S(1)} %add.115), channel_id=1, source_target_pairs={{0,32},{1,33},{2,34},{3,35},{4,36},{5,37},{6,38},{7,39},{8,40},{9,... | collective-permute-start | bytes 49160 | tf_op jit(solution)/shard_map/ppermute | solution.py:380
  97.5 4.7 %collective-permute-start.11 = (f32[64,64]{1,0:T(8,128)S(1)}, f32[64,64]{1,0:T(8,128)S(1)}, u32[]{:S(2)}, u32[]{:S(2)}) collective-permute-start(f32[64,64]{1,0:T(8,128)S(1)} %add.115), channel_id=1, source_target_pairs={{0,48},{1,49},{2,50},{3,51},{4,52},{5,53},{6,54},{7,55},{8,56},{9,... | collective-permute-start | bytes 49160 | tf_op jit(solution)/shard_map/ppermute | solution.py:380
  97.5 4.9 %collective-permute-start.9 = (f32[64,64]{1,0:T(8,128)S(1)}, f32[64,64]{1,0:T(8,128)S(1)}, u32[]{:S(2)}, u32[]{:S(2)}) collective-permute-start(f32[64,64]{1,0:T(8,128)S(1)} %add.115), channel_id=1, source_target_pairs={{0,16},{1,17},{2,18},{3,19},{4,20},{5,21},{6,22},{7,23},{8,24},{9,... | collective-permute-start | bytes 49160 | tf_op jit(solution)/shard_map/ppermute | solution.py:380
  102.4 25.0 %collective-permute-start.13 = (f32[64,64]{1,0:T(8,128)S(1)}, f32[64,64]{1,0:T(8,128)S(1)}, u32[]{:S(2)}, u32[]{:S(2)}) collective-permute-start(f32[64,64]{1,0:T(8,128)S(1)} %add_add_fusion.1), channel_id=1, source_target_pairs={{0,4},{1,5},{2,6},{3,7},{4,0},{5,1},{6,2},{7,3},{8,12},{9,13},{10,... | collective-permute-start | bytes 49160 | tf_op jit(solution)/shard_map/ppermute | solution.py:380
  104.8 22.8 %collective-permute-start.14 = (f32[64,64]{1,0:T(8,128)S(1)}, f32[64,64]{1,0:T(8,128)S(1)}, u32[]{:S(2)}, u32[]{:S(2)}) collective-permute-start(f32[64,64]{1,0:T(8,128)S(1)} %add_add_fusion.1), channel_id=1, source_target_pairs={{0,6},{1,7},{2,4},{3,5},{4,2},{5,3},{6,0},{7,1},{8,14},{9,15},{10,... | collective-permute-start | bytes 49160 | tf_op jit(solution)/shard_map/ppermute | solution.py:380
  106.7 20.9 %collective-permute-start.12 = (f32[64,64]{1,0:T(8,128)S(1)}, f32[64,64]{1,0:T(8,128)S(1)}, u32[]{:S(2)}, u32[]{:S(2)}) collective-permute-start(f32[64,64]{1,0:T(8,128)S(1)} %add_add_fusion.1), channel_id=1, source_target_pairs={{0,2},{1,3},{2,0},{3,1},{4,6},{5,7},{6,4},{7,5},{8,10},{9,11},{10,... | collective-permute-start | bytes 49160 | tf_op jit(solution)/shard_map/ppermute | solution.py:380
  127.6 8.1 %collective-permute-start.15 = (f32[64,64]{1,0:T(8,128)S(1)}, f32[64,64]{1,0:T(8,128)S(1)}, u32[]{:S(2)}, u32[]{:S(2)}) collective-permute-start(f32[64,64]{1,0:T(8,128)S(1)} %add_add_fusion), channel_id=1, source_target_pairs={{0,8},{1,9},{2,10},{3,11},{4,12},{5,13},{6,14},{7,15},{8,0},{9,1},... | collective-permute-start | bytes 49160 | tf_op jit(solution)/shard_map/ppermute | solution.py:380
  (9 other events, 17.3 us)

commit v4 on v3

--- a/solution.py
+++ b/solution.py
@@ -372,16 +372,21 @@
 
 
 def all_sum(block, last_after):
-    for axis, bits in (("gx", (1, 2)), ("wa", (1,)), ("wa", (16, 32)), ("wa", (2, 4)), ("wa", (8,))):
-        if bits == (8,):
-            block, last_after = lax.optimization_barrier((block, last_after))
-        count = lax.axis_size(axis)
-        moves = bits if len(bits) == 1 else (bits[0], bits[1], bits[0] + bits[1])
-        arrived = [lax.ppermute(block, axis, [(i, i ^ move) for i in range(count)]) for move in moves]
-        block = block + arrived[0]
-        if len(arrived) == 3:
-            block = block + (arrived[1] + arrived[2])
-    return block, last_after
+    def moved(axis, move):
+        return lax.ppermute(block, axis, [(i, i ^ move) for i in range(lax.axis_size(axis))])
+
+    for axis, bit in (("gx", 1), ("wa", 16)):
+        arrived = [moved(axis, move) for move in (bit, 2 * bit, 3 * bit)]
+        block = (block + arrived[0]) + (arrived[1] + arrived[2])
+        if axis == "gx":
+            block = block + moved("wa", 1)
+    lines = lax.axis_size("wa")
+    across = lax.ppermute(block, "wa", [(i, i ^ 8) for i in range(lines) if i % 2 == 1])
+    near = jnp.where(lax.axis_index("wa") % 2 == 1, across, block)
+    arrived = [lax.ppermute(block, "wa", [(i, i ^ (move + 8 * (i % 2))) for i in range(lines)]) for move in (2, 4, 6)]
+    block = (near + arrived[0]) + (arrived[1] + arrived[2])
+    block, last_after = lax.optimization_barrier((block, last_after))
+    return block + moved("wa", 1), last_after
 
 
 def body(
@@ -457,9 +462,8 @@
     bins = bin_sums(
         jnp.concatenate([own_values, line_values]), jnp.concatenate([own_classes, line_classes])
     )
-    summed, back = all_sum(bins, back)
     per_bin = row_count * lines * plane_count * slab_count * depth_count // (HB * HB)
-    histogram = summed / per_bin
+    histogram, back = all_sum(bins / per_bin, back)
 
     mixture_next, temperature_next = unpack_add(parts, back)
     return (jnp.transpose(mixture_next, (1, 0, 2)), jnp.transpose(temperature_next, (1, 0, 2)), histogram)

time: 138 us -> 136 us (0.986)
  waiting for transfers between devices: 28.6 us -> 19.9 us
  local copies, waits for them, and re-layouts: 10.9 us -> 16.8 us
  other arithmetic: 6.47 us -> 8.01 us
  starting transfers between devices: 50.8 us -> 49.4 us
    ppermute x11 -> x12, waiting for transfers between devices: 27.3 us -> 18.5 us  [the longest x3 12 us: all_sum(): lax.ppermute(block, 'wa', [(i, i ^ move + 8 * (i % 2)) for i in range(lin...]
    unnamed x33 -> x35, local copies, waits for them, and re-layouts: 7.64 us -> 10.3 us
    ppermute x11 -> x12, starting transfers between devices: 17.5 us -> 16.1 us  [the longest x8 11.9 us: moved(): lax.ppermute(block, axis, [(i, i ^ move) for i in range(lax.axis_size(axi...]
  transfers between devices with their start and end apart: 18 -> 19, of which waited for: 10 -> 10; matrix products, arithmetic and copies ran while one was open for 17% -> 23% of each run, Pallas kernels for 6% -> 6%
where the time goes in v4:
time: 136 us; the launch traced here: 134 us
  starting transfers between devices  49.4 us (36%)
  Pallas kernels  24.4 us (18%)
  waiting for transfers between devices  19.9 us (15%)
  local copies, waits for them, and re-layouts  16.8 us (12%)
  matrix products  13.5 us (10%)
  other arithmetic  8.01 us (6%)
  between operations  1.7 us (1%)
    all_to_all x2, starting transfers between devices, exchange(): lax.all_to_all(packets, 'wa', split_axis=0, concat_axis=0, tiled=True)  21.7 us
    pallas_call x1, Pallas kernels, line_terms(): pl.pallas_call(line_kernel, out_shape=(jax.ShapeDtypeStruct(received.shap...  12.8 us
    ppermute x3, waiting for transfers between devices, all_sum(): lax.ppermute(block, 'wa', [(i, i ^ move + 8 * (i % 2)) for i in range(lin...  12 us
    ppermute x8, starting transfers between devices, moved(): lax.ppermute(block, axis, [(i, i ^ move) for i in range(lax.axis_size(axi...  11.9 us
    unnamed x35, local copies, waits for them, and re-layouts  10.3 us
    dot_general x1, matrix products, body(): jnp.einsum('fxyj,kj->fxyk', depth_slope, matrix, preferred_element_type=j...  7.57 us
    ppermute x8, waiting for transfers between devices, moved(): lax.ppermute(block, axis, [(i, i ^ move) for i in range(lax.axis_size(axi...  6.5 us
    ppermute x1, starting transfers between devices, body(): lax.ppermute(first.astype(jnp.bfloat16), 'gx', backward).astype(jnp.float32)  4.88 us
  transfers between devices with their start and end apart: 19, of which 10 were waited for; matrix products, arithmetic and copies ran while one was open for 23% of the time, Pallas kernels for 6%

profile of v4, /device:TPU:10, one launch (start us, length us, event | category | flops | bytes accessed | tf_op | source)
XLA Modules:
  0.0 133.7 jit_solution(9501912478837605936)
XLA Ops:
  0.6 3.5 %pack.1 = bf16[64,14,8,128]{3,2,1,0:T(8,128)(2,1)} custom-call(f32[12,24,1536]{2,1,0:T(8,128)} %bitcast.42, f32[12,24,1536]{2,1,0:T(8,128)} %bitcast.35, s32[12,12,24]{2,1,0:T(8,128)} %bitcast.51), custom_call_target="tpu_custom_call" | custom-call | flops 884736 | bytes 5308416 | tf_op jit(solution)/shard_map/pack/pallas_call | solution.py:104
  4.2 12.5 %all-to-all-start = ((bf16[64,14,8,128]{3,2,1,0:T(8,128)(2,1)}), bf16[64,14,8,128]{3,2,1,0:T(8,128)(2,1)}, u32[]{:S(2)}, u32[]{:S(2)}) async-start(bf16[64,14,8,128]{3,2,1,0:T(8,128)(2,1)} %pack.1), calls=%async_computation | async-start | bytes 3670016 | tf_op jit(solution)/shard_map/all_to_all | solution.py:411
  17.6 2.1 %copy-done.15 = bf16[1536,1536]{1,0:T(8,128)(2,1)S(1)} copy-done((bf16[1536,1536]{1,0:T(8,128)(2,1)S(1)}, bf16[1536,1536]{1,0:T(8,128)(2,1)}, u32[]{:S(2)}) %copy-start.15) | copy-done | bytes 4718616
  19.7 4.1 %fusion.4.refs_6_ = bf16[2,12,24,1536]{3,2,1,0:T(8,128)(2,1)} fusion(bf16[1536,1536]{1,0:T(8,128)(2,1)S(1)} %copy-done.15, bf16[1,12,24,1536]{3,2,1,0:T(8,128)(2,1)S(1)} %get-tuple-element.46, bf16[1,12,24,1536]{3,2,1,0:T(8,128)(2,1)S(1)} %get-tuple-element.47), kind=kOutput, calls=%fused_computation.4 | convolution fusion | flops 2719678464 | bytes 8257536 | tf_op jit(solution)/shard_map/fxyj,kj->fxyk/dot_general | solution.py:419
  24.6 1.6 %dynamic-slice_bitcast_fusion = bf16[2,24,1536]{2,1,0:T(8,128)(2,1)} fusion(bf16[2,24,2,1536]{3,1,0,2:T(8,128)(2,1)} %copy.17, s32[]{:T(128)S(6)} %select_n.111), kind=kLoop, calls=%fused_computation.43 | loop fusion | bytes 294916 | tf_op jit(solution)/shard_map/jit(dynamic_index_in_dim)/squeeze | solution.py:427
  26.7 2.4 %collective-permute-start.1 = (bf16[2,24,1536]{2,1,0:T(8,128)(2,1)}, bf16[2,24,1536]{2,1,0:T(8,128)(2,1)}, u32[]{:S(2)}, u32[]{:S(2)}) collective-permute-start(bf16[2,24,1536]{2,1,0:T(8,128)(2,1)} %dynamic-slice_bitcast_fusion), channel_id=1, source_target_pairs={{0,128},{64,192},{128,0},{192,64},{1,129},{65,193},{129,1},{193,65... | collective-permute-start | bytes 442376 | tf_op jit(solution)/shard_map/ppermute | solution.py:431
  29.2 1.8 %collective-permute-start.2 = (bf16[2,24,1536]{2,1,0:T(8,128)(2,1)}, bf16[2,24,1536]{2,1,0:T(8,128)(2,1)}, u32[]{:S(2)}, u32[]{:S(2)}) collective-permute-start(bf16[2,24,1536]{2,1,0:T(8,128)(2,1)} %dynamic-slice_bitcast_fusion), channel_id=1, source_target_pairs={{0,64},{64,128},{128,192},{192,0},{1,65},{65,129},{129,193},{193,1... | collective-permute-start | bytes 442376 | tf_op jit(solution)/shard_map/ppermute | solution.py:431
  32.3 1.9 %collective-permute-start.3 = (bf16[2,24,1536]{2,1,0:T(8,128)(2,1)}, bf16[2,24,1536]{2,1,0:T(8,128)(2,1)}, u32[]{:S(2)}, u32[]{:S(2)}) collective-permute-start(bf16[2,24,1536]{2,1,0:T(8,128)(2,1)} %fusion.34), channel_id=1, source_target_pairs={{0,64},{64,128},{128,192},{1,65},{65,129},{129,193},{2,66},{66,130... | collective-permute-start | bytes 442376 | tf_op jit(solution)/shard_map/ppermute | solution.py:437
  35.0 4.9 %collective-permute-start.4 = (bf16[2,24,1536]{2,1,0:T(8,128)(2,1)}, bf16[2,24,1536]{2,1,0:T(8,128)(2,1)}, u32[]{:S(2)}, u32[]{:S(2)}) collective-permute-start(bf16[2,24,1536]{2,1,0:T(8,128)(2,1)} %pad_maximum_fusion.1), channel_id=1, source_target_pairs={{64,0},{128,64},{192,128},{65,1},{129,65},{193,129},{66,2},{130,66... | collective-permute-start | bytes 442376 | tf_op jit(solution)/shard_map/ppermute | solution.py:438
  39.9 7.6 %fusion.refs_7_ = f32[2,12,24,1536]{3,2,1,0:T(8,128)} fusion(bf16[2,12,24,1536]{3,2,1,0:T(8,128)(2,1)} %fusion.4.refs_6_, bf16[1536,1536]{1,0:T(8,128)(2,1)} %matrix_ref.1), kind=kOutput, calls=%fused_computation | convolution fusion | flops 2717908992 | bytes 10027008 | tf_op jit(solution)/shard_map/fxyj,kj->fxyk/dot_general | solution.py:444
  50.6 2.0 %copy-done.2 = f32[2,12,24,1536]{3,2,1,0:T(8,128)S(1)} copy-done((f32[2,12,24,1536]{3,2,1,0:T(8,128)S(1)}, f32[2,12,24,1536]{3,2,1,0:T(8,128)}, u32[]{:S(2)}) %copy-start.2) | copy-done | bytes 3538968
  52.6 4.4 %local_terms.1 = (f32[2,12,24,1536]{3,2,1,0:T(8,128)S(1)}, f32[12,24,128]{2,1,0:T(8,128)S(1)}) custom-call(f32[12]{0:T(128)S(1)} %add_divide_fusion.fringe_ref, f32[2,24,1536]{2,1,0:T(8,128)S(1)} %get-tuple-element.39.lo_ref, f32[2,24,1536]{2,1,0:T(8,128)S(1)} %convert_select_fusion.hi_ref, f32[12,24,1536]{2,1,0:T(8,128)S(1)} %bitcast.46, ...), custom_call_target="tpu_custom_call" | custom-call | flops 26542080 | bytes 15040512 | tf_op jit(solution)/shard_map/local_terms/pallas_call | solution.py:328
  57.0 1.7 %copy-done.3 = f32[2,12,24,1536]{3,2,1,0:T(8,128)} copy-done((f32[2,12,24,1536]{3,2,1,0:T(8,128)}, f32[2,12,24,1536]{3,2,1,0:T(8,128)S(1)}, u32[]{:S(2)}) %copy-start.3) | copy-done | bytes 3538968
  60.7 12.8 %line_terms.1 = (bf16[64,14,8,128]{3,2,1,0:T(8,128)(2,1)}, f32[1536,128]{1,0:T(8,128)}) custom-call(bf16[64,14,8,128]{3,2,1,0:T(8,128)(2,1)} %all-to-all-done.r_ref, bf16[1536,1536]{1,0:T(8,128)(2,1)} %matrix_ref.1), custom_call_target="tpu_custom_call" | custom-call | flops 7247757312 | bytes 8388608 | tf_op jit(solution)/shard_map/line_terms/pallas_call | solution.py:271
  73.6 9.2 %all-to-all-start.1 = ((bf16[64,14,8,128]{3,2,1,0:T(8,128)(2,1)}), bf16[64,14,8,128]{3,2,1,0:T(8,128)(2,1)S(1)}, u32[]{:S(2)}, u32[]{:S(2)}) async-start(bf16[64,14,8,128]{3,2,1,0:T(8,128)(2,1)} %get-tuple-element.34), calls=%async_computation.1 | async-start | bytes 3670016 | tf_op jit(solution)/shard_map/all_to_all | solution.py:411
  82.9 1.3 %constant_dynamic-update-slice_fusion.2 = s32[8064]{0:T(1024)} fusion(s32[8064]{0:T(1024)} %custom-call.1, s32[3456]{0:T(1024)S(1)} %concatenate.50), kind=kLoop, calls=%fused_computation.64 | loop fusion | bytes 30208
  96.0 3.5 %collective-permute-start.5 = (f32[64,64]{1,0:T(8,128)S(1)}, f32[64,64]{1,0:T(8,128)S(1)}, u32[]{:S(2)}, u32[]{:S(2)}) collective-permute-start(f32[64,64]{1,0:T(8,128)S(1)} %fusion.18), channel_id=1, source_target_pairs={{0,64},{64,0},{128,192},{192,128},{1,65},{65,1},{129,193},{193,129... | collective-permute-start | bytes 49160 | tf_op jit(solution)/shard_map/ppermute | solution.py:376
  102.7 2.3 %collective-permute-start.10 = (f32[64,64]{1,0:T(8,128)S(1)}, f32[64,64]{1,0:T(8,128)S(1)}, u32[]{:S(2)}, u32[]{:S(2)}) collective-permute-start(f32[64,64]{1,0:T(8,128)S(1)} %add.119), channel_id=1, source_target_pairs={{0,32},{1,33},{2,34},{3,35},{4,36},{5,37},{6,38},{7,39},{8,40},{9,... | collective-permute-start | bytes 49160 | tf_op jit(solution)/shard_map/ppermute | solution.py:376
  104.9 2.4 %collective-permute-start.9 = (f32[64,64]{1,0:T(8,128)S(1)}, f32[64,64]{1,0:T(8,128)S(1)}, u32[]{:S(2)}, u32[]{:S(2)}) collective-permute-start(f32[64,64]{1,0:T(8,128)S(1)} %add.119), channel_id=1, source_target_pairs={{0,16},{1,17},{2,18},{3,19},{4,20},{5,21},{6,22},{7,23},{8,24},{9,... | collective-permute-start | bytes 49160 | tf_op jit(solution)/shard_map/ppermute | solution.py:376
  109.3 1.5 %collective-permute-done.9 = f32[64,64]{1,0:T(8,128)S(1)} collective-permute-done((f32[64,64]{1,0:T(8,128)S(1)}, f32[64,64]{1,0:T(8,128)S(1)}, u32[]{:S(2)}, u32[]{:S(2)}) %collective-permute-start.9) | collective-permute-done | bytes 16416 | tf_op jit(solution)/shard_map/ppermute | solution.py:376
  112.0 1.6 %collective-permute-start.15 = (f32[64,64]{1,0:T(8,128)S(1)}, f32[64,64]{1,0:T(8,128)S(1)}, u32[]{:S(2)}, u32[]{:S(2)}) collective-permute-start(f32[64,64]{1,0:T(8,128)S(1)} %add_add_fusion.1), channel_id=1, source_target_pairs={{0,6},{1,15},{2,4},{3,13},{4,2},{5,11},{6,0},{7,9},{8,14},{9,7},{1... | collective-permute-start | bytes 49160 | tf_op jit(solution)/shard_map/ppermute | solution.py:386
  115.0 11.5 %collective-permute-done.14 = f32[64,64]{1,0:T(8,128)S(1)} collective-permute-done((f32[64,64]{1,0:T(8,128)S(1)}, f32[64,64]{1,0:T(8,128)S(1)}, u32[]{:S(2)}, u32[]{:S(2)}) %collective-permute-start.14) | collective-permute-done | bytes 16416 | tf_op jit(solution)/shard_map/ppermute | solution.py:386
  127.2 2.3 %collective-permute-start.16 = (f32[64,64]{1,0:T(8,128)S(1)}, f32[64,64]{1,0:T(8,128)S(1)}, u32[]{:S(2)}, u32[]{:S(2)}) collective-permute-start(f32[64,64]{1,0:T(8,128)S(1)} %add_add_fusion), channel_id=1, source_target_pairs={{0,1},{1,0},{2,3},{3,2},{4,5},{5,4},{6,7},{7,6},{8,9},{9,8},{10,11... | collective-permute-start | bytes 49160 | tf_op jit(solution)/shard_map/ppermute | solution.py:376
  129.5 3.6 %unpack_add.1 = (f32[12,24,1536]{2,1,0:T(8,128)}, f32[12,24,1536]{2,1,0:T(8,128)}) custom-call(f32[2,12,24,1536]{3,2,1,0:T(8,128)} %copy-done.3, bf16[64,14,8,128]{3,2,1,0:T(8,128)(2,1)S(1)} %all-to-all-done.1.ret_ref), custom_call_target="tpu_custom_call" | custom-call | flops 1769472 | bytes 8847360 | tf_op jit(solution)/shard_map/unpack_add/pallas_call | solution.py:169
  (93 shorter events, 29.3 us)
Async XLA Ops:
  4.2 13.2 %copy-start = (f32[24,12,1536]{2,0,1:T(8,128)S(1)}, f32[24,12,1536]{2,0,1:T(8,128)}, u32[]{:S(2)}) copy-start(f32[24,12,1536]{2,0,1:T(8,128)} %param.10) | copy-start | bytes 5308420
  4.2 13.2 %copy-start.1 = (f32[24,12,1536]{2,0,1:T(8,128)S(1)}, f32[24,12,1536]{2,0,1:T(8,128)}, u32[]{:S(2)}) copy-start(f32[24,12,1536]{2,0,1:T(8,128)} %param.9) | copy-start | bytes 5308420
  4.2 56.6 %all-to-all-start = ((bf16[64,14,8,128]{3,2,1,0:T(8,128)(2,1)}), bf16[64,14,8,128]{3,2,1,0:T(8,128)(2,1)}, u32[]{:S(2)}, u32[]{:S(2)}) async-start(bf16[64,14,8,128]{3,2,1,0:T(8,128)(2,1)} %pack.1), calls=%async_computation | async-start | bytes 3670016 | tf_op jit(solution)/shard_map/all_to_all | solution.py:411
  26.2 23.1 %collective-permute-start = (bf16[2,24,1536]{2,1,0:T(8,128)(2,1)}, bf16[2,24,1536]{2,1,0:T(8,128)(2,1)}, u32[]{:S(2)}, u32[]{:S(2)}) collective-permute-start(bf16[2,24,1536]{2,1,0:T(8,128)(2,1)} %dynamic-slice_bitcast_fusion), channel_id=1, source_target_pairs={{0,192},{64,0},{128,64},{192,128},{1,193},{65,1},{129,65},{193,129... | collective-permute-start | bytes 442376 | tf_op jit(solution)/shard_map/ppermute | solution.py:431
  26.7 22.6 %collective-permute-start.1 = (bf16[2,24,1536]{2,1,0:T(8,128)(2,1)}, bf16[2,24,1536]{2,1,0:T(8,128)(2,1)}, u32[]{:S(2)}, u32[]{:S(2)}) collective-permute-start(bf16[2,24,1536]{2,1,0:T(8,128)(2,1)} %dynamic-slice_bitcast_fusion), channel_id=1, source_target_pairs={{0,128},{64,192},{128,0},{192,64},{1,129},{65,193},{129,1},{193,65... | collective-permute-start | bytes 442376 | tf_op jit(solution)/shard_map/ppermute | solution.py:431
  29.2 20.2 %collective-permute-start.2 = (bf16[2,24,1536]{2,1,0:T(8,128)(2,1)}, bf16[2,24,1536]{2,1,0:T(8,128)(2,1)}, u32[]{:S(2)}, u32[]{:S(2)}) collective-permute-start(bf16[2,24,1536]{2,1,0:T(8,128)(2,1)} %dynamic-slice_bitcast_fusion), channel_id=1, source_target_pairs={{0,64},{64,128},{128,192},{192,0},{1,65},{65,129},{129,193},{193,1... | collective-permute-start | bytes 442376 | tf_op jit(solution)/shard_map/ppermute | solution.py:431
  32.3 17.0 %collective-permute-start.3 = (bf16[2,24,1536]{2,1,0:T(8,128)(2,1)}, bf16[2,24,1536]{2,1,0:T(8,128)(2,1)}, u32[]{:S(2)}, u32[]{:S(2)}) collective-permute-start(bf16[2,24,1536]{2,1,0:T(8,128)(2,1)} %fusion.34), channel_id=1, source_target_pairs={{0,64},{64,128},{128,192},{1,65},{65,129},{129,193},{2,66},{66,130... | collective-permute-start | bytes 442376 | tf_op jit(solution)/shard_map/ppermute | solution.py:437
  35.0 12.5 %copy-start.13 = (s32[24,1536]{1,0:T(8,128)S(1)}, s32[24,1536]{1,0:T(8,128)}, u32[]{:S(2)}) copy-start(s32[24,1536]{1,0:T(8,128)} %param.14) | copy-start | bytes 442372
  35.0 13.1 %collective-permute-start.4 = (bf16[2,24,1536]{2,1,0:T(8,128)(2,1)}, bf16[2,24,1536]{2,1,0:T(8,128)(2,1)}, u32[]{:S(2)}, u32[]{:S(2)}) collective-permute-start(bf16[2,24,1536]{2,1,0:T(8,128)(2,1)} %pad_maximum_fusion.1), channel_id=1, source_target_pairs={{64,0},{128,64},{192,128},{65,1},{129,65},{193,129},{66,2},{130,66... | collective-permute-start | bytes 442376 | tf_op jit(solution)/shard_map/ppermute | solution.py:438
  73.6 12.7 %copy-start.6 = (f32[12,24,128]{2,1,0:T(8,128)S(1)}, f32[12,24,128]{2,1,0:T(8,128)}, u32[]{:S(2)}) copy-start(f32[12,24,128]{2,1,0:T(8,128)} %copy-done.5) | copy-start | bytes 442372
  73.6 13.0 %copy-start.10 = (f32[1536,128]{1,0:T(8,128)S(1)}, f32[1536,128]{1,0:T(8,128)}, u32[]{:S(2)}) copy-start(f32[1536,128]{1,0:T(8,128)} %get-tuple-element.33) | copy-start | bytes 2359300
  73.6 53.6 %all-to-all-start.1 = ((bf16[64,14,8,128]{3,2,1,0:T(8,128)(2,1)}), bf16[64,14,8,128]{3,2,1,0:T(8,128)(2,1)S(1)}, u32[]{:S(2)}, u32[]{:S(2)}) async-start(bf16[64,14,8,128]{3,2,1,0:T(8,128)(2,1)} %get-tuple-element.34), calls=%async_computation.1 | async-start | bytes 3670016 | tf_op jit(solution)/shard_map/all_to_all | solution.py:411
  94.7 5.6 %collective-permute-start.6 = (f32[64,64]{1,0:T(8,128)S(1)}, f32[64,64]{1,0:T(8,128)S(1)}, u32[]{:S(2)}, u32[]{:S(2)}) collective-permute-start(f32[64,64]{1,0:T(8,128)S(1)} %fusion.18), channel_id=1, source_target_pairs={{0,128},{64,192},{128,0},{192,64},{1,129},{65,193},{129,1},{193,65... | collective-permute-start | bytes 49160 | tf_op jit(solution)/shard_map/ppermute | solution.py:376
  96.0 4.3 %collective-permute-start.7 = (f32[64,64]{1,0:T(8,128)S(1)}, f32[64,64]{1,0:T(8,128)S(1)}, u32[]{:S(2)}, u32[]{:S(2)}) collective-permute-start(f32[64,64]{1,0:T(8,128)S(1)} %fusion.18), channel_id=1, source_target_pairs={{0,192},{64,128},{128,64},{192,0},{1,193},{65,129},{129,65},{193,1... | collective-permute-start | bytes 49160 | tf_op jit(solution)/shard_map/ppermute | solution.py:376
  96.0 5.4 %collective-permute-start.5 = (f32[64,64]{1,0:T(8,128)S(1)}, f32[64,64]{1,0:T(8,128)S(1)}, u32[]{:S(2)}, u32[]{:S(2)}) collective-permute-start(f32[64,64]{1,0:T(8,128)S(1)} %fusion.18), channel_id=1, source_target_pairs={{0,64},{64,0},{128,192},{192,128},{1,65},{65,1},{129,193},{193,129... | collective-permute-start | bytes 49160 | tf_op jit(solution)/shard_map/ppermute | solution.py:376
  101.4 1.3 collective-permute-start.8
  102.7 5.7 %collective-permute-start.10 = (f32[64,64]{1,0:T(8,128)S(1)}, f32[64,64]{1,0:T(8,128)S(1)}, u32[]{:S(2)}, u32[]{:S(2)}) collective-permute-start(f32[64,64]{1,0:T(8,128)S(1)} %add.119), channel_id=1, source_target_pairs={{0,32},{1,33},{2,34},{3,35},{4,36},{5,37},{6,38},{7,39},{8,40},{9,... | collective-permute-start | bytes 49160 | tf_op jit(solution)/shard_map/ppermute | solution.py:376
  104.9 4.3 %collective-permute-start.11 = (f32[64,64]{1,0:T(8,128)S(1)}, f32[64,64]{1,0:T(8,128)S(1)}, u32[]{:S(2)}, u32[]{:S(2)}) collective-permute-start(f32[64,64]{1,0:T(8,128)S(1)} %add.119), channel_id=1, source_target_pairs={{0,48},{1,49},{2,50},{3,51},{4,52},{5,53},{6,54},{7,55},{8,56},{9,... | collective-permute-start | bytes 49160 | tf_op jit(solution)/shard_map/ppermute | solution.py:376
  104.9 5.8 %collective-permute-start.9 = (f32[64,64]{1,0:T(8,128)S(1)}, f32[64,64]{1,0:T(8,128)S(1)}, u32[]{:S(2)}, u32[]{:S(2)}) collective-permute-start(f32[64,64]{1,0:T(8,128)S(1)} %add.119), channel_id=1, source_target_pairs={{0,16},{1,17},{2,18},{3,19},{4,20},{5,21},{6,22},{7,23},{8,24},{9,... | collective-permute-start | bytes 49160 | tf_op jit(solution)/shard_map/ppermute | solution.py:376
  110.8 15.8 %collective-permute-start.14 = (f32[64,64]{1,0:T(8,128)S(1)}, f32[64,64]{1,0:T(8,128)S(1)}, u32[]{:S(2)}, u32[]{:S(2)}) collective-permute-start(f32[64,64]{1,0:T(8,128)S(1)} %add_add_fusion.1), channel_id=1, source_target_pairs={{0,4},{1,13},{2,6},{3,15},{4,0},{5,9},{6,2},{7,11},{8,12},{9,5},{1... | collective-permute-start | bytes 49160 | tf_op jit(solution)/shard_map/ppermute | solution.py:386
  112.0 14.5 %collective-permute-start.15 = (f32[64,64]{1,0:T(8,128)S(1)}, f32[64,64]{1,0:T(8,128)S(1)}, u32[]{:S(2)}, u32[]{:S(2)}) collective-permute-start(f32[64,64]{1,0:T(8,128)S(1)} %add_add_fusion.1), channel_id=1, source_target_pairs={{0,6},{1,15},{2,4},{3,13},{4,2},{5,11},{6,0},{7,9},{8,14},{9,7},{1... | collective-permute-start | bytes 49160 | tf_op jit(solution)/shard_map/ppermute | solution.py:386
  113.6 13.4 %collective-permute-start.13 = (f32[64,64]{1,0:T(8,128)S(1)}, f32[64,64]{1,0:T(8,128)S(1)}, u32[]{:S(2)}, u32[]{:S(2)}) collective-permute-start(f32[64,64]{1,0:T(8,128)S(1)} %add_add_fusion.1), channel_id=1, source_target_pairs={{0,2},{1,11},{2,0},{3,9},{4,6},{5,15},{6,4},{7,13},{8,10},{9,3},{1... | collective-permute-start | bytes 49160 | tf_op jit(solution)/shard_map/ppermute | solution.py:386
  114.4 12.7 %collective-permute-start.12 = (f32[64,64]{1,0:T(8,128)S(1)}, f32[64,64]{1,0:T(8,128)S(1)}, u32[]{:S(2)}, u32[]{:S(2)}) collective-permute-start(f32[64,64]{1,0:T(8,128)S(1)} %add_add_fusion.1), channel_id=1, source_target_pairs={{1,9},{3,11},{5,13},{7,15},{9,1},{11,3},{13,5},{15,7},{17,25},{19,... | collective-permute-start | bytes 49160 | tf_op jit(solution)/shard_map/ppermute | solution.py:384
  127.2 5.9 %collective-permute-start.16 = (f32[64,64]{1,0:T(8,128)S(1)}, f32[64,64]{1,0:T(8,128)S(1)}, u32[]{:S(2)}, u32[]{:S(2)}) collective-permute-start(f32[64,64]{1,0:T(8,128)S(1)} %add_add_fusion), channel_id=1, source_target_pairs={{0,1},{1,0},{2,3},{3,2},{4,5},{5,4},{6,7},{7,6},{8,9},{9,8},{10,11... | collective-permute-start | bytes 49160 | tf_op jit(solution)/shard_map/ppermute | solution.py:376
  (11 other events, 28.8 us)

commit v5 on v4

--- a/solution.py
+++ b/solution.py
@@ -186,7 +186,7 @@
 MATMUL_ROWS = 1536
 
 
-def unpack_lines(r_ref, x_ref):
+def unpack_lines(r_ref, x_ref, first, last):
     def step(i, carry):
         src = pl.ds(i * SOURCES, SOURCES)
         rows = pl.ds(pl.multiple_of(i * (24 * SOURCES), 24 * SOURCES), 24 * SOURCES)
@@ -194,13 +194,13 @@
             for b in range(2):
                 tiles = r_ref[src, 7 * f + 3 * b : 7 * f + 3 * b + 3].astype(jnp.float32)
                 x_ref[f, rows, b * LANES : (b + 1) * LANES] = tiles.reshape(24 * SOURCES, LANES).astype(jnp.bfloat16)
-            last = r_ref[src, 7 * f + 6].astype(jnp.float32).reshape(ROWS * SOURCES, LANES)
-            parts = [rolled(last, -32 * g).reshape(SOURCES, ROWS, LANES) for g in range(3)]
+            quarter = r_ref[src, 7 * f + 6].astype(jnp.float32).reshape(ROWS * SOURCES, LANES)
+            parts = [rolled(quarter, -32 * g).reshape(SOURCES, ROWS, LANES) for g in range(3)]
             tiles = jnp.stack(parts, axis=1)
             x_ref[2, rows, f * LANES : (f + 1) * LANES] = tiles.reshape(24 * SOURCES, LANES).astype(jnp.bfloat16)
         return carry
 
-    lax.fori_loop(0, r_ref.shape[0] // SOURCES, step, 0)
+    lax.fori_loop(first, last, step, 0)
 
 
 def pack_whole(values, out_ref, src, f):
@@ -218,13 +218,28 @@
     out_ref[src, 7 * f + 6] = packed.reshape(-1, ROWS, LANES).astype(jnp.bfloat16)
 
 
-def line_kernel(r_ref, matrix_ref, out_ref, sums_ref, x_ref, slope_ref, d_ref, arrived):
-    copy = pltpu.make_async_copy(matrix_ref, d_ref, arrived)
-    copy.start()
-    unpack_lines(r_ref, x_ref)
-    copy.wait()
+R_CHUNKS = 4
+
+
+def line_kernel(
+    lines_ref, matrix_ref, out_ref, sums_ref, x_ref, slope_ref, r_ref, d_ref, r_arrived, d_arrived
+):
+    sources, rows_all = r_ref.shape[0], d_ref.shape[0]
+    r_step = sources // R_CHUNKS
+
+    def r_copy(c):
+        part = pl.ds(c * r_step, r_step)
+        return pltpu.make_async_copy(lines_ref.at[part], r_ref.at[part], r_arrived.at[c])
+
+    for c in range(R_CHUNKS):
+        r_copy(c).start()
+    d_copy = pltpu.make_async_copy(matrix_ref, d_ref, d_arrived)
+    d_copy.start()
+    for c in range(R_CHUNKS):
+        r_copy(c).wait()
+        unpack_lines(r_ref, x_ref, c * (r_step // SOURCES), (c + 1) * (r_step // SOURCES))
+    d_copy.wait()
     tile = MATMUL_ROWS
-    count = d_ref.shape[0] // tile
 
     def slope_step(i, carry):
         rows = pl.ds(pl.multiple_of(i * tile, tile), tile)
@@ -243,26 +258,25 @@
         sums_ref[rows, :] = sums
         return carry
 
-    lax.fori_loop(0, count, slope_step, 0)
+    lax.fori_loop(0, rows_all // tile, slope_step, 0)
 
     def curve_step(i, carry):
         rows = pl.ds(pl.multiple_of(i * tile, tile), tile)
         src = pl.ds(i * (tile // 24), tile // 24)
-        matrix = d_ref[rows, :]
 
         def heat(curve, slope):
             slope = slope.astype(jnp.float32)
             return heat_diffusivity * curve + (release_rate * 2.0 * mixing_diffusivity) * slope**2
 
-        pack_whole(jnp.dot(matrix, slope_ref[0], preferred_element_type=jnp.float32), out_ref, src, 0)
-        curve = jnp.dot(matrix, slope_ref[1], preferred_element_type=jnp.float32)
+        pack_whole(jnp.dot(d_ref[rows, :], slope_ref[0], preferred_element_type=jnp.float32), out_ref, src, 0)
+        curve = jnp.dot(d_ref[rows, :], slope_ref[1], preferred_element_type=jnp.float32)
         pack_whole(heat(curve, slope_ref[0, rows, :]), out_ref, src, 1)
-        curve = jnp.dot(matrix, slope_ref[2], preferred_element_type=jnp.float32)
+        curve = jnp.dot(d_ref[rows, :], slope_ref[2], preferred_element_type=jnp.float32)
         pack_quarter(curve[:, :LANES], out_ref, src, 0)
         pack_quarter(heat(curve[:, LANES:], slope_ref[2, rows, :LANES]), out_ref, src, 1)
         return carry
 
-    lax.fori_loop(0, count, curve_step, 0)
+    lax.fori_loop(0, rows_all // tile, curve_step, 0)
 
 
 def line_terms(received, matrix):
@@ -274,11 +288,13 @@
             jax.ShapeDtypeStruct(received.shape, jnp.bfloat16),
             jax.ShapeDtypeStruct((rows, LANES), jnp.float32),
         ),
-        in_specs=[pl.BlockSpec(memory_space=pltpu.VMEM), pl.BlockSpec(memory_space=pl.ANY)],
+        in_specs=[pl.BlockSpec(memory_space=pl.ANY)] * 2,
         scratch_shapes=[
             pltpu.VMEM(wide, jnp.bfloat16),
             pltpu.VMEM(wide, jnp.bfloat16),
+            pltpu.VMEM(received.shape, received.dtype),
             pltpu.VMEM(matrix.shape, matrix.dtype),
+            pltpu.SemaphoreType.DMA((R_CHUNKS,)),
             pltpu.SemaphoreType.DMA,
         ],
         compiler_params=pltpu.CompilerParams(vmem_limit_bytes=LINE_VMEM_LIMIT),
@@ -357,13 +373,11 @@
     )(fringe, lo, hi, x0, x0, x0, x1, x1, x1, slope, curve, speed, inflow)
 
 
-def bin_sums(values, classes):
-    row = classes // HB
-    column = classes % HB
+def bin_sums(values, row, column):
     bins = jnp.arange(HB, dtype=jnp.int32)[:, None]
     columns = (bins == column[None]).astype(jnp.bfloat16)
     total = 0.0
-    for _ in range(3):
+    for _ in range(2):
         term = values.astype(jnp.bfloat16)
         values = values - term.astype(jnp.float32)
         rows = jnp.where(bins == row[None], term[None], jnp.zeros((), jnp.bfloat16))
@@ -457,11 +471,9 @@
     own_classes = classes.reshape(-1)
     line_values = (2.0 * mixing_diffusivity) * line_sums.reshape(lines, row_count, LANES)[..., :3]
     line_values = line_values.transpose(0, 2, 1).reshape(-1)
-    codes = received[:, 6, :6, 96:120].astype(jnp.int32).reshape(lines, 2, 3, row_count)
-    line_classes = (codes[:, 0] * HB + codes[:, 1]).reshape(-1)
-    bins = bin_sums(
-        jnp.concatenate([own_values, line_values]), jnp.concatenate([own_classes, line_classes])
-    )
+    codes = received[:, 6, :6, 96:120].astype(jnp.int32).reshape(lines, 2, 3 * row_count)
+    bins = bin_sums(own_values, own_classes // HB, own_classes % HB)
+    bins = bins + bin_sums(line_values, codes[:, 0].reshape(-1), codes[:, 1].reshape(-1))
     per_bin = row_count * lines * plane_count * slab_count * depth_count // (HB * HB)
     histogram, back = all_sum(bins / per_bin, back)
 

time: 136 us -> 133 us (0.978)
  waiting for transfers between devices: 19.9 us -> 27.1 us
  local copies, waits for them, and re-layouts: 16.8 us -> 11.1 us
  other arithmetic: 8.01 us -> 6.41 us
    ppermute x3, waiting for transfers between devices: 12 us -> 19.7 us  [all_sum(): lax.ppermute(block, 'wa', [(i, i ^ move + 8 * (i % 2)) for i in range(lin...]
    concatenate x5 -> x0, local copies, waits for them, and re-layouts: 3.02 us -> none  [the longest x3 1.58 us: body(): jnp.concatenate([own_values, line_values])]
    unnamed x35 -> x33, local copies, waits for them, and re-layouts: 10.3 us -> 7.64 us
  transfers between devices with their start and end apart: 19 -> 19, of which waited for: 10 -> 10; matrix products, arithmetic and copies ran while one was open for 23% -> 17% of each run, Pallas kernels for 6% -> 6%
where the time goes in v5:
time: 133 us; the launch traced here: 132 us
  starting transfers between devices  49.4 us (37%)
  waiting for transfers between devices  27.1 us (20%)
  Pallas kernels  23.4 us (18%)
  matrix products  12.6 us (9%)
  local copies, waits for them, and re-layouts  11.1 us (8%)
  other arithmetic  6.41 us (5%)
  between operations  1.73 us (1%)
    all_to_all x2, starting transfers between devices, exchange(): lax.all_to_all(packets, 'wa', split_axis=0, concat_axis=0, tiled=True)  21.4 us
    ppermute x3, waiting for transfers between devices, all_sum(): lax.ppermute(block, 'wa', [(i, i ^ move + 8 * (i % 2)) for i in range(lin...  19.7 us
    pallas_call x1, Pallas kernels, line_terms(): pl.pallas_call(line_kernel, out_shape=(jax.ShapeDtypeStruct(received.shap...  11.9 us
    ppermute x8, starting transfers between devices, moved(): lax.ppermute(block, axis, [(i, i ^ move) for i in range(lax.axis_size(axi...  11.4 us
    unnamed x33, local copies, waits for them, and re-layouts  7.64 us
    dot_general x1, matrix products, body(): jnp.einsum('fxyj,kj->fxyk', depth_slope, matrix, preferred_element_type=j...  7.05 us
    ppermute x8, waiting for transfers between devices, moved(): lax.ppermute(block, axis, [(i, i ^ move) for i in range(lax.axis_size(axi...  5.55 us
    ppermute x1, starting transfers between devices, body(): lax.ppermute(first.astype(jnp.bfloat16), 'gx', backward).astype(jnp.float32)  4.87 us
  transfers between devices with their start and end apart: 19, of which 10 were waited for; matrix products, arithmetic and copies ran while one was open for 17% of the time, Pallas kernels for 6%

profile of v5, /device:TPU:10, one launch (start us, length us, event | category | flops | bytes accessed | tf_op | source)
XLA Modules:
  0.0 131.8 jit_solution(15434705974646316996)
XLA Ops:
  0.6 3.5 %pack.1 = bf16[64,14,8,128]{3,2,1,0:T(8,128)(2,1)} custom-call(f32[12,24,1536]{2,1,0:T(8,128)} %bitcast.44, f32[12,24,1536]{2,1,0:T(8,128)} %bitcast.37, s32[12,12,24]{2,1,0:T(8,128)} %bitcast.53), custom_call_target="tpu_custom_call" | custom-call | flops 884736 | bytes 5308416 | tf_op jit(solution)/shard_map/pack/pallas_call | solution.py:104
  4.2 12.5 %all-to-all-start = ((bf16[64,14,8,128]{3,2,1,0:T(8,128)(2,1)}), bf16[64,14,8,128]{3,2,1,0:T(8,128)(2,1)}, u32[]{:S(2)}, u32[]{:S(2)}) async-start(bf16[64,14,8,128]{3,2,1,0:T(8,128)(2,1)} %pack.1), calls=%async_computation | async-start | bytes 3670016 | tf_op jit(solution)/shard_map/all_to_all | solution.py:425
  17.6 2.1 %copy-done.15 = bf16[1536,1536]{1,0:T(8,128)(2,1)S(1)} copy-done((bf16[1536,1536]{1,0:T(8,128)(2,1)S(1)}, bf16[1536,1536]{1,0:T(8,128)(2,1)}, u32[]{:S(2)}) %copy-start.15) | copy-done | bytes 4718616
  19.7 4.1 %fusion.4.refs_6_ = bf16[2,12,24,1536]{3,2,1,0:T(8,128)(2,1)} fusion(bf16[1536,1536]{1,0:T(8,128)(2,1)S(1)} %copy-done.15, bf16[1,12,24,1536]{3,2,1,0:T(8,128)(2,1)S(1)} %get-tuple-element.49, bf16[1,12,24,1536]{3,2,1,0:T(8,128)(2,1)S(1)} %get-tuple-element.50), kind=kOutput, calls=%fused_computation.4 | convolution fusion | flops 2719678464 | bytes 8257536 | tf_op jit(solution)/shard_map/fxyj,kj->fxyk/dot_general | solution.py:433
  24.6 1.7 %dynamic-slice_bitcast_fusion = bf16[2,24,1536]{2,1,0:T(8,128)(2,1)} fusion(bf16[2,24,2,1536]{3,1,0,2:T(8,128)(2,1)} %copy.22, s32[]{:T(128)S(6)} %select_n.115), kind=kLoop, calls=%fused_computation.51 | loop fusion | bytes 294916 | tf_op jit(solution)/shard_map/jit(dynamic_index_in_dim)/squeeze | solution.py:441
  26.9 2.4 %collective-permute-start.1 = (bf16[2,24,1536]{2,1,0:T(8,128)(2,1)}, bf16[2,24,1536]{2,1,0:T(8,128)(2,1)}, u32[]{:S(2)}, u32[]{:S(2)}) collective-permute-start(bf16[2,24,1536]{2,1,0:T(8,128)(2,1)} %dynamic-slice_bitcast_fusion), channel_id=1, source_target_pairs={{0,128},{64,192},{128,0},{192,64},{1,129},{65,193},{129,1},{193,65... | collective-permute-start | bytes 442376 | tf_op jit(solution)/shard_map/ppermute | solution.py:445
  29.3 1.8 %collective-permute-start.2 = (bf16[2,24,1536]{2,1,0:T(8,128)(2,1)}, bf16[2,24,1536]{2,1,0:T(8,128)(2,1)}, u32[]{:S(2)}, u32[]{:S(2)}) collective-permute-start(bf16[2,24,1536]{2,1,0:T(8,128)(2,1)} %dynamic-slice_bitcast_fusion), channel_id=1, source_target_pairs={{0,64},{64,128},{128,192},{192,0},{1,65},{65,129},{129,193},{193,1... | collective-permute-start | bytes 442376 | tf_op jit(solution)/shard_map/ppermute | solution.py:445
  32.5 1.9 %collective-permute-start.3 = (bf16[2,24,1536]{2,1,0:T(8,128)(2,1)}, bf16[2,24,1536]{2,1,0:T(8,128)(2,1)}, u32[]{:S(2)}, u32[]{:S(2)}) collective-permute-start(bf16[2,24,1536]{2,1,0:T(8,128)(2,1)} %fusion.36), channel_id=1, source_target_pairs={{0,64},{64,128},{128,192},{1,65},{65,129},{129,193},{2,66},{66,130... | collective-permute-start | bytes 442376 | tf_op jit(solution)/shard_map/ppermute | solution.py:451
  35.1 4.9 %collective-permute-start.4 = (bf16[2,24,1536]{2,1,0:T(8,128)(2,1)}, bf16[2,24,1536]{2,1,0:T(8,128)(2,1)}, u32[]{:S(2)}, u32[]{:S(2)}) collective-permute-start(bf16[2,24,1536]{2,1,0:T(8,128)(2,1)} %pad_maximum_fusion.1), channel_id=1, source_target_pairs={{64,0},{128,64},{192,128},{65,1},{129,65},{193,129},{66,2},{130,66... | collective-permute-start | bytes 442376 | tf_op jit(solution)/shard_map/ppermute | solution.py:452
  40.0 7.1 %fusion.refs_7_ = f32[2,12,24,1536]{3,2,1,0:T(8,128)} fusion(bf16[2,12,24,1536]{3,2,1,0:T(8,128)(2,1)S(1)} %copy-done.4, bf16[1536,1536]{1,0:T(8,128)(2,1)} %matrix_ref.1), kind=kOutput, calls=%fused_computation | convolution fusion | flops 2717908992 | bytes 10027008 | tf_op jit(solution)/shard_map/fxyj,kj->fxyk/dot_general | solution.py:458
  50.2 2.0 %copy-done.2 = f32[2,12,24,1536]{3,2,1,0:T(8,128)S(1)} copy-done((f32[2,12,24,1536]{3,2,1,0:T(8,128)S(1)}, f32[2,12,24,1536]{3,2,1,0:T(8,128)}, u32[]{:S(2)}) %copy-start.2) | copy-done | bytes 3538968
  52.2 4.4 %local_terms.1 = (f32[2,12,24,1536]{3,2,1,0:T(8,128)S(1)}, f32[12,24,128]{2,1,0:T(8,128)S(1)}) custom-call(f32[12]{0:T(128)S(1)} %add_divide_fusion.fringe_ref, f32[2,24,1536]{2,1,0:T(8,128)S(1)} %get-tuple-element.43.lo_ref, f32[2,24,1536]{2,1,0:T(8,128)S(1)} %convert_select_fusion.hi_ref, f32[12,24,1536]{2,1,0:T(8,128)S(1)} %bitcast.48, ...), custom_call_target="tpu_custom_call" | custom-call | flops 26542080 | bytes 15040512 | tf_op jit(solution)/shard_map/local_terms/pallas_call | solution.py:344
  56.7 1.7 %copy-done.3 = f32[2,12,24,1536]{3,2,1,0:T(8,128)} copy-done((f32[2,12,24,1536]{3,2,1,0:T(8,128)}, f32[2,12,24,1536]{3,2,1,0:T(8,128)S(1)}, u32[]{:S(2)}) %copy-start.3) | copy-done | bytes 3538968
  59.0 1.7 %all-to-all-done.lines_ref = bf16[64,14,8,128]{3,2,1,0:T(8,128)(2,1)} async-done(((bf16[64,14,8,128]{3,2,1,0:T(8,128)(2,1)}), bf16[64,14,8,128]{3,2,1,0:T(8,128)(2,1)}, u32[]{:S(2)}, u32[]{:S(2)}) %all-to-all-start) | async-done | bytes 1835040 | tf_op jit(solution)/shard_map/all_to_all | solution.py:425
  60.7 11.9 %line_terms.1 = (bf16[64,14,8,128]{3,2,1,0:T(8,128)(2,1)}, f32[1536,128]{1,0:T(8,128)}) custom-call(bf16[64,14,8,128]{3,2,1,0:T(8,128)(2,1)} %all-to-all-done.lines_ref, bf16[1536,1536]{1,0:T(8,128)(2,1)} %matrix_ref.1), custom_call_target="tpu_custom_call" | custom-call | flops 7247757312 | bytes 8388608 | tf_op jit(solution)/shard_map/line_terms/pallas_call | solution.py:285
  72.7 8.8 %all-to-all-start.1 = ((bf16[64,14,8,128]{3,2,1,0:T(8,128)(2,1)}), bf16[64,14,8,128]{3,2,1,0:T(8,128)(2,1)S(1)}, u32[]{:S(2)}, u32[]{:S(2)}) async-start(bf16[64,14,8,128]{3,2,1,0:T(8,128)(2,1)} %get-tuple-element.34), calls=%async_computation.1 | async-start | bytes 3670016 | tf_op jit(solution)/shard_map/all_to_all | solution.py:425
  86.9 3.5 %collective-permute-start.5 = (f32[64,64]{1,0:T(8,128)S(1)}, f32[64,64]{1,0:T(8,128)S(1)}, u32[]{:S(2)}, u32[]{:S(2)}) collective-permute-start(f32[64,64]{1,0:T(8,128)S(1)} %fusion.16), channel_id=1, source_target_pairs={{0,64},{64,0},{128,192},{192,128},{1,65},{65,1},{129,193},{193,129... | collective-permute-start | bytes 49160 | tf_op jit(solution)/shard_map/ppermute | solution.py:390
  93.6 2.3 %collective-permute-start.10 = (f32[64,64]{1,0:T(8,128)S(1)}, f32[64,64]{1,0:T(8,128)S(1)}, u32[]{:S(2)}, u32[]{:S(2)}) collective-permute-start(f32[64,64]{1,0:T(8,128)S(1)} %add.106), channel_id=1, source_target_pairs={{0,32},{1,33},{2,34},{3,35},{4,36},{5,37},{6,38},{7,39},{8,40},{9,... | collective-permute-start | bytes 49160 | tf_op jit(solution)/shard_map/ppermute | solution.py:390
  95.9 2.4 %collective-permute-start.9 = (f32[64,64]{1,0:T(8,128)S(1)}, f32[64,64]{1,0:T(8,128)S(1)}, u32[]{:S(2)}, u32[]{:S(2)}) collective-permute-start(f32[64,64]{1,0:T(8,128)S(1)} %add.106), channel_id=1, source_target_pairs={{0,16},{1,17},{2,18},{3,19},{4,20},{5,21},{6,22},{7,23},{8,24},{9,... | collective-permute-start | bytes 49160 | tf_op jit(solution)/shard_map/ppermute | solution.py:390
  98.3 1.7 %collective-permute-done.10 = f32[64,64]{1,0:T(8,128)S(1)} collective-permute-done((f32[64,64]{1,0:T(8,128)S(1)}, f32[64,64]{1,0:T(8,128)S(1)}, u32[]{:S(2)}, u32[]{:S(2)}) %collective-permute-start.10) | collective-permute-done | bytes 16416 | tf_op jit(solution)/shard_map/ppermute | solution.py:390
  100.8 2.6 %collective-permute-start.14 = (f32[64,64]{1,0:T(8,128)S(1)}, f32[64,64]{1,0:T(8,128)S(1)}, u32[]{:S(2)}, u32[]{:S(2)}) collective-permute-start(f32[64,64]{1,0:T(8,128)S(1)} %add_add_fusion.1), channel_id=1, source_target_pairs={{0,4},{1,13},{2,6},{3,15},{4,0},{5,9},{6,2},{7,11},{8,12},{9,5},{1... | collective-permute-start | bytes 49160 | tf_op jit(solution)/shard_map/ppermute | solution.py:400
  106.0 19.3 %collective-permute-done.14 = f32[64,64]{1,0:T(8,128)S(1)} collective-permute-done((f32[64,64]{1,0:T(8,128)S(1)}, f32[64,64]{1,0:T(8,128)S(1)}, u32[]{:S(2)}, u32[]{:S(2)}) %collective-permute-start.14) | collective-permute-done | bytes 16416 | tf_op jit(solution)/shard_map/ppermute | solution.py:400
  125.9 1.8 %collective-permute-start.16 = (f32[64,64]{1,0:T(8,128)S(1)}, f32[64,64]{1,0:T(8,128)S(1)}, u32[]{:S(2)}, u32[]{:S(2)}) collective-permute-start(f32[64,64]{1,0:T(8,128)S(1)} %add_add_fusion), channel_id=1, source_target_pairs={{0,1},{1,0},{2,3},{3,2},{4,5},{5,4},{6,7},{7,6},{8,9},{9,8},{10,11... | collective-permute-start | bytes 49160 | tf_op jit(solution)/shard_map/ppermute | solution.py:390
  127.7 3.6 %unpack_add.1 = (f32[12,24,1536]{2,1,0:T(8,128)}, f32[12,24,1536]{2,1,0:T(8,128)}) custom-call(f32[2,12,24,1536]{3,2,1,0:T(8,128)} %copy-done.3, bf16[64,14,8,128]{3,2,1,0:T(8,128)(2,1)S(1)} %all-to-all-done.1.ret_ref), custom_call_target="tpu_custom_call" | custom-call | flops 1769472 | bytes 8847360 | tf_op jit(solution)/shard_map/unpack_add/pallas_call | solution.py:169
  (91 shorter events, 20.4 us)
Async XLA Ops:
  4.2 13.2 %copy-start = (f32[24,12,1536]{2,0,1:T(8,128)S(1)}, f32[24,12,1536]{2,0,1:T(8,128)}, u32[]{:S(2)}) copy-start(f32[24,12,1536]{2,0,1:T(8,128)} %param.10) | copy-start | bytes 5308420
  4.2 13.2 %copy-start.1 = (f32[24,12,1536]{2,0,1:T(8,128)S(1)}, f32[24,12,1536]{2,0,1:T(8,128)}, u32[]{:S(2)}) copy-start(f32[24,12,1536]{2,0,1:T(8,128)} %param.9) | copy-start | bytes 5308420
  4.2 56.6 %all-to-all-start = ((bf16[64,14,8,128]{3,2,1,0:T(8,128)(2,1)}), bf16[64,14,8,128]{3,2,1,0:T(8,128)(2,1)}, u32[]{:S(2)}, u32[]{:S(2)}) async-start(bf16[64,14,8,128]{3,2,1,0:T(8,128)(2,1)} %pack.1), calls=%async_computation | async-start | bytes 3670016 | tf_op jit(solution)/shard_map/all_to_all | solution.py:425
  24.6 15.4 %copy-start.4 = (bf16[2,12,24,1536]{3,2,1,0:T(8,128)(2,1)S(1)}, bf16[2,12,24,1536]{3,2,1,0:T(8,128)(2,1)}, u32[]{:S(2)}) copy-start(bf16[2,12,24,1536]{3,2,1,0:T(8,128)(2,1)} %fusion.4.refs_6_) | copy-start | bytes 5308420
  26.3 22.6 %collective-permute-start = (bf16[2,24,1536]{2,1,0:T(8,128)(2,1)}, bf16[2,24,1536]{2,1,0:T(8,128)(2,1)}, u32[]{:S(2)}, u32[]{:S(2)}) collective-permute-start(bf16[2,24,1536]{2,1,0:T(8,128)(2,1)} %dynamic-slice_bitcast_fusion), channel_id=1, source_target_pairs={{0,192},{64,0},{128,64},{192,128},{1,193},{65,1},{129,65},{193,129... | collective-permute-start | bytes 442376 | tf_op jit(solution)/shard_map/ppermute | solution.py:445
  26.9 22.1 %collective-permute-start.1 = (bf16[2,24,1536]{2,1,0:T(8,128)(2,1)}, bf16[2,24,1536]{2,1,0:T(8,128)(2,1)}, u32[]{:S(2)}, u32[]{:S(2)}) collective-permute-start(bf16[2,24,1536]{2,1,0:T(8,128)(2,1)} %dynamic-slice_bitcast_fusion), channel_id=1, source_target_pairs={{0,128},{64,192},{128,0},{192,64},{1,129},{65,193},{129,1},{193,65... | collective-permute-start | bytes 442376 | tf_op jit(solution)/shard_map/ppermute | solution.py:445
  29.3 19.7 %collective-permute-start.2 = (bf16[2,24,1536]{2,1,0:T(8,128)(2,1)}, bf16[2,24,1536]{2,1,0:T(8,128)(2,1)}, u32[]{:S(2)}, u32[]{:S(2)}) collective-permute-start(bf16[2,24,1536]{2,1,0:T(8,128)(2,1)} %dynamic-slice_bitcast_fusion), channel_id=1, source_target_pairs={{0,64},{64,128},{128,192},{192,0},{1,65},{65,129},{129,193},{193,1... | collective-permute-start | bytes 442376 | tf_op jit(solution)/shard_map/ppermute | solution.py:445
  32.5 16.5 %collective-permute-start.3 = (bf16[2,24,1536]{2,1,0:T(8,128)(2,1)}, bf16[2,24,1536]{2,1,0:T(8,128)(2,1)}, u32[]{:S(2)}, u32[]{:S(2)}) collective-permute-start(bf16[2,24,1536]{2,1,0:T(8,128)(2,1)} %fusion.36), channel_id=1, source_target_pairs={{0,64},{64,128},{128,192},{1,65},{65,129},{129,193},{2,66},{66,130... | collective-permute-start | bytes 442376 | tf_op jit(solution)/shard_map/ppermute | solution.py:451
  35.1 11.9 %copy-start.14 = (s32[24,1536]{1,0:T(8,128)S(1)}, s32[24,1536]{1,0:T(8,128)}, u32[]{:S(2)}) copy-start(s32[24,1536]{1,0:T(8,128)} %param.14) | copy-start | bytes 442372
  35.1 12.6 %collective-permute-start.4 = (bf16[2,24,1536]{2,1,0:T(8,128)(2,1)}, bf16[2,24,1536]{2,1,0:T(8,128)(2,1)}, u32[]{:S(2)}, u32[]{:S(2)}) collective-permute-start(bf16[2,24,1536]{2,1,0:T(8,128)(2,1)} %pad_maximum_fusion.1), channel_id=1, source_target_pairs={{64,0},{128,64},{192,128},{65,1},{129,65},{193,129},{66,2},{130,66... | collective-permute-start | bytes 442376 | tf_op jit(solution)/shard_map/ppermute | solution.py:452
  72.7 9.0 %copy-start.7 = (f32[12,24,128]{2,1,0:T(8,128)S(1)}, f32[12,24,128]{2,1,0:T(8,128)}, u32[]{:S(2)}) copy-start(f32[12,24,128]{2,1,0:T(8,128)} %copy-done.6) | copy-start | bytes 442372
  72.7 53.2 %all-to-all-start.1 = ((bf16[64,14,8,128]{3,2,1,0:T(8,128)(2,1)}), bf16[64,14,8,128]{3,2,1,0:T(8,128)(2,1)S(1)}, u32[]{:S(2)}, u32[]{:S(2)}) async-start(bf16[64,14,8,128]{3,2,1,0:T(8,128)(2,1)} %get-tuple-element.34), calls=%async_computation.1 | async-start | bytes 3670016 | tf_op jit(solution)/shard_map/all_to_all | solution.py:425
  85.6 5.6 %collective-permute-start.6 = (f32[64,64]{1,0:T(8,128)S(1)}, f32[64,64]{1,0:T(8,128)S(1)}, u32[]{:S(2)}, u32[]{:S(2)}) collective-permute-start(f32[64,64]{1,0:T(8,128)S(1)} %fusion.16), channel_id=1, source_target_pairs={{0,128},{64,192},{128,0},{192,64},{1,129},{65,193},{129,1},{193,65... | collective-permute-start | bytes 49160 | tf_op jit(solution)/shard_map/ppermute | solution.py:390
  86.9 4.4 %collective-permute-start.7 = (f32[64,64]{1,0:T(8,128)S(1)}, f32[64,64]{1,0:T(8,128)S(1)}, u32[]{:S(2)}, u32[]{:S(2)}) collective-permute-start(f32[64,64]{1,0:T(8,128)S(1)} %fusion.16), channel_id=1, source_target_pairs={{0,192},{64,128},{128,64},{192,0},{1,193},{65,129},{129,65},{193,1... | collective-permute-start | bytes 49160 | tf_op jit(solution)/shard_map/ppermute | solution.py:390
  86.9 5.4 %collective-permute-start.5 = (f32[64,64]{1,0:T(8,128)S(1)}, f32[64,64]{1,0:T(8,128)S(1)}, u32[]{:S(2)}, u32[]{:S(2)}) collective-permute-start(f32[64,64]{1,0:T(8,128)S(1)} %fusion.16), channel_id=1, source_target_pairs={{0,64},{64,0},{128,192},{192,128},{1,65},{65,1},{129,193},{193,129... | collective-permute-start | bytes 49160 | tf_op jit(solution)/shard_map/ppermute | solution.py:390
  92.3 1.3 collective-permute-start.8
  93.6 6.4 %collective-permute-start.10 = (f32[64,64]{1,0:T(8,128)S(1)}, f32[64,64]{1,0:T(8,128)S(1)}, u32[]{:S(2)}, u32[]{:S(2)}) collective-permute-start(f32[64,64]{1,0:T(8,128)S(1)} %add.106), channel_id=1, source_target_pairs={{0,32},{1,33},{2,34},{3,35},{4,36},{5,37},{6,38},{7,39},{8,40},{9,... | collective-permute-start | bytes 49160 | tf_op jit(solution)/shard_map/ppermute | solution.py:390
  95.9 4.7 %collective-permute-start.11 = (f32[64,64]{1,0:T(8,128)S(1)}, f32[64,64]{1,0:T(8,128)S(1)}, u32[]{:S(2)}, u32[]{:S(2)}) collective-permute-start(f32[64,64]{1,0:T(8,128)S(1)} %add.106), channel_id=1, source_target_pairs={{0,48},{1,49},{2,50},{3,51},{4,52},{5,53},{6,54},{7,55},{8,56},{9,... | collective-permute-start | bytes 49160 | tf_op jit(solution)/shard_map/ppermute | solution.py:390
  95.9 4.9 %collective-permute-start.9 = (f32[64,64]{1,0:T(8,128)S(1)}, f32[64,64]{1,0:T(8,128)S(1)}, u32[]{:S(2)}, u32[]{:S(2)}) collective-permute-start(f32[64,64]{1,0:T(8,128)S(1)} %add.106), channel_id=1, source_target_pairs={{0,16},{1,17},{2,18},{3,19},{4,20},{5,21},{6,22},{7,23},{8,24},{9,... | collective-permute-start | bytes 49160 | tf_op jit(solution)/shard_map/ppermute | solution.py:390
  100.8 24.4 %collective-permute-start.14 = (f32[64,64]{1,0:T(8,128)S(1)}, f32[64,64]{1,0:T(8,128)S(1)}, u32[]{:S(2)}, u32[]{:S(2)}) collective-permute-start(f32[64,64]{1,0:T(8,128)S(1)} %add_add_fusion.1), channel_id=1, source_target_pairs={{0,4},{1,13},{2,6},{3,15},{4,0},{5,9},{6,2},{7,11},{8,12},{9,5},{1... | collective-permute-start | bytes 49160 | tf_op jit(solution)/shard_map/ppermute | solution.py:400
  103.4 21.8 %collective-permute-start.15 = (f32[64,64]{1,0:T(8,128)S(1)}, f32[64,64]{1,0:T(8,128)S(1)}, u32[]{:S(2)}, u32[]{:S(2)}) collective-permute-start(f32[64,64]{1,0:T(8,128)S(1)} %add_add_fusion.1), channel_id=1, source_target_pairs={{0,6},{1,15},{2,4},{3,13},{4,2},{5,11},{6,0},{7,9},{8,14},{9,7},{1... | collective-permute-start | bytes 49160 | tf_op jit(solution)/shard_map/ppermute | solution.py:400
  105.0 20.6 %collective-permute-start.13 = (f32[64,64]{1,0:T(8,128)S(1)}, f32[64,64]{1,0:T(8,128)S(1)}, u32[]{:S(2)}, u32[]{:S(2)}) collective-permute-start(f32[64,64]{1,0:T(8,128)S(1)} %add_add_fusion.1), channel_id=1, source_target_pairs={{0,2},{1,11},{2,0},{3,9},{4,6},{5,15},{6,4},{7,13},{8,10},{9,3},{1... | collective-permute-start | bytes 49160 | tf_op jit(solution)/shard_map/ppermute | solution.py:400
  105.3 20.4 %collective-permute-start.12 = (f32[64,64]{1,0:T(8,128)S(1)}, f32[64,64]{1,0:T(8,128)S(1)}, u32[]{:S(2)}, u32[]{:S(2)}) collective-permute-start(f32[64,64]{1,0:T(8,128)S(1)} %add_add_fusion.1), channel_id=1, source_target_pairs={{1,9},{3,11},{5,13},{7,15},{9,1},{11,3},{13,5},{15,7},{17,25},{19,... | collective-permute-start | bytes 49160 | tf_op jit(solution)/shard_map/ppermute | solution.py:398
  125.9 5.4 %collective-permute-start.16 = (f32[64,64]{1,0:T(8,128)S(1)}, f32[64,64]{1,0:T(8,128)S(1)}, u32[]{:S(2)}, u32[]{:S(2)}) collective-permute-start(f32[64,64]{1,0:T(8,128)S(1)} %add_add_fusion), channel_id=1, source_target_pairs={{0,1},{1,0},{2,3},{3,2},{4,5},{5,4},{6,7},{7,6},{8,9},{9,8},{10,11... | collective-permute-start | bytes 49160 | tf_op jit(solution)/shard_map/ppermute | solution.py:390
  (11 other events, 28.0 us)

commit v6 on v5

--- a/solution.py
+++ b/solution.py
@@ -118,7 +118,7 @@
     )(x0, x1, classes)
 
 
-def unpack_add_kernel(parts_ref, ret_ref, out0_ref, out1_ref):
+def unpack_add_kernel(scale, parts_ref, ret_ref, out_ref):
     step = pl.program_id(0)
     steps = pl.num_programs(0)
     lines = ret_ref.shape[0]
@@ -127,21 +127,16 @@
     left = per_plane * PACK_PLANES - (2 * lines - per_plane * PACK_PLANES * (steps - 1))
     first_left = per_plane * PACK_PLANES - left
     group = lane_group((ROWS, LANES))
-    fields = (
-        (out0_ref, phase_step * mixing_diffusivity),
-        (out1_ref, phase_step),
-    )
 
     def add_pairs(count):
         for pair in range(count):
             p, k = pair // pairs, (pair % pairs) * 2 * ZBLK
             line = step * (PACK_PLANES * pairs) + pair
-            for f, (out_ref, scale) in enumerate(fields):
-                for b in range(2):
-                    for t in range(3):
-                        at = (p, slice(ROWS * t, ROWS * t + ROWS), slice(k + b * ZBLK, k + (b + 1) * ZBLK))
-                        tile = ret_ref[line, 7 * f + 3 * b + t].astype(jnp.float32)
-                        out_ref[at] = parts_ref[(f, *at)] + scale * tile
+            for b in range(2):
+                for t in range(3):
+                    at = (p, slice(ROWS * t, ROWS * t + ROWS), slice(k + b * ZBLK, k + (b + 1) * ZBLK))
+                    tile = ret_ref[line, 3 * b + t].astype(jnp.float32)
+                    out_ref[at] = parts_ref[(0, *at)] + scale * tile
 
     @pl.when(step < steps - 1)
     def _():
@@ -153,30 +148,29 @@
         for m in range(left):
             block = first_left + m
             p, k = block // per_plane, (block % per_plane) * ZBLK
-            for f, (out_ref, scale) in enumerate(fields):
-                quarters = [ret_ref[4 * m + q, 7 * f + 6].astype(jnp.float32) for q in range(4)]
-                for g in range(3):
-                    tile = rolled(quarters[0], -32 * g)
-                    for q in range(1, 4):
-                        tile = jnp.where(group == q, rolled(quarters[q], 32 * (q - g)), tile)
-                    at = (p, slice(ROWS * g, ROWS * g + ROWS), slice(k, k + ZBLK))
-                    out_ref[at] = parts_ref[(f, *at)] + scale * tile
-
-
-def unpack_add(parts, returned):
+            quarters = [ret_ref[4 * m + q, 6].astype(jnp.float32) for q in range(4)]
+            for g in range(3):
+                tile = rolled(quarters[0], -32 * g)
+                for q in range(1, 4):
+                    tile = jnp.where(group == q, rolled(quarters[q], 32 * (q - g)), tile)
+                at = (p, slice(ROWS * g, ROWS * g + ROWS), slice(k, k + ZBLK))
+                out_ref[at] = parts_ref[(0, *at)] + scale * tile
+
+
+def unpack_add(parts, returned, field, scale):
     _, planes, rows, depth = parts.shape
-    part = pl.BlockSpec((PACK_PLANES, rows, depth), lambda i: (i, 0, 0))
+    lines = returned.shape[0]
     return pl.pallas_call(
-        unpack_add_kernel,
+        functools.partial(unpack_add_kernel, scale),
         grid=(planes // PACK_PLANES,),
         in_specs=[
-            pl.BlockSpec((2, PACK_PLANES, rows, depth), lambda i: (0, i, 0, 0)),
-            pl.BlockSpec(returned.shape, lambda i: (0, 0, 0, 0)),
-        ],
-        out_specs=[part, part],
-        out_shape=[jax.ShapeDtypeStruct(parts.shape[1:], jnp.float32)] * 2,
+            pl.BlockSpec((1, PACK_PLANES, rows, depth), lambda i: (field, i, 0, 0)),
+            pl.BlockSpec((lines, 7, ROWS, LANES), lambda i: (0, field, 0, 0)),
+        ],
+        out_specs=pl.BlockSpec((PACK_PLANES, rows, depth), lambda i: (i, 0, 0)),
+        out_shape=jax.ShapeDtypeStruct(parts.shape[1:], jnp.float32),
         compiler_params=pltpu.CompilerParams(vmem_limit_bytes=UNPACK_VMEM_LIMIT),
-        cost_estimate=pl.CostEstimate(flops=2 * parts.size, bytes_accessed=10 * parts.size, transcendentals=0),
+        cost_estimate=pl.CostEstimate(flops=parts.size, bytes_accessed=5 * parts.size, transcendentals=0),
         name="unpack_add",
     )(parts, returned)
 
@@ -385,7 +379,7 @@
     return total
 
 
-def all_sum(block, last_after):
+def all_sum(block, finish, back):
     def moved(axis, move):
         return lax.ppermute(block, axis, [(i, i ^ move) for i in range(lax.axis_size(axis))])
 
@@ -396,11 +390,14 @@
             block = block + moved("wa", 1)
     lines = lax.axis_size("wa")
     across = lax.ppermute(block, "wa", [(i, i ^ 8) for i in range(lines) if i % 2 == 1])
+    arrived = [lax.ppermute(block, "wa", [(i, i ^ (move + 8 * (i % 2))) for i in range(lines)]) for move in (2, 4, 6)]
+    mixture_next = finish(back, 0, phase_step * mixing_diffusivity)
+    mixture_next, across, arrived = lax.optimization_barrier((mixture_next, across, arrived))
     near = jnp.where(lax.axis_index("wa") % 2 == 1, across, block)
-    arrived = [lax.ppermute(block, "wa", [(i, i ^ (move + 8 * (i % 2))) for i in range(lines)]) for move in (2, 4, 6)]
     block = (near + arrived[0]) + (arrived[1] + arrived[2])
-    block, last_after = lax.optimization_barrier((block, last_after))
-    return block + moved("wa", 1), last_after
+    block, back = lax.optimization_barrier((block, back))
+    temperature_next = finish(back, 1, phase_step)
+    return block + moved("wa", 1), mixture_next, temperature_next
 
 
 def body(
@@ -475,9 +472,9 @@
     bins = bin_sums(own_values, own_classes // HB, own_classes % HB)
     bins = bins + bin_sums(line_values, codes[:, 0].reshape(-1), codes[:, 1].reshape(-1))
     per_bin = row_count * lines * plane_count * slab_count * depth_count // (HB * HB)
-    histogram, back = all_sum(bins / per_bin, back)
-
-    mixture_next, temperature_next = unpack_add(parts, back)
+    finish = functools.partial(unpack_add, parts)
+    histogram, mixture_next, temperature_next = all_sum(bins / per_bin, finish, back)
+
     return (jnp.transpose(mixture_next, (1, 0, 2)), jnp.transpose(temperature_next, (1, 0, 2)), histogram)
 
 

time: 133 us -> 135 us (1.015)
  Pallas kernels: 23.4 us -> 25.1 us
    ppermute x3, waiting for transfers between devices: 19.7 us -> 0.01 us  [all_sum(): lax.ppermute(block, 'wa', [(i, i ^ move + 8 * (i % 2)) for i in range(lin...]
    all_to_all x2, waiting for transfers between devices: 1.82 us -> 21.2 us  [exchange(): lax.all_to_all(packets, 'wa', split_axis=0, concat_axis=0, tiled=True)]
    pallas_call x1 -> x2, Pallas kernels: 3.55 us -> 5.16 us  [unpack_add(): pl.pallas_call(functools.partial(unpack_add_kernel, scale), grid=(planes...]
  transfers between devices with their start and end apart: 19 -> 19, of which waited for: 10 -> 8; matrix products, arithmetic and copies ran while one was open for 17% -> 17% of each run, Pallas kernels for 6% -> 7%
where the time goes in v6:
time: 135 us; the launch traced here: 133 us
  starting transfers between devices  49.1 us (36%)
  waiting for transfers between devices  26.8 us (20%)
  Pallas kernels  25.1 us (19%)
  matrix products  12.7 us (9%)
  local copies, waits for them, and re-layouts  11.1 us (8%)
  other arithmetic  6.43 us (5%)
  between operations  1.73 us (1%)
    all_to_all x2, starting transfers between devices, exchange(): lax.all_to_all(packets, 'wa', split_axis=0, concat_axis=0, tiled=True)  21.3 us
    all_to_all x2, waiting for transfers between devices, exchange(): lax.all_to_all(packets, 'wa', split_axis=0, concat_axis=0, tiled=True)  21.2 us
    pallas_call x1, Pallas kernels, line_terms(): pl.pallas_call(line_kernel, out_shape=(jax.ShapeDtypeStruct(received.shap...  11.9 us
    ppermute x8, starting transfers between devices, moved(): lax.ppermute(block, axis, [(i, i ^ move) for i in range(lax.axis_size(axi...  11.1 us
    unnamed x33, local copies, waits for them, and re-layouts  7.63 us
    dot_general x1, matrix products, body(): jnp.einsum('fxyj,kj->fxyk', depth_slope, matrix, preferred_element_type=j...  7.06 us
    ppermute x8, waiting for transfers between devices, moved(): lax.ppermute(block, axis, [(i, i ^ move) for i in range(lax.axis_size(axi...  5.56 us
    pallas_call x2, Pallas kernels, unpack_add(): pl.pallas_call(functools.partial(unpack_add_kernel, scale), grid=(planes...  5.16 us
  transfers between devices with their start and end apart: 19, of which 8 were waited for; matrix products, arithmetic and copies ran while one was open for 17% of the time, Pallas kernels for 7%

profile of v6, /device:TPU:10, one launch (start us, length us, event | category | flops | bytes accessed | tf_op | source)
XLA Modules:
  0.0 132.9 jit_solution(829895181974336855)
XLA Ops:
  0.6 3.5 %pack.1 = bf16[64,14,8,128]{3,2,1,0:T(8,128)(2,1)} custom-call(f32[12,24,1536]{2,1,0:T(8,128)} %bitcast.44, f32[12,24,1536]{2,1,0:T(8,128)} %bitcast.37, s32[12,12,24]{2,1,0:T(8,128)} %bitcast.55), custom_call_target="tpu_custom_call" | custom-call | flops 884736 | bytes 5308416 | tf_op jit(solution)/shard_map/pack/pallas_call | solution.py:104
  4.2 12.5 %all-to-all-start = ((bf16[64,14,8,128]{3,2,1,0:T(8,128)(2,1)}), bf16[64,14,8,128]{3,2,1,0:T(8,128)(2,1)}, u32[]{:S(2)}, u32[]{:S(2)}) async-start(bf16[64,14,8,128]{3,2,1,0:T(8,128)(2,1)} %pack.1), calls=%async_computation | async-start | bytes 3670016 | tf_op jit(solution)/shard_map/all_to_all | solution.py:422
  17.6 2.1 %copy-done.15 = bf16[1536,1536]{1,0:T(8,128)(2,1)S(1)} copy-done((bf16[1536,1536]{1,0:T(8,128)(2,1)S(1)}, bf16[1536,1536]{1,0:T(8,128)(2,1)}, u32[]{:S(2)}) %copy-start.15) | copy-done | bytes 4718616
  19.7 4.1 %fusion.4.refs_6_ = bf16[2,12,24,1536]{3,2,1,0:T(8,128)(2,1)} fusion(bf16[1536,1536]{1,0:T(8,128)(2,1)S(1)} %copy-done.15, bf16[1,12,24,1536]{3,2,1,0:T(8,128)(2,1)S(1)} %get-tuple-element.55, bf16[1,12,24,1536]{3,2,1,0:T(8,128)(2,1)S(1)} %get-tuple-element.56), kind=kOutput, calls=%fused_computation.4 | convolution fusion | flops 2719678464 | bytes 8257536 | tf_op jit(solution)/shard_map/fxyj,kj->fxyk/dot_general | solution.py:430
  24.6 1.7 %dynamic-slice_bitcast_fusion = bf16[2,24,1536]{2,1,0:T(8,128)(2,1)} fusion(bf16[2,24,2,1536]{3,1,0,2:T(8,128)(2,1)} %copy.22, s32[]{:T(128)S(6)} %select_n.115), kind=kLoop, calls=%fused_computation.51 | loop fusion | bytes 294916 | tf_op jit(solution)/shard_map/jit(dynamic_index_in_dim)/squeeze | solution.py:438
  26.9 2.4 %collective-permute-start.1 = (bf16[2,24,1536]{2,1,0:T(8,128)(2,1)}, bf16[2,24,1536]{2,1,0:T(8,128)(2,1)}, u32[]{:S(2)}, u32[]{:S(2)}) collective-permute-start(bf16[2,24,1536]{2,1,0:T(8,128)(2,1)} %dynamic-slice_bitcast_fusion), channel_id=1, source_target_pairs={{0,128},{64,192},{128,0},{192,64},{1,129},{65,193},{129,1},{193,65... | collective-permute-start | bytes 442376 | tf_op jit(solution)/shard_map/ppermute | solution.py:442
  29.3 1.8 %collective-permute-start.2 = (bf16[2,24,1536]{2,1,0:T(8,128)(2,1)}, bf16[2,24,1536]{2,1,0:T(8,128)(2,1)}, u32[]{:S(2)}, u32[]{:S(2)}) collective-permute-start(bf16[2,24,1536]{2,1,0:T(8,128)(2,1)} %dynamic-slice_bitcast_fusion), channel_id=1, source_target_pairs={{0,64},{64,128},{128,192},{192,0},{1,65},{65,129},{129,193},{193,1... | collective-permute-start | bytes 442376 | tf_op jit(solution)/shard_map/ppermute | solution.py:442
  32.5 1.9 %collective-permute-start.3 = (bf16[2,24,1536]{2,1,0:T(8,128)(2,1)}, bf16[2,24,1536]{2,1,0:T(8,128)(2,1)}, u32[]{:S(2)}, u32[]{:S(2)}) collective-permute-start(bf16[2,24,1536]{2,1,0:T(8,128)(2,1)} %fusion.36), channel_id=1, source_target_pairs={{0,64},{64,128},{128,192},{1,65},{65,129},{129,193},{2,66},{66,130... | collective-permute-start | bytes 442376 | tf_op jit(solution)/shard_map/ppermute | solution.py:448
  35.1 4.9 %collective-permute-start.4 = (bf16[2,24,1536]{2,1,0:T(8,128)(2,1)}, bf16[2,24,1536]{2,1,0:T(8,128)(2,1)}, u32[]{:S(2)}, u32[]{:S(2)}) collective-permute-start(bf16[2,24,1536]{2,1,0:T(8,128)(2,1)} %pad_maximum_fusion.1), channel_id=1, source_target_pairs={{64,0},{128,64},{192,128},{65,1},{129,65},{193,129},{66,2},{130,66... | collective-permute-start | bytes 442376 | tf_op jit(solution)/shard_map/ppermute | solution.py:449
  40.0 7.1 %fusion.refs_7_ = f32[2,12,24,1536]{3,2,1,0:T(8,128)} fusion(bf16[2,12,24,1536]{3,2,1,0:T(8,128)(2,1)S(1)} %copy-done.4, bf16[1536,1536]{1,0:T(8,128)(2,1)} %matrix_ref.1), kind=kOutput, calls=%fused_computation | convolution fusion | flops 2717908992 | bytes 10027008 | tf_op jit(solution)/shard_map/fxyj,kj->fxyk/dot_general | solution.py:455
  50.2 2.0 %copy-done.3 = f32[2,12,24,1536]{3,2,1,0:T(8,128)S(1)} copy-done((f32[2,12,24,1536]{3,2,1,0:T(8,128)S(1)}, f32[2,12,24,1536]{3,2,1,0:T(8,128)}, u32[]{:S(2)}) %copy-start.3) | copy-done | bytes 3538968
  52.2 4.4 %local_terms.1 = (f32[2,12,24,1536]{3,2,1,0:T(8,128)S(1)}, f32[12,24,128]{2,1,0:T(8,128)S(1)}) custom-call(f32[12]{0:T(128)S(1)} %add_divide_fusion.fringe_ref, f32[2,24,1536]{2,1,0:T(8,128)S(1)} %get-tuple-element.49.lo_ref, f32[2,24,1536]{2,1,0:T(8,128)S(1)} %convert_select_fusion.hi_ref, f32[12,24,1536]{2,1,0:T(8,128)S(1)} %bitcast.48, ...), custom_call_target="tpu_custom_call" | custom-call | flops 26542080 | bytes 15040512 | tf_op jit(solution)/shard_map/local_terms/pallas_call | solution.py:338
  56.7 1.7 %copy-done.2 = f32[2,12,24,1536]{3,2,1,0:T(8,128)} copy-done((f32[2,12,24,1536]{3,2,1,0:T(8,128)}, f32[2,12,24,1536]{3,2,1,0:T(8,128)S(1)}, u32[]{:S(2)}) %copy-start.2) | copy-done | bytes 3538968
  60.7 11.9 %line_terms.1 = (bf16[64,14,8,128]{3,2,1,0:T(8,128)(2,1)}, f32[1536,128]{1,0:T(8,128)}) custom-call(bf16[64,14,8,128]{3,2,1,0:T(8,128)(2,1)} %all-to-all-done.lines_ref, bf16[1536,1536]{1,0:T(8,128)(2,1)} %matrix_ref.1), custom_call_target="tpu_custom_call" | custom-call | flops 7247757312 | bytes 8388608 | tf_op jit(solution)/shard_map/line_terms/pallas_call | solution.py:279
  72.7 8.8 %all-to-all-start.1 = ((bf16[64,14,8,128]{3,2,1,0:T(8,128)(2,1)}), bf16[64,14,8,128]{3,2,1,0:T(8,128)(2,1)S(1)}, u32[]{:S(2)}, u32[]{:S(2)}) async-start(bf16[64,14,8,128]{3,2,1,0:T(8,128)(2,1)} %get-tuple-element.35), calls=%async_computation.1 | async-start | bytes 3670016 | tf_op jit(solution)/shard_map/all_to_all | solution.py:422
  86.9 3.5 %collective-permute-start.5 = (f32[64,64]{1,0:T(8,128)S(1)}, f32[64,64]{1,0:T(8,128)S(1)}, u32[]{:S(2)}, u32[]{:S(2)}) collective-permute-start(f32[64,64]{1,0:T(8,128)S(1)} %fusion.16), channel_id=1, source_target_pairs={{0,64},{64,0},{128,192},{192,128},{1,65},{65,1},{129,193},{193,129... | collective-permute-start | bytes 49160 | tf_op jit(solution)/shard_map/ppermute | solution.py:384
  93.7 2.3 %collective-permute-start.10 = (f32[64,64]{1,0:T(8,128)S(1)}, f32[64,64]{1,0:T(8,128)S(1)}, u32[]{:S(2)}, u32[]{:S(2)}) collective-permute-start(f32[64,64]{1,0:T(8,128)S(1)} %add.105), channel_id=1, source_target_pairs={{0,32},{1,33},{2,34},{3,35},{4,36},{5,37},{6,38},{7,39},{8,40},{9,... | collective-permute-start | bytes 49160 | tf_op jit(solution)/shard_map/ppermute | solution.py:384
  95.9 2.4 %collective-permute-start.9 = (f32[64,64]{1,0:T(8,128)S(1)}, f32[64,64]{1,0:T(8,128)S(1)}, u32[]{:S(2)}, u32[]{:S(2)}) collective-permute-start(f32[64,64]{1,0:T(8,128)S(1)} %add.105), channel_id=1, source_target_pairs={{0,16},{1,17},{2,18},{3,19},{4,20},{5,21},{6,22},{7,23},{8,24},{9,... | collective-permute-start | bytes 49160 | tf_op jit(solution)/shard_map/ppermute | solution.py:384
  98.4 1.7 %collective-permute-done.10 = f32[64,64]{1,0:T(8,128)S(1)} collective-permute-done((f32[64,64]{1,0:T(8,128)S(1)}, f32[64,64]{1,0:T(8,128)S(1)}, u32[]{:S(2)}, u32[]{:S(2)}) %collective-permute-start.10) | collective-permute-done | bytes 16416 | tf_op jit(solution)/shard_map/ppermute | solution.py:384
  101.5 1.8 %collective-permute-start.13 = (f32[64,64]{1,0:T(8,128)S(1)}, f32[64,64]{1,0:T(8,128)S(1)}, u32[]{:S(2)}, u32[]{:S(2)}) collective-permute-start(f32[64,64]{1,0:T(8,128)S(1)} %add_add_fusion.1), channel_id=1, source_target_pairs={{0,2},{1,11},{2,0},{3,9},{4,6},{5,15},{6,4},{7,13},{8,10},{9,3},{1... | collective-permute-start | bytes 49160 | tf_op jit(solution)/shard_map/ppermute | solution.py:393
  103.4 2.6 %collective-permute-start.14 = (f32[64,64]{1,0:T(8,128)S(1)}, f32[64,64]{1,0:T(8,128)S(1)}, u32[]{:S(2)}, u32[]{:S(2)}) collective-permute-start(f32[64,64]{1,0:T(8,128)S(1)} %add_add_fusion.1), channel_id=1, source_target_pairs={{0,4},{1,13},{2,6},{3,15},{4,0},{5,9},{6,2},{7,11},{8,12},{9,5},{1... | collective-permute-start | bytes 49160 | tf_op jit(solution)/shard_map/ppermute | solution.py:393
  106.0 19.6 %all-to-all-done.1.ret_ref = bf16[64,14,8,128]{3,2,1,0:T(8,128)(2,1)S(1)} async-done(((bf16[64,14,8,128]{3,2,1,0:T(8,128)(2,1)}), bf16[64,14,8,128]{3,2,1,0:T(8,128)(2,1)S(1)}, u32[]{:S(2)}, u32[]{:S(2)}) %all-to-all-start.1) | async-done | bytes 1835040 | tf_op jit(solution)/shard_map/all_to_all | solution.py:422
  125.6 2.6 %unpack_add.2 = f32[12,24,1536]{2,1,0:T(8,128)} custom-call(f32[2,12,24,1536]{3,2,1,0:T(8,128)} %copy-done.2, bf16[64,14,8,128]{3,2,1,0:T(8,128)(2,1)S(1)} %all-to-all-done.1.ret_ref), custom_call_target="tpu_custom_call" | custom-call | flops 884736 | bytes 4423680 | tf_op jit(solution)/shard_map/unpack_add/pallas_call | solution.py:163
  129.7 2.6 %unpack_add.3 = f32[12,24,1536]{2,1,0:T(8,128)} custom-call(f32[2,12,24,1536]{3,2,1,0:T(8,128)} %copy-done.2, bf16[64,14,8,128]{3,2,1,0:T(8,128)(2,1)S(1)} %all-to-all-done.1.ret_ref), custom_call_target="tpu_custom_call" | custom-call | flops 884736 | bytes 4423680 | tf_op jit(solution)/shard_map/unpack_add/pallas_call | solution.py:163
  (92 shorter events, 21.0 us)
Async XLA Ops:
  4.2 13.2 %copy-start = (f32[24,12,1536]{2,0,1:T(8,128)S(1)}, f32[24,12,1536]{2,0,1:T(8,128)}, u32[]{:S(2)}) copy-start(f32[24,12,1536]{2,0,1:T(8,128)} %param.10) | copy-start | bytes 5308420
  4.2 13.2 %copy-start.1 = (f32[24,12,1536]{2,0,1:T(8,128)S(1)}, f32[24,12,1536]{2,0,1:T(8,128)}, u32[]{:S(2)}) copy-start(f32[24,12,1536]{2,0,1:T(8,128)} %param.9) | copy-start | bytes 5308420
  4.2 56.6 %all-to-all-start = ((bf16[64,14,8,128]{3,2,1,0:T(8,128)(2,1)}), bf16[64,14,8,128]{3,2,1,0:T(8,128)(2,1)}, u32[]{:S(2)}, u32[]{:S(2)}) async-start(bf16[64,14,8,128]{3,2,1,0:T(8,128)(2,1)} %pack.1), calls=%async_computation | async-start | bytes 3670016 | tf_op jit(solution)/shard_map/all_to_all | solution.py:422
  24.6 15.4 %copy-start.4 = (bf16[2,12,24,1536]{3,2,1,0:T(8,128)(2,1)S(1)}, bf16[2,12,24,1536]{3,2,1,0:T(8,128)(2,1)}, u32[]{:S(2)}) copy-start(bf16[2,12,24,1536]{3,2,1,0:T(8,128)(2,1)} %fusion.4.refs_6_) | copy-start | bytes 5308420
  26.3 22.6 %collective-permute-start = (bf16[2,24,1536]{2,1,0:T(8,128)(2,1)}, bf16[2,24,1536]{2,1,0:T(8,128)(2,1)}, u32[]{:S(2)}, u32[]{:S(2)}) collective-permute-start(bf16[2,24,1536]{2,1,0:T(8,128)(2,1)} %dynamic-slice_bitcast_fusion), channel_id=1, source_target_pairs={{0,192},{64,0},{128,64},{192,128},{1,193},{65,1},{129,65},{193,129... | collective-permute-start | bytes 442376 | tf_op jit(solution)/shard_map/ppermute | solution.py:442
  26.9 22.1 %collective-permute-start.1 = (bf16[2,24,1536]{2,1,0:T(8,128)(2,1)}, bf16[2,24,1536]{2,1,0:T(8,128)(2,1)}, u32[]{:S(2)}, u32[]{:S(2)}) collective-permute-start(bf16[2,24,1536]{2,1,0:T(8,128)(2,1)} %dynamic-slice_bitcast_fusion), channel_id=1, source_target_pairs={{0,128},{64,192},{128,0},{192,64},{1,129},{65,193},{129,1},{193,65... | collective-permute-start | bytes 442376 | tf_op jit(solution)/shard_map/ppermute | solution.py:442
  29.3 19.7 %collective-permute-start.2 = (bf16[2,24,1536]{2,1,0:T(8,128)(2,1)}, bf16[2,24,1536]{2,1,0:T(8,128)(2,1)}, u32[]{:S(2)}, u32[]{:S(2)}) collective-permute-start(bf16[2,24,1536]{2,1,0:T(8,128)(2,1)} %dynamic-slice_bitcast_fusion), channel_id=1, source_target_pairs={{0,64},{64,128},{128,192},{192,0},{1,65},{65,129},{129,193},{193,1... | collective-permute-start | bytes 442376 | tf_op jit(solution)/shard_map/ppermute | solution.py:442
  32.5 16.5 %collective-permute-start.3 = (bf16[2,24,1536]{2,1,0:T(8,128)(2,1)}, bf16[2,24,1536]{2,1,0:T(8,128)(2,1)}, u32[]{:S(2)}, u32[]{:S(2)}) collective-permute-start(bf16[2,24,1536]{2,1,0:T(8,128)(2,1)} %fusion.36), channel_id=1, source_target_pairs={{0,64},{64,128},{128,192},{1,65},{65,129},{129,193},{2,66},{66,130... | collective-permute-start | bytes 442376 | tf_op jit(solution)/shard_map/ppermute | solution.py:448
  35.1 12.0 %copy-start.14 = (s32[24,1536]{1,0:T(8,128)S(1)}, s32[24,1536]{1,0:T(8,128)}, u32[]{:S(2)}) copy-start(s32[24,1536]{1,0:T(8,128)} %param.14) | copy-start | bytes 442372
  35.1 12.6 %collective-permute-start.4 = (bf16[2,24,1536]{2,1,0:T(8,128)(2,1)}, bf16[2,24,1536]{2,1,0:T(8,128)(2,1)}, u32[]{:S(2)}, u32[]{:S(2)}) collective-permute-start(bf16[2,24,1536]{2,1,0:T(8,128)(2,1)} %pad_maximum_fusion.1), channel_id=1, source_target_pairs={{64,0},{128,64},{192,128},{65,1},{129,65},{193,129},{66,2},{130,66... | collective-permute-start | bytes 442376 | tf_op jit(solution)/shard_map/ppermute | solution.py:449
  72.7 9.0 %copy-start.7 = (f32[12,24,128]{2,1,0:T(8,128)S(1)}, f32[12,24,128]{2,1,0:T(8,128)}, u32[]{:S(2)}) copy-start(f32[12,24,128]{2,1,0:T(8,128)} %copy-done.6) | copy-start | bytes 442372
  72.7 52.9 %all-to-all-start.1 = ((bf16[64,14,8,128]{3,2,1,0:T(8,128)(2,1)}), bf16[64,14,8,128]{3,2,1,0:T(8,128)(2,1)S(1)}, u32[]{:S(2)}, u32[]{:S(2)}) async-start(bf16[64,14,8,128]{3,2,1,0:T(8,128)(2,1)} %get-tuple-element.35), calls=%async_computation.1 | async-start | bytes 3670016 | tf_op jit(solution)/shard_map/all_to_all | solution.py:422
  85.7 5.6 %collective-permute-start.6 = (f32[64,64]{1,0:T(8,128)S(1)}, f32[64,64]{1,0:T(8,128)S(1)}, u32[]{:S(2)}, u32[]{:S(2)}) collective-permute-start(f32[64,64]{1,0:T(8,128)S(1)} %fusion.16), channel_id=1, source_target_pairs={{0,128},{64,192},{128,0},{192,64},{1,129},{65,193},{129,1},{193,65... | collective-permute-start | bytes 49160 | tf_op jit(solution)/shard_map/ppermute | solution.py:384
  86.9 4.4 %collective-permute-start.7 = (f32[64,64]{1,0:T(8,128)S(1)}, f32[64,64]{1,0:T(8,128)S(1)}, u32[]{:S(2)}, u32[]{:S(2)}) collective-permute-start(f32[64,64]{1,0:T(8,128)S(1)} %fusion.16), channel_id=1, source_target_pairs={{0,192},{64,128},{128,64},{192,0},{1,193},{65,129},{129,65},{193,1... | collective-permute-start | bytes 49160 | tf_op jit(solution)/shard_map/ppermute | solution.py:384
  86.9 5.4 %collective-permute-start.5 = (f32[64,64]{1,0:T(8,128)S(1)}, f32[64,64]{1,0:T(8,128)S(1)}, u32[]{:S(2)}, u32[]{:S(2)}) collective-permute-start(f32[64,64]{1,0:T(8,128)S(1)} %fusion.16), channel_id=1, source_target_pairs={{0,64},{64,0},{128,192},{192,128},{1,65},{65,1},{129,193},{193,129... | collective-permute-start | bytes 49160 | tf_op jit(solution)/shard_map/ppermute | solution.py:384
  92.4 1.3 collective-permute-start.8
  93.7 6.4 %collective-permute-start.10 = (f32[64,64]{1,0:T(8,128)S(1)}, f32[64,64]{1,0:T(8,128)S(1)}, u32[]{:S(2)}, u32[]{:S(2)}) collective-permute-start(f32[64,64]{1,0:T(8,128)S(1)} %add.105), channel_id=1, source_target_pairs={{0,32},{1,33},{2,34},{3,35},{4,36},{5,37},{6,38},{7,39},{8,40},{9,... | collective-permute-start | bytes 49160 | tf_op jit(solution)/shard_map/ppermute | solution.py:384
  95.9 4.8 %collective-permute-start.11 = (f32[64,64]{1,0:T(8,128)S(1)}, f32[64,64]{1,0:T(8,128)S(1)}, u32[]{:S(2)}, u32[]{:S(2)}) collective-permute-start(f32[64,64]{1,0:T(8,128)S(1)} %add.105), channel_id=1, source_target_pairs={{0,48},{1,49},{2,50},{3,51},{4,52},{5,53},{6,54},{7,55},{8,56},{9,... | collective-permute-start | bytes 49160 | tf_op jit(solution)/shard_map/ppermute | solution.py:384
  95.9 4.9 %collective-permute-start.9 = (f32[64,64]{1,0:T(8,128)S(1)}, f32[64,64]{1,0:T(8,128)S(1)}, u32[]{:S(2)}, u32[]{:S(2)}) collective-permute-start(f32[64,64]{1,0:T(8,128)S(1)} %add.105), channel_id=1, source_target_pairs={{0,16},{1,17},{2,18},{3,19},{4,20},{5,21},{6,22},{7,23},{8,24},{9,... | collective-permute-start | bytes 49160 | tf_op jit(solution)/shard_map/ppermute | solution.py:384
  100.8 27.3 %collective-permute-start.12 = (f32[64,64]{1,0:T(8,128)S(1)}, f32[64,64]{1,0:T(8,128)S(1)}, u32[]{:S(2)}, u32[]{:S(2)}) collective-permute-start(f32[64,64]{1,0:T(8,128)S(1)} %add_add_fusion.1), channel_id=1, source_target_pairs={{1,9},{3,11},{5,13},{7,15},{9,1},{11,3},{13,5},{15,7},{17,25},{19,... | collective-permute-start | bytes 49160 | tf_op jit(solution)/shard_map/ppermute | solution.py:392
  101.5 26.6 %collective-permute-start.13 = (f32[64,64]{1,0:T(8,128)S(1)}, f32[64,64]{1,0:T(8,128)S(1)}, u32[]{:S(2)}, u32[]{:S(2)}) collective-permute-start(f32[64,64]{1,0:T(8,128)S(1)} %add_add_fusion.1), channel_id=1, source_target_pairs={{0,2},{1,11},{2,0},{3,9},{4,6},{5,15},{6,4},{7,13},{8,10},{9,3},{1... | collective-permute-start | bytes 49160 | tf_op jit(solution)/shard_map/ppermute | solution.py:393
  103.4 24.8 %collective-permute-start.14 = (f32[64,64]{1,0:T(8,128)S(1)}, f32[64,64]{1,0:T(8,128)S(1)}, u32[]{:S(2)}, u32[]{:S(2)}) collective-permute-start(f32[64,64]{1,0:T(8,128)S(1)} %add_add_fusion.1), channel_id=1, source_target_pairs={{0,4},{1,13},{2,6},{3,15},{4,0},{5,9},{6,2},{7,11},{8,12},{9,5},{1... | collective-permute-start | bytes 49160 | tf_op jit(solution)/shard_map/ppermute | solution.py:393
  106.0 22.2 %collective-permute-start.15 = (f32[64,64]{1,0:T(8,128)S(1)}, f32[64,64]{1,0:T(8,128)S(1)}, u32[]{:S(2)}, u32[]{:S(2)}) collective-permute-start(f32[64,64]{1,0:T(8,128)S(1)} %add_add_fusion.1), channel_id=1, source_target_pairs={{0,6},{1,15},{2,4},{3,13},{4,2},{5,11},{6,0},{7,9},{8,14},{9,7},{1... | collective-permute-start | bytes 49160 | tf_op jit(solution)/shard_map/ppermute | solution.py:393
  128.2 4.1 %collective-permute-start.16 = (f32[64,64]{1,0:T(8,128)S(1)}, f32[64,64]{1,0:T(8,128)S(1)}, u32[]{:S(2)}, u32[]{:S(2)}) collective-permute-start(f32[64,64]{1,0:T(8,128)S(1)} %add_add_fusion), channel_id=1, source_target_pairs={{0,1},{1,0},{2,3},{3,2},{4,5},{5,4},{6,7},{7,6},{8,9},{9,8},{10,11... | collective-permute-start | bytes 49160 | tf_op jit(solution)/shard_map/ppermute | solution.py:384
  (11 other events, 28.0 us)
